TPU v7x, 256 devices: a whole 4x4x8 slice. The times are simulated.
256 devices in a mesh: owner: 16 (over y_hi, x, core), rep: 16 (over z, y_lo).
Axes of the slice: x: 4, y: 4 (y_hi: 2, y_lo: 2; y = y_hi * 2 + y_lo), z: 8, core: 2. Of those that a mesh axis runs over, the one named last changes fastest.
Arguments:
- shots: bfloat16 [65536, 768], P(('owner', 'rep'))
- basis: float32 [65536, 64], P(('owner', 'rep'))
- round_masks: int32 [3], replicated, may hold values from 1 to 15, as said below
Outputs:
- iterate: float32 [65536, 64], P(('owner', 'rep'))
- ritz: float32 [64, 64], replicated
Inputs may be any that keep to these rules, and one draw needn't show every extreme that they name: `round_masks`: the masks are distinct, so every round pairs every block with a different block.
All inputs are finite; a program needn't handle non-finite values.
Results may differ from a plain program's by a relative error of at most 0.0039.
Values may be sent and summed in bfloat16 or wider, within the bound.
A program may use at most 64 MiB of HBM per device.

v0:
```python
import math

import jax
import jax.numpy as jnp
from jax import lax
from jax.sharding import PartitionSpec as P

ROUNDS = 3


sharpness = 1.6


def swapped_2(shard, axis, distance):
    return lax.ppermute(shard, axis, [(i, i ^ 1 << distance) for i in range(lax.axis_size(axis))])


def normalize(shots):
    values = shots.astype(jnp.float32)
    scale = lax.rsqrt(jnp.mean(values * values, axis=-1, keepdims=True) + 1e-06)
    return (values * scale).astype(jnp.bfloat16)


def apply_inverse(lower_factor, values):
    return lax.linalg.triangular_solve(
        lower_factor, values, left_side=False, lower=True, transpose_a=True
    )


def pair_rows(units, values, swap_flag, bit_index):
    return (
        jnp.where(swap_flag, swapped_2(units, "owner", bit_index), units),
        jnp.where(swap_flag, swapped_2(values, "owner", bit_index), values),
    )


def shards(shots, basis, round_masks):
    row_count, feature_count = shots.shape
    owner_bits = lax.axis_size("owner").bit_length() - 1
    total_rows = float(lax.axis_size("owner") * lax.axis_size("rep") * row_count)
    score_scale = sharpness / math.sqrt(feature_count)
    unit_rows = normalize(shots)
    sent_values = basis
    lower_factor = None
    grown_rows = basis
    ritz_sum = None
    for round_index in range(ROUNDS):
        round_mask = round_masks[round_index]
        partner_units = unit_rows
        partner_values = sent_values
        for bit_index in range(owner_bits):
            swap_flag = round_mask // 2**bit_index % 2 == 1
            partner_units, partner_values = pair_rows(
                partner_units, partner_values, swap_flag, bit_index
            )
        whole_units = lax.all_gather(partner_units, "rep", axis=0, tiled=True)
        whole_values = lax.all_gather(partner_values, "rep", axis=0, tiled=True)
        scores = lax.dot_general(
            unit_rows, whole_units, (((1,), (1,)), ((), ())), preferred_element_type=jnp.float32
        )
        affinity = jnp.exp(scores * score_scale)
        totals = jnp.sum(affinity, axis=1)
        product = jnp.dot(
            affinity,
            whole_values,
            precision=lax.Precision.HIGHEST,
            preferred_element_type=jnp.float32,
        )
        carried = product / totals[:, None]
        own_values = sent_values
        grown_rows = own_values + carried
        gram_part = lax.dot_general(
            grown_rows,
            grown_rows,
            (((0,), (0,)), ((), ())),
            precision=lax.Precision.HIGHEST,
            preferred_element_type=jnp.float32,
        )
        ritz_part = lax.dot_general(
            own_values,
            grown_rows,
            (((0,), (0,)), ((), ())),
            precision=lax.Precision.HIGHEST,
            preferred_element_type=jnp.float32,
        )
        gram_sum, ritz_sum = lax.psum((gram_part, ritz_part), ("owner", "rep"))
        gram_sum = gram_sum / total_rows
        ritz_sum = ritz_sum / total_rows
        lower_factor = jnp.linalg.cholesky(gram_sum)
        sent_values = apply_inverse(lower_factor, grown_rows)
    return (sent_values, ritz_sum)


def solution(mesh):
    in_specs = (P(("owner", "rep"), None), P(("owner", "rep"), None), P())
    out_specs = (P(("owner", "rep"), None), P())
    return jax.shard_map(shards, mesh=mesh, in_specs=in_specs, out_specs=out_specs, check_vma=False)
```

profile of v0, /device:TPU:1, one launch (start us, length us, event | category | flops | bytes accessed | tf_op | source)
XLA Modules:
  0.0 819.7 jit_solution(13880695875674532215)
XLA Ops:
  7.2 1.2 fusion.6
  8.4 1.1 fusion.7
  9.5 3.3 collective-permute-start
  12.8 1.4 fusion.21
  20.0 1.2 broadcast_select_fusion
  22.0 10.0 %collective-permute-done.1 = bf16[256,768]{1,0:T(8,128)(2,1)S(1)} collective-permute-done((bf16[256,768]{1,0:T(8,128)(2,1)S(1)}, bf16[256,768]{1,0:T(8,128)(2,1)S(1)}, u32[]{:S(2)}, u32[]{:S(2)}) %collective-permute-start.1) | collective-permute-done | bytes 393248 | tf_op jit(solution)/shard_map/ppermute | solution.py:15
  32.0 1.1 collective-permute-start.2
  33.1 10.3 %collective-permute-done.2 = bf16[256,768]{1,0:T(8,128)(2,1)S(1)} collective-permute-done((bf16[256,768]{1,0:T(8,128)(2,1)S(1)}, bf16[256,768]{1,0:T(8,128)(2,1)S(1)}, u32[]{:S(2)}, u32[]{:S(2)}) %collective-permute-start.2) | collective-permute-done | bytes 393248 | tf_op jit(solution)/shard_map/ppermute | solution.py:15
  43.5 1.3 collective-permute-start.3
  44.8 9.2 %collective-permute-done.3 = bf16[256,768]{1,0:T(8,128)(2,1)S(1)} collective-permute-done((bf16[256,768]{1,0:T(8,128)(2,1)S(1)}, bf16[256,768]{1,0:T(8,128)(2,1)S(1)}, u32[]{:S(2)}, u32[]{:S(2)}) %collective-permute-start.3) | collective-permute-done | bytes 393248 | tf_op jit(solution)/shard_map/ppermute | solution.py:15
  54.0 0.8 broadcast_select_fusion.11
  54.9 2.7 collective-permute-start.4
  57.6 0.9 collective-permute-done.4
  59.1 2.7 collective-permute-done.5
  61.8 1.1 collective-permute-start.6
  62.9 3.6 collective-permute-done.6
  66.5 1.3 collective-permute-start.7
  67.8 3.4 collective-permute-done.7
  73.1 5.9 collective-permute-done.8
  79.1 1.1 collective-permute-start.9
  80.2 11.3 %collective-permute-done.9 = bf16[256,768]{1,0:T(8,128)(2,1)S(1)} collective-permute-done((bf16[256,768]{1,0:T(8,128)(2,1)S(1)}, bf16[256,768]{1,0:T(8,128)(2,1)S(1)}, u32[]{:S(2)}, u32[]{:S(2)}) %collective-permute-start.9) | collective-permute-done | bytes 393248 | tf_op jit(solution)/shard_map/ppermute | solution.py:15
  91.9 26.1 %collective-permute-done.10 = bf16[256,768]{1,0:T(8,128)(2,1)S(1)} collective-permute-done((bf16[256,768]{1,0:T(8,128)(2,1)S(1)}, bf16[256,768]{1,0:T(8,128)(2,1)S(1)}, u32[]{:S(2)}, u32[]{:S(2)}) %collective-permute-start.10) | collective-permute-done | bytes 393248 | tf_op jit(solution)/shard_map/ppermute | solution.py:15
  118.0 0.8 broadcast_select_fusion.7
  118.8 88.1 %all-gather.7.cloned.1.call-done = bf16[4096,768]{1,0:T(8,128)(2,1)} async-done(((bf16[256,768]{1,0:T(8,128)(2,1)}), bf16[4096,768]{1,0:T(8,128)(2,1)}) %all-gather.7.cloned.1.call-update) | async-done | bytes 6291472 | tf_op jit(solution)/shard_map/all_gather | solution.py:56
  207.0 6.6 fusion.22
  213.6 56.1 %all-gather.9.cloned.1.call-done = f32[4096,64]{0,1:T(8,128)} async-done(((f32[256,64]{0,1:T(8,128)}), f32[4096,64]{0,1:T(8,128)}) %all-gather.9.cloned.1.call-update) | async-done | bytes 1048592 | tf_op jit(solution)/shard_map/all_gather | solution.py:57
  269.7 6.4 fusion.3
  276.3 94.7 %psum.28 = f32[64,64]{0,1:T(8,128)S(1)} all-reduce(f32[64,64]{0,1:T(8,128)S(1)} %fusion.25), channel_id=1, replica_groups=mesh['owner'=16,'rep'=16] {'owner','rep'}, use_global_device_ids=true, to_apply=%region_2.3 | all-reduce | flops 4096 | bytes 32768 | tf_op jit(solution)/shard_map/psum | solution.py:86
  371.1 5.8 cholesky.59
  378.3 4.9 custom-call.7
  383.5 0.7 collective-permute-start.11
  384.2 0.9 collective-permute-done.11
  385.2 3.5 collective-permute-done.12
  388.7 1.4 collective-permute-start.13
  390.1 3.7 collective-permute-done.13
  393.8 1.8 collective-permute-start.14
  395.7 4.7 collective-permute-done.14
  401.0 3.3 collective-permute-start.15
  405.1 5.2 collective-permute-done.15
  410.3 4.4 collective-permute-start.16
  414.7 6.2 collective-permute-done.16
  420.9 3.1 collective-permute-start.17
  424.0 7.8 collective-permute-done.17
  431.7 0.8 broadcast_select_fusion.3
  432.6 6.6 fusion.23
  439.3 49.2 %all-gather.13.cloned.1.call-done = f32[4096,64]{0,1:T(8,128)} async-done(((f32[256,64]{0,1:T(8,128)}), f32[4096,64]{0,1:T(8,128)}) %all-gather.13.cloned.1.call-update) | async-done | bytes 1048592 | tf_op jit(solution)/shard_map/all_gather | solution.py:57
  488.5 6.4 fusion.4
  495.1 95.7 %psum.29 = f32[64,64]{0,1:T(8,128)S(1)} all-reduce(f32[64,64]{0,1:T(8,128)S(1)} %fusion.26), channel_id=1, replica_groups=mesh['owner'=16,'rep'=16] {'owner','rep'}, use_global_device_ids=true, to_apply=%region_6.9 | all-reduce | flops 4096 | bytes 32768 | tf_op jit(solution)/shard_map/psum | solution.py:86
  590.9 5.8 cholesky.70
  598.1 4.9 custom-call.8
  603.3 1.6 collective-permute-start.18
  604.9 0.9 collective-permute-done.18
  605.9 3.5 collective-permute-done.19
  609.5 5.0 collective-permute-done.20
  614.6 7.6 collective-permute-done.21
  622.9 21.3 %all-gather.15.cloned.1.call-done = bf16[4096,768]{1,0:T(8,128)(2,1)} async-done(((bf16[256,768]{1,0:T(8,128)(2,1)}), bf16[4096,768]{1,0:T(8,128)(2,1)}) %all-gather.15.cloned.1.call-update) | async-done | bytes 6291472 | tf_op jit(solution)/shard_map/all_gather | solution.py:56
  644.2 6.7 fusion.24
  650.8 55.6 %all-gather.17.cloned.1.call-done = f32[4096,64]{0,1:T(8,128)} async-done(((f32[256,64]{0,1:T(8,128)}), f32[4096,64]{0,1:T(8,128)}) %all-gather.17.cloned.1.call-update) | async-done | bytes 1048592 | tf_op jit(solution)/shard_map/all_gather | solution.py:57
  706.5 6.4 fusion.5
  713.3 85.7 %all-reduce = (f32[64,64]{0,1:T(8,128)S(1)}, f32[64,64]{0,1:T(8,128)S(1)}) all-reduce(f32[64,64]{0,1:T(8,128)S(1)} %fusion.27, f32[64,64]{0,1:T(8,128)S(1)} %fusion.28), channel_id=1, replica_groups=mesh['owner'=16,'rep'=16] {'owner','rep'}, use_global_device_ids=true, to_apply=%region_8.11 | all-reduce | flops 8192 | bytes 65536 | tf_op jit(solution)/shard_map/psum | solution.py:86
  799.1 5.8 cholesky.81
  806.3 4.9 custom-call.9
  811.2 0.9 convolution_bitcast_fusion
  812.1 0.7 copy.12
  (67 shorter events, 10.1 us)
Async XLA Ops:
  7.2 47.8 %copy-start = (f32[256,64]{0,1:T(8,128)S(1)}, f32[256,64]{0,1:T(8,128)}, u32[]{:S(2)}) copy-start(f32[256,64]{0,1:T(8,128)} %param.7) | copy-start | bytes 196612
  7.2 199.8 %all-gather.7.cloned.1.call-start = ((), (), s32[]{:S(2)}) async-start(), calls=%async_computation | async-start | bytes 6684672 | tf_op jit(solution)/shard_map/all_gather | solution.py:56
  9.5 10.5 %collective-permute-start = (bf16[256,768]{1,0:T(8,128)(2,1)S(1)}, bf16[256,768]{1,0:T(8,128)(2,1)S(1)}, u32[]{:S(2)}, u32[]{:S(2)}) collective-permute-start(bf16[256,768]{1,0:T(8,128)(2,1)S(1)} %fusion.7), channel_id=1, source_target_pairs={{0,16},{16,0},{32,48},{48,32},{64,80},{80,64},{96,112},{112,96},{1... | collective-permute-start | bytes 1179656 | tf_op jit(solution)/shard_map/ppermute | solution.py:15
  21.2 10.8 %collective-permute-start.1 = (bf16[256,768]{1,0:T(8,128)(2,1)S(1)}, bf16[256,768]{1,0:T(8,128)(2,1)S(1)}, u32[]{:S(2)}, u32[]{:S(2)}) collective-permute-start(bf16[256,768]{1,0:T(8,128)(2,1)S(1)} %get-tuple-element.10), channel_id=1, source_target_pairs={{0,32},{16,48},{32,0},{48,16},{64,96},{80,112},{96,64},{112,80},{1... | collective-permute-start | bytes 1179656 | tf_op jit(solution)/shard_map/ppermute | solution.py:15
  32.0 11.4 %collective-permute-start.2 = (bf16[256,768]{1,0:T(8,128)(2,1)S(1)}, bf16[256,768]{1,0:T(8,128)(2,1)S(1)}, u32[]{:S(2)}, u32[]{:S(2)}) collective-permute-start(bf16[256,768]{1,0:T(8,128)(2,1)S(1)} %broadcast_select_fusion.9), channel_id=1, source_target_pairs={{0,64},{16,80},{32,96},{48,112},{64,0},{80,16},{96,32},{112,48},{1... | collective-permute-start | bytes 1179656 | tf_op jit(solution)/shard_map/ppermute | solution.py:15
  43.5 10.5 %collective-permute-start.3 = (bf16[256,768]{1,0:T(8,128)(2,1)S(1)}, bf16[256,768]{1,0:T(8,128)(2,1)S(1)}, u32[]{:S(2)}, u32[]{:S(2)}) collective-permute-start(bf16[256,768]{1,0:T(8,128)(2,1)S(1)} %broadcast_select_fusion.10), channel_id=1, source_target_pairs={{0,128},{16,144},{32,160},{48,176},{64,192},{80,208},{96,224},{112... | collective-permute-start | bytes 1179656 | tf_op jit(solution)/shard_map/ppermute | solution.py:15
  54.9 214.8 %all-gather.9.cloned.1.call-start = ((), (), s32[]{:S(2)}) async-start(), calls=%async_computation.1 | async-start | bytes 1114112 | tf_op jit(solution)/shard_map/all_gather | solution.py:57
  54.9 3.6 collective-permute-start.4
  58.6 3.2 collective-permute-start.5
  61.8 4.7 collective-permute-start.6
  66.5 4.7 collective-permute-start.7
  71.9 360.8 %all-gather.11.cloned.1.call-start = ((), (), s32[]{:S(2)}) async-start(), calls=%async_computation.2 | async-start | bytes 6684672 | tf_op jit(solution)/shard_map/all_gather | solution.py:56
  71.9 7.1 collective-permute-start.8
  79.1 12.4 %collective-permute-start.9 = (bf16[256,768]{1,0:T(8,128)(2,1)S(1)}, bf16[256,768]{1,0:T(8,128)(2,1)S(1)}, u32[]{:S(2)}, u32[]{:S(2)}) collective-permute-start(bf16[256,768]{1,0:T(8,128)(2,1)S(1)} %broadcast_select_fusion.5), channel_id=1, source_target_pairs={{0,64},{16,80},{32,96},{48,112},{64,0},{80,16},{96,32},{112,48},{1... | collective-permute-start | bytes 1179656 | tf_op jit(solution)/shard_map/ppermute | solution.py:15
  91.5 26.5 %collective-permute-start.10 = (bf16[256,768]{1,0:T(8,128)(2,1)S(1)}, bf16[256,768]{1,0:T(8,128)(2,1)S(1)}, u32[]{:S(2)}, u32[]{:S(2)}) collective-permute-start(bf16[256,768]{1,0:T(8,128)(2,1)S(1)} %broadcast_select_fusion.6), channel_id=1, source_target_pairs={{0,128},{16,144},{32,160},{48,176},{64,192},{80,208},{96,224},{112... | collective-permute-start | bytes 1179656 | tf_op jit(solution)/shard_map/ppermute | solution.py:15
  118.8 369.7 %all-gather.13.cloned.1.call-start = ((), (), s32[]{:S(2)}) async-start(), calls=%async_computation.3 | async-start | bytes 1114112 | tf_op jit(solution)/shard_map/all_gather | solution.py:57
  383.5 1.6 collective-permute-start.11
  385.1 3.6 collective-permute-start.12
  388.7 5.1 collective-permute-start.13
  393.8 6.5 collective-permute-start.14
  401.0 243.2 %all-gather.15.cloned.1.call-start = ((), (), s32[]{:S(2)}) async-start(), calls=%async_computation.4 | async-start | bytes 6684672 | tf_op jit(solution)/shard_map/all_gather | solution.py:56
  401.0 9.3 %collective-permute-start.15 = (bf16[256,768]{1,0:T(8,128)(2,1)S(1)}, bf16[256,768]{1,0:T(8,128)(2,1)S(1)}, u32[]{:S(2)}, u32[]{:S(2)}) collective-permute-start(bf16[256,768]{1,0:T(8,128)(2,1)S(1)} %get-tuple-element.8), channel_id=1, source_target_pairs={{0,32},{16,48},{32,0},{48,16},{64,96},{80,112},{96,64},{112,80},{1... | collective-permute-start | bytes 1179656 | tf_op jit(solution)/shard_map/ppermute | solution.py:15
  410.3 10.5 %collective-permute-start.16 = (bf16[256,768]{1,0:T(8,128)(2,1)S(1)}, bf16[256,768]{1,0:T(8,128)(2,1)S(1)}, u32[]{:S(2)}, u32[]{:S(2)}) collective-permute-start(bf16[256,768]{1,0:T(8,128)(2,1)S(1)} %broadcast_select_fusion.1), channel_id=1, source_target_pairs={{0,64},{16,80},{32,96},{48,112},{64,0},{80,16},{96,32},{112,48},{1... | collective-permute-start | bytes 1179656 | tf_op jit(solution)/shard_map/ppermute | solution.py:15
  420.9 10.8 %collective-permute-start.17 = (bf16[256,768]{1,0:T(8,128)(2,1)S(1)}, bf16[256,768]{1,0:T(8,128)(2,1)S(1)}, u32[]{:S(2)}, u32[]{:S(2)}) collective-permute-start(bf16[256,768]{1,0:T(8,128)(2,1)S(1)} %broadcast_select_fusion.2), channel_id=1, source_target_pairs={{0,128},{16,144},{32,160},{48,176},{64,192},{80,208},{96,224},{112... | collective-permute-start | bytes 1179656 | tf_op jit(solution)/shard_map/ppermute | solution.py:15
  432.6 273.9 %all-gather.17.cloned.1.call-start = ((), (), s32[]{:S(2)}) async-start(), calls=%async_computation.5 | async-start | bytes 1114112 | tf_op jit(solution)/shard_map/all_gather | solution.py:57
  603.3 2.5 collective-permute-start.18
  605.8 3.6 collective-permute-start.19
  609.4 5.1 collective-permute-start.20
  614.5 7.7 collective-permute-start.21
Sparse Core Ops, SparseCore 0:
  55.0 151.9 all-gather.6
  209.3 60.3 all-gather.8
  271.5 153.5 all-gather.10
  427.3 61.1 all-gather.12
  490.1 154.0 all-gather.14
  646.4 60.0 all-gather.16
where the time goes:
time: 820 us
  waiting for transfers between devices  403 us (49%)
  blocking collectives  276 us (34%)
  other arithmetic  44.4 us (5%)
  matrix products  41.4 us (5%)
  starting transfers between devices  30.2 us (4%)
  between operations  22.2 us (3%)
    psum x3, blocking collectives, shards(): gram_sum, ritz_sum = lax.psum((gram_part, ritz_part), ('owner', 'rep'))  276 us
    all_gather x3, waiting for transfers between devices, shards(): whole_values = lax.all_gather(partner_values, 'rep', axis=0, tiled=True)  161 us
    ppermute x22, waiting for transfers between devices, swapped_2(): lax.ppermute(shard, axis, [(i, i ^ 1 << distance) for i in range(lax.axis...  133 us
    all_gather x3, waiting for transfers between devices, shards(): whole_units = lax.all_gather(partner_units, 'rep', axis=0, tiled=True)  109 us
    ppermute x22, starting transfers between devices, swapped_2(): lax.ppermute(shard, axis, [(i, i ^ 1 << distance) for i in range(lax.axis...  29.9 us
    dot_general x3, matrix products, shards(): lax.dot_general(unit_rows, whole_units, (((1,), (1,)), ((), ())), preferr...  19.9 us
    another operation x9, other arithmetic, shards(): lower_factor = jnp.linalg.cholesky(gram_sum)  19.6 us
    dot_general x3, matrix products, shards(): jnp.dot(affinity, whole_values, precision=lax.Precision.HIGHEST, preferre...  19.2 us
  transfers between devices with their start and end apart: 28, of which 26 were waited for; matrix products, arithmetic and copies ran while one was open for 8% of the time, Pallas kernels for 0%

commit v1 on v0

v1 whole, which is shorter than its diff:
```python
import math

import jax
import jax.numpy as jnp
from jax import lax
from jax.sharding import PartitionSpec as P

ROUNDS = 3


sharpness = 1.6


def swapped_2(shard, axis, distance):
    return lax.ppermute(shard, axis, [(i, i ^ 1 << distance) for i in range(lax.axis_size(axis))])


def normalize(shots):
    values = shots.astype(jnp.float32)
    scale = lax.rsqrt(jnp.mean(values * values, axis=-1, keepdims=True) + 1e-06)
    return (values * scale).astype(jnp.bfloat16)


def to_partner(values, mask, owner_bits):
    for bit in range(owner_bits):
        flag = mask // 2**bit % 2 == 1
        values = jnp.where(flag, swapped_2(values, "owner", bit), values)
    return values


def dot_tn(a, b):
    return lax.dot_general(
        a, b, (((0,), (0,)), ((), ())), precision=lax.Precision.HIGHEST, preferred_element_type=jnp.float32
    )


def shards(shots, basis, round_masks):
    row_count, feature_count = shots.shape
    owner_bits = lax.axis_size("owner").bit_length() - 1
    total_rows = float(lax.axis_size("owner") * lax.axis_size("rep") * row_count)
    score_scale = sharpness / math.sqrt(feature_count)
    unit_rows = normalize(shots)
    own_units = lax.all_gather(unit_rows, "rep", axis=0, tiled=True)
    affinities = []
    for t in range(ROUNDS):
        theirs = to_partner(unit_rows, round_masks[t], owner_bits)
        scores = lax.dot_general(
            theirs, own_units, (((1,), (1,)), ((), ())), preferred_element_type=jnp.float32
        )
        affinities.append(jnp.exp(scores * score_scale).astype(jnp.bfloat16))
    grown = basis
    before = basis
    for t in range(ROUNDS):
        before = grown
        whole = lax.all_gather(grown.astype(jnp.bfloat16), "rep", axis=0, tiled=True)
        totals = jnp.sum(affinities[t].astype(jnp.float32), axis=1, keepdims=True)
        carried = jnp.dot(affinities[t], whole, preferred_element_type=jnp.float32) / totals
        grown = before + to_partner(carried, round_masks[t], owner_bits)
    both = jnp.concatenate([before, grown], axis=1)
    k = basis.shape[1]
    sums = lax.psum(dot_tn(both, both), ("owner", "rep")) / total_rows
    lower = jnp.linalg.cholesky(jnp.stack([sums[:k, :k], sums[k:, k:]]))
    iterate = lax.linalg.triangular_solve(lower[1], grown, left_side=False, lower=True, transpose_a=True)
    half = lax.linalg.triangular_solve(lower[0], sums[:k, k:], left_side=True, lower=True)
    ritz = lax.linalg.triangular_solve(lower[0], half, left_side=False, lower=True, transpose_a=True)
    return (iterate, ritz)


def solution(mesh):
    in_specs = (P(("owner", "rep"), None), P(("owner", "rep"), None), P())
    out_specs = (P(("owner", "rep"), None), P())
    return jax.shard_map(shards, mesh=mesh, in_specs=in_specs, out_specs=out_specs, check_vma=False)
```

time: 820 us -> 585 us (0.71)
  blocking collectives: 276 us -> 117 us
  waiting for transfers between devices: 403 us -> 341 us
  starting transfers between devices: 30.2 us -> 55.8 us
  matrix products: 41.4 us -> 19.4 us
  other arithmetic: 44.4 us -> 27.3 us
    psum x3 -> x0, blocking collectives: 276 us -> none  [shards(): gram_sum, ritz_sum = lax.psum((gram_part, ritz_part), ('owner', 'rep'))]
    psum x0 -> x1, waiting for transfers between devices: none -> 239 us  [shards(): sums = lax.psum(dot_tn(both, both), ('owner', 'rep')) / total_rows]
    all_gather x6 -> x1, waiting for transfers between devices: 270 us -> 57.5 us  [shards(): own_units = lax.all_gather(unit_rows, 'rep', axis=0, tiled=True)]
    all_gather x0 -> x3, blocking collectives: none -> 117 us  [shards(): lax.all_gather(grown.astype(jnp.bfloat16), 'rep', axis=0, tiled=True)]
    ppermute x22, waiting for transfers between devices: 133 us -> 44.6 us  [swapped_2(): lax.ppermute(shard, axis, [(i, i ^ 1 << distance) for i in range(lax.axis...]
    ppermute x22, starting transfers between devices: 29.9 us -> 55.7 us  [swapped_2(): lax.ppermute(shard, axis, [(i, i ^ 1 << distance) for i in range(lax.axis...]
    dot_general x10 -> x7, matrix products: 40 us -> 17.5 us  [the longest x3 14.3 us: shards(): lax.dot_general(theirs, own_units, (((1,), (1,)), ((), ())), preferred_el...]
    another operation x15 -> x8, other arithmetic: 36.2 us -> 21.7 us  [the longest x5 11.9 us: shards(): lower = jnp.linalg.cholesky(jnp.stack([sums[:k, :k], sums[k:, k:]]))]
  transfers between devices with their start and end apart: 28 -> 24, of which waited for: 26 -> 14; matrix products, arithmetic and copies ran while one was open for 8% -> 3% of each run, Pallas kernels for 0% -> 0%
where the time goes in v1:
time: 585 us
  waiting for transfers between devices  341 us (58%)
  blocking collectives  117 us (20%)
  starting transfers between devices  55.8 us (10%)
  other arithmetic  27.3 us (5%)
  between operations  22.2 us (4%)
  matrix products  19.4 us (3%)
    psum x1, waiting for transfers between devices, shards(): sums = lax.psum(dot_tn(both, both), ('owner', 'rep')) / total_rows  239 us
    all_gather x3, blocking collectives, shards(): lax.all_gather(grown.astype(jnp.bfloat16), 'rep', axis=0, tiled=True)  117 us
    all_gather x1, waiting for transfers between devices, shards(): own_units = lax.all_gather(unit_rows, 'rep', axis=0, tiled=True)  57.5 us
    ppermute x22, starting transfers between devices, swapped_2(): lax.ppermute(shard, axis, [(i, i ^ 1 << distance) for i in range(lax.axis...  55.7 us
    ppermute x22, waiting for transfers between devices, swapped_2(): lax.ppermute(shard, axis, [(i, i ^ 1 << distance) for i in range(lax.axis...  44.6 us
    dot_general x3, matrix products, shards(): lax.dot_general(theirs, own_units, (((1,), (1,)), ((), ())), preferred_el...  14.3 us
    another operation x5, other arithmetic, shards(): lower = jnp.linalg.cholesky(jnp.stack([sums[:k, :k], sums[k:, k:]]))  11.9 us
  transfers between devices with their start and end apart: 24, of which 14 were waited for; matrix products, arithmetic and copies ran while one was open for 3% of the time, Pallas kernels for 0%

profile of v1, /device:TPU:1, one launch (start us, length us, event | category | flops | bytes accessed | tf_op | source)
XLA Modules:
  0.0 585.0 jit_solution(10625355796196969609)
XLA Ops:
  7.2 0.0 all-gather.2.cloned.1.call-start
  7.2 1.2 fusion.6
  8.4 1.9 fusion.7
  10.3 0.0 all-reduce.2.cloned.1.call-start
  10.4 3.3 collective-permute-start
  13.7 1.4 fusion.29
  20.9 1.2 broadcast_select_fusion
  22.1 0.1 collective-permute-start.1
  22.9 10.1 %collective-permute-done.1 = bf16[256,768]{1,0:T(8,128)(2,1)S(1)} collective-permute-done((bf16[256,768]{1,0:T(8,128)(2,1)S(1)}, bf16[256,768]{1,0:T(8,128)(2,1)S(1)}, u32[]{:S(2)}, u32[]{:S(2)}) %collective-permute-start.1) | collective-permute-done | bytes 393248 | tf_op jit(solution)/shard_map/ppermute | solution.py:15
  33.1 1.1 collective-permute-start.2
  34.9 0.4 collective-permute-start.8
  35.3 9.3 %collective-permute-done.2 = bf16[256,768]{1,0:T(8,128)(2,1)S(1)} collective-permute-done((bf16[256,768]{1,0:T(8,128)(2,1)S(1)}, bf16[256,768]{1,0:T(8,128)(2,1)S(1)}, u32[]{:S(2)}, u32[]{:S(2)}) %collective-permute-start.2) | collective-permute-done | bytes 393248 | tf_op jit(solution)/shard_map/ppermute | solution.py:15
  44.7 1.3 collective-permute-start.3
  45.9 63.9 %all_gather.13 = bf16[4096,64]{0,1:T(8,128)(2,1)S(1)} all-gather(bf16[256,64]{0,1:T(8,128)(2,1)S(1)} %convert_element_type.36), channel_id=1, replica_groups=mesh['owner'=16,'rep'=16] {'rep'}, dimensions={0}, use_global_device_ids=true | all-gather | bytes 557056 | tf_op jit(solution)/shard_map/all_gather | solution.py:55
  109.9 5.7 collective-permute-start.9
  115.6 57.5 %all-gather.2.cloned.1.call-done = bf16[4096,768]{1,0:T(8,128)(2,1)} async-done(((bf16[256,768]{1,0:T(8,128)(2,1)}), bf16[4096,768]{1,0:T(8,128)(2,1)}) %all-gather.2.cloned.1.call-update) | async-done | bytes 6291472 | tf_op jit(solution)/shard_map/all_gather | solution.py:43
  173.1 4.8 convert_reduce_fusion.2
  177.9 0.8 broadcast_divide_fusion
  178.6 1.4 collective-permute-start.4
  180.7 1.5 collective-permute-start.15
  182.2 0.2 collective-permute-start.5
  182.5 3.0 collective-permute-start.10
  185.5 7.4 %collective-permute-done.5 = f32[256,64]{0,1:T(8,128)S(1)} collective-permute-done((f32[256,64]{0,1:T(8,128)S(1)}, f32[256,64]{0,1:T(8,128)S(1)}, u32[]{:S(2)}, u32[]{:S(2)}) %collective-permute-start.5) | collective-permute-done | bytes 65568 | tf_op jit(solution)/shard_map/ppermute | solution.py:15
  192.9 3.1 collective-permute-start.6
  196.1 0.1 collective-permute-start.16
  196.2 1.5 collective-permute-done.6
  197.7 3.2 collective-permute-start.7
  200.8 4.8 convert_reduce_fusion.1
  205.6 27.6 %all_gather.14 = bf16[4096,64]{0,1:T(8,128)(2,1)S(1)} all-gather(bf16[256,64]{0,1:T(8,128)(2,1)S(1)} %get-tuple-element.4), channel_id=1, replica_groups=mesh['owner'=16,'rep'=16] {'rep'}, dimensions={0}, use_global_device_ids=true | all-gather | bytes 557056 | tf_op jit(solution)/shard_map/all_gather | solution.py:55
  233.2 0.8 convolution_divide_fusion.1
  234.0 9.5 %collective-permute-start.11 = (f32[256,64]{0,1:T(8,128)S(1)}, f32[256,64]{0,1:T(8,128)S(1)}, u32[]{:S(2)}, u32[]{:S(2)}) collective-permute-start(f32[256,64]{0,1:T(8,128)S(1)} %convolution_divide_fusion.1), channel_id=1, source_target_pairs={{0,16},{16,0},{32,48},{48,32},{64,80},{80,64},{96,112},{112,96},{1... | collective-permute-start | bytes 196616 | tf_op jit(solution)/shard_map/ppermute | solution.py:15
  243.5 0.9 collective-permute-done.11
  244.4 1.7 collective-permute-start.12
  246.1 1.2 collective-permute-start.17
  247.3 0.8 collective-permute-done.12
  248.1 3.3 collective-permute-start.13
  251.4 2.0 collective-permute-done.13
  253.3 1.5 collective-permute-start.14
  254.8 2.9 collective-permute-done.17
  257.7 4.8 convert_reduce_fusion
  262.5 26.0 %all_gather.15 = bf16[4096,64]{0,1:T(8,128)(2,1)S(1)} all-gather(bf16[256,64]{0,1:T(8,128)(2,1)S(1)} %get-tuple-element.2), channel_id=1, replica_groups=mesh['owner'=16,'rep'=16] {'rep'}, dimensions={0}, use_global_device_ids=true | all-gather | bytes 557056 | tf_op jit(solution)/shard_map/all_gather | solution.py:55
  288.5 0.8 convolution_divide_fusion
  289.3 9.3 %collective-permute-start.18 = (f32[256,64]{0,1:T(8,128)S(1)}, f32[256,64]{0,1:T(8,128)S(1)}, u32[]{:S(2)}, u32[]{:S(2)}) collective-permute-start(f32[256,64]{0,1:T(8,128)S(1)} %convolution_divide_fusion), channel_id=1, source_target_pairs={{0,16},{16,0},{32,48},{48,32},{64,80},{80,64},{96,112},{112,96},{1... | collective-permute-start | bytes 196616 | tf_op jit(solution)/shard_map/ppermute | solution.py:15
  298.5 0.9 collective-permute-done.18
  299.5 0.4 collective-permute-start.19
  299.9 2.8 collective-permute-done.19
  302.7 3.8 collective-permute-start.20
  306.5 1.7 collective-permute-done.20
  308.2 0.7 collective-permute-start.21
  308.9 4.2 collective-permute-done.21
  313.1 0.9 fusion.14
  314.0 0.0 all-reduce.2.cloned.1.call-update
  314.1 239.3 %all-reduce.2.cloned.1.call-done = f32[128,128]{0,1:T(8,128)} async-done(((f32[128,128]{0,1:T(8,128)}), f32[128,128]{0,1:T(8,128)}) %all-reduce.2.cloned.1.call-update) | async-done | bytes 65552 | tf_op jit(solution)/shard_map/psum | solution.py:61
  553.4 0.8 broadcast_multiply_fusion
  554.2 0.1 slice_bitcast_fusion.1
  554.3 0.1 copy.8
  554.4 11.7 %custom-call.12 = f32[2,64,64]{2,1,0:T(8,128)S(1)} custom-call(f32[2,64,64]{2,1,0:T(8,128)S(1)} %fusion.18), custom_call_target="Cholesky" | custom-call | tf_op jit(solution)/shard_map/jit(cholesky)/cholesky | solution.py:62
  566.2 0.1 compare_reduce_fusion
  566.3 0.1 select_select_fusion
  566.4 4.9 custom-call.13
  571.3 0.9 fusion.24
  572.2 4.9 custom-call.14
  577.1 0.3 fusion.19
  577.4 0.8 fusion.21
  (39 shorter events, 0.5 us)
Async XLA Ops:
  7.2 27.7 %copy-start = (f32[256,64]{0,1:T(8,128)S(1)}, f32[256,64]{0,1:T(8,128)}, u32[]{:S(2)}) copy-start(f32[256,64]{0,1:T(8,128)} %param.4) | copy-start | bytes 196612
  7.2 165.9 %all-gather.2.cloned.1.call-start = ((), (), s32[]{:S(2)}) async-start(), calls=%async_computation | async-start | bytes 6684672 | tf_op jit(solution)/shard_map/all_gather | solution.py:43
  10.3 543.1 %all-reduce.2.cloned.1.call-start = ((), (), s32[]{:S(2)}) async-start(), calls=%async_computation.1 | async-start | bytes 131072 | tf_op jit(solution)/shard_map/psum | solution.py:61
  10.4 10.5 %collective-permute-start = (bf16[256,768]{1,0:T(8,128)(2,1)}, bf16[256,768]{1,0:T(8,128)(2,1)S(1)}, u32[]{:S(2)}, u32[]{:S(2)}) collective-permute-start(bf16[256,768]{1,0:T(8,128)(2,1)} %fusion.7), channel_id=1, source_target_pairs={{0,16},{16,0},{32,48},{48,32},{64,80},{80,64},{96,112},{112,96},{1... | collective-permute-start | bytes 1179656 | tf_op jit(solution)/shard_map/ppermute | solution.py:15
  22.1 10.9 %collective-permute-start.1 = (bf16[256,768]{1,0:T(8,128)(2,1)S(1)}, bf16[256,768]{1,0:T(8,128)(2,1)S(1)}, u32[]{:S(2)}, u32[]{:S(2)}) collective-permute-start(bf16[256,768]{1,0:T(8,128)(2,1)S(1)} %get-tuple-element.8), channel_id=1, source_target_pairs={{0,32},{16,48},{32,0},{48,16},{64,96},{80,112},{96,64},{112,80},{1... | collective-permute-start | bytes 1179656 | tf_op jit(solution)/shard_map/ppermute | solution.py:15
  33.1 11.6 %collective-permute-start.2 = (bf16[256,768]{1,0:T(8,128)(2,1)S(1)}, bf16[256,768]{1,0:T(8,128)(2,1)S(1)}, u32[]{:S(2)}, u32[]{:S(2)}) collective-permute-start(bf16[256,768]{1,0:T(8,128)(2,1)S(1)} %broadcast_select_fusion.7), channel_id=1, source_target_pairs={{0,64},{16,80},{32,96},{48,112},{64,0},{80,16},{96,32},{112,48},{1... | collective-permute-start | bytes 1179656 | tf_op jit(solution)/shard_map/ppermute | solution.py:15
  34.9 75.0 %collective-permute-start.8 = (bf16[256,768]{1,0:T(8,128)(2,1)S(1)}, bf16[256,768]{1,0:T(8,128)(2,1)S(1)}, u32[]{:S(2)}, u32[]{:S(2)}) collective-permute-start(bf16[256,768]{1,0:T(8,128)(2,1)S(1)} %get-tuple-element.7), channel_id=1, source_target_pairs={{0,32},{16,48},{32,0},{48,16},{64,96},{80,112},{96,64},{112,80},{1... | collective-permute-start | bytes 1179656 | tf_op jit(solution)/shard_map/ppermute | solution.py:15
  44.7 71.0 %collective-permute-start.3 = (bf16[256,768]{1,0:T(8,128)(2,1)S(1)}, bf16[256,768]{1,0:T(8,128)(2,1)S(1)}, u32[]{:S(2)}, u32[]{:S(2)}) collective-permute-start(bf16[256,768]{1,0:T(8,128)(2,1)S(1)} %broadcast_select_fusion.8), channel_id=1, source_target_pairs={{0,128},{16,144},{32,160},{48,176},{64,192},{80,208},{96,224},{112... | collective-permute-start | bytes 1179656 | tf_op jit(solution)/shard_map/ppermute | solution.py:15
  109.9 72.5 %collective-permute-start.9 = (bf16[256,768]{1,0:T(8,128)(2,1)S(1)}, bf16[256,768]{1,0:T(8,128)(2,1)S(1)}, u32[]{:S(2)}, u32[]{:S(2)}) collective-permute-start(bf16[256,768]{1,0:T(8,128)(2,1)S(1)} %broadcast_select_fusion.4), channel_id=1, source_target_pairs={{0,64},{16,80},{32,96},{48,112},{64,0},{80,16},{96,32},{112,48},{1... | collective-permute-start | bytes 1179656 | tf_op jit(solution)/shard_map/ppermute | solution.py:15
  178.6 3.6 collective-permute-start.4
  180.7 15.3 %collective-permute-start.15 = (bf16[256,768]{1,0:T(8,128)(2,1)S(1)}, bf16[256,768]{1,0:T(8,128)(2,1)S(1)}, u32[]{:S(2)}, u32[]{:S(2)}) collective-permute-start(bf16[256,768]{1,0:T(8,128)(2,1)S(1)} %get-tuple-element.6), channel_id=1, source_target_pairs={{0,32},{16,48},{32,0},{48,16},{64,96},{80,112},{96,64},{112,80},{1... | collective-permute-start | bytes 1179656 | tf_op jit(solution)/shard_map/ppermute | solution.py:15
  182.2 10.6 %collective-permute-start.5 = (f32[256,64]{0,1:T(8,128)S(1)}, f32[256,64]{0,1:T(8,128)S(1)}, u32[]{:S(2)}, u32[]{:S(2)}) collective-permute-start(f32[256,64]{0,1:T(8,128)S(1)} %broadcast_select_fusion.15), channel_id=1, source_target_pairs={{0,32},{16,48},{32,0},{48,16},{64,96},{80,112},{96,64},{112,80},{1... | collective-permute-start | bytes 196616 | tf_op jit(solution)/shard_map/ppermute | solution.py:15
  182.5 18.4 %collective-permute-start.10 = (bf16[256,768]{1,0:T(8,128)(2,1)S(1)}, bf16[256,768]{1,0:T(8,128)(2,1)S(1)}, u32[]{:S(2)}, u32[]{:S(2)}) collective-permute-start(bf16[256,768]{1,0:T(8,128)(2,1)S(1)} %broadcast_select_fusion.5), channel_id=1, source_target_pairs={{0,128},{16,144},{32,160},{48,176},{64,192},{80,208},{96,224},{112... | collective-permute-start | bytes 1179656 | tf_op jit(solution)/shard_map/ppermute | solution.py:15
  192.9 4.8 collective-permute-start.6
  196.1 50.0 %collective-permute-start.16 = (bf16[256,768]{1,0:T(8,128)(2,1)S(1)}, bf16[256,768]{1,0:T(8,128)(2,1)S(1)}, u32[]{:S(2)}, u32[]{:S(2)}) collective-permute-start(bf16[256,768]{1,0:T(8,128)(2,1)S(1)} %broadcast_select_fusion.1), channel_id=1, source_target_pairs={{0,64},{16,80},{32,96},{48,112},{64,0},{80,16},{96,32},{112,48},{1... | collective-permute-start | bytes 1179656 | tf_op jit(solution)/shard_map/ppermute | solution.py:15
  197.7 7.9 %collective-permute-start.7 = (f32[256,64]{0,1:T(8,128)S(1)}, f32[256,64]{0,1:T(8,128)S(1)}, u32[]{:S(2)}, u32[]{:S(2)}) collective-permute-start(f32[256,64]{0,1:T(8,128)S(1)} %broadcast_select_fusion.17), channel_id=1, source_target_pairs={{0,128},{16,144},{32,160},{48,176},{64,192},{80,208},{96,224},{112... | collective-permute-start | bytes 196616 | tf_op jit(solution)/shard_map/ppermute | solution.py:15
  234.0 10.4 %collective-permute-start.11 = (f32[256,64]{0,1:T(8,128)S(1)}, f32[256,64]{0,1:T(8,128)S(1)}, u32[]{:S(2)}, u32[]{:S(2)}) collective-permute-start(f32[256,64]{0,1:T(8,128)S(1)} %convolution_divide_fusion.1), channel_id=1, source_target_pairs={{0,16},{16,0},{32,48},{48,32},{64,80},{80,64},{96,112},{112,96},{1... | collective-permute-start | bytes 196616 | tf_op jit(solution)/shard_map/ppermute | solution.py:15
  244.4 3.7 collective-permute-start.12
  246.1 11.6 %collective-permute-start.17 = (bf16[256,768]{1,0:T(8,128)(2,1)S(1)}, bf16[256,768]{1,0:T(8,128)(2,1)S(1)}, u32[]{:S(2)}, u32[]{:S(2)}) collective-permute-start(bf16[256,768]{1,0:T(8,128)(2,1)S(1)} %broadcast_select_fusion.2), channel_id=1, source_target_pairs={{0,128},{16,144},{32,160},{48,176},{64,192},{80,208},{96,224},{112... | collective-permute-start | bytes 1179656 | tf_op jit(solution)/shard_map/ppermute | solution.py:15
  248.1 5.2 collective-permute-start.13
  253.3 9.2 %collective-permute-start.14 = (f32[256,64]{0,1:T(8,128)S(1)}, f32[256,64]{0,1:T(8,128)S(1)}, u32[]{:S(2)}, u32[]{:S(2)}) collective-permute-start(f32[256,64]{0,1:T(8,128)S(1)} %broadcast_select_fusion.14), channel_id=1, source_target_pairs={{0,128},{16,144},{32,160},{48,176},{64,192},{80,208},{96,224},{112... | collective-permute-start | bytes 196616 | tf_op jit(solution)/shard_map/ppermute | solution.py:15
  289.3 10.2 %collective-permute-start.18 = (f32[256,64]{0,1:T(8,128)S(1)}, f32[256,64]{0,1:T(8,128)S(1)}, u32[]{:S(2)}, u32[]{:S(2)}) collective-permute-start(f32[256,64]{0,1:T(8,128)S(1)} %convolution_divide_fusion), channel_id=1, source_target_pairs={{0,16},{16,0},{32,48},{48,32},{64,80},{80,64},{96,112},{112,96},{1... | collective-permute-start | bytes 196616 | tf_op jit(solution)/shard_map/ppermute | solution.py:15
  299.5 3.2 collective-permute-start.19
  302.7 5.5 collective-permute-start.20
  308.2 4.9 collective-permute-start.21
Sparse Core Ops, SparseCore 0:
  10.4 162.6 all-gather.1
  314.2 239.1 all-reduce.1

commit v2 on v1

v2 whole, which is shorter than its diff:
```python
import functools
import math

import jax
import jax.numpy as jnp
from jax import lax
from jax.experimental import pallas as pl
from jax.experimental.pallas import tpu as pltpu
from jax.sharding import PartitionSpec as P

ROUNDS = 3
SHARPNESS = 1.6
MESH = pl.DeviceIdType.MESH
NT = (((1,), (1,)), ((), ()))
TN = (((0,), (0,)), ((), ()))
NX, NZ = 4, 8


def dot32(a, b, dims):
    return lax.dot_general(a, b, dims, precision=lax.Precision.HIGHEST, preferred_element_type=jnp.float32)


def pack(rows):
    half = rows.shape[0] // 2
    return jnp.concatenate([rows[:half], rows[half:]], axis=1)


def rounds_kernel(
    scale, masks, shots, basis, grown_out, sums_out,
    own, oth, stage, sib_stage, theirs, aff, gpart, gfull, xbufs, ybufs, rs, ys, zs, fin, prod,
    s1, r1, sg, rg, sc, rc, sa, ra,
):
    n, feat = shots.shape
    half, quarter = n // 2, n // 4
    k = basis.shape[1]
    o, r = lax.axis_index("owner"), lax.axis_index("rep")
    c, x, yh = o % 2, (o // 2) % NX, o // (2 * NX)
    z, yl = r // 2, r % 2
    y, q = yh * 2 + yl, o % (2 * NX)

    def dev(yh=yh, x=x, c=c, z=z, yl=yl):
        return ((yh * NX + x) * 2 + c, z * 2 + yl)

    sibling = dev(yl=1 - yl)

    bar = pltpu.get_barrier_semaphore()

    def hello(device):
        pl.semaphore_signal(bar, inc=1, device_id=device, device_id_type=MESH)

    @pl.loop(1, NZ)
    def _(i):
        hello((o, ((z + i) % NZ) * 2 + yl))

    @pl.loop(1, 2 * NX)
    def _(i):
        hello((yh * 2 * NX + (q + i) % (2 * NX), r))

    @pl.loop(1, 4)
    def _(i):
        there = (y + i) % 4
        hello(((there // 2) * 2 * NX + q, z * 2 + there % 2))

    hello(dev(yh=1 - yh, c=1 - c))

    values = shots[...].astype(jnp.float32)
    inv = lax.rsqrt(jnp.mean(values * values, axis=-1, keepdims=True) + 1e-06)
    units = (values * inv).astype(jnp.bfloat16)
    own[r] = units
    oth[yh, x] = units
    g0 = pack(basis[...])
    gpart[0, r] = g0.astype(jnp.bfloat16)
    pl.semaphore_wait(bar, (NZ - 1) + (2 * NX - 1) + 3 + 1)

    def send(src, dst, ssem, rsem, device):
        return pltpu.make_async_remote_copy(
            src_ref=src, dst_ref=dst, send_sem=ssem, recv_sem=rsem, device_id=device, device_id_type=MESH
        )

    pending = []

    def same(ref, number, device):
        copy = send(ref, ref, s1.at[number], r1.at[number], device)
        pending.append(copy)
        copy.start()

    def landed(ref, number):
        send(ref, ref, s1.at[number], r1.at[number], sibling).wait_recv()

    full, low, high = pl.ds(0, n), pl.ds(0, half), pl.ds(half, half)
    low_a, low_b = pl.ds(0, quarter), pl.ds(quarter, quarter)

    def col(distance, column):
        return ((z + NZ + distance) % NZ) * 2 + column

    YH, XR, XL, XR2, XL2, HR, HL, HR2, HL2 = range(9)
    SIB0 = 9
    UP, DN, UPS, DNS = 18, 22, 26, 30
    CORE = 34
    up, down = dev(z=(z + 1) % NZ), dev(z=(z + NZ - 1) % NZ)
    right, left = dev(x=(x + 1) % NX), dev(x=(x + NX - 1) % NX)

    def g_send(t):
        mine = gpart.at[t, r]

        @pl.loop(1, NZ)
        def _(i):
            send(mine, mine, sg.at[t, i], rg.at[t, i], (o, ((z + i) % NZ) * 2 + yl)).start()

        send(mine, mine, sg.at[t, 8], rg.at[t, 8], sibling).start()

    lane = lax.broadcasted_iota(jnp.int32, (half, 128), 1)

    def unpack(t, item):
        p = gpart[t, item].astype(jnp.float32)
        tail = jnp.where(lane == k, 1.0, 0.0)
        at = pl.multiple_of(item * n, n)
        gfull[pl.ds(at, half), :] = jnp.where(lane < k, p, tail).astype(jnp.bfloat16)
        gfull[pl.ds(at + half, half), :] = jnp.where(lane < k, pltpu.roll(p, 128 - k, 1), tail).astype(jnp.bfloat16)

    def near(j):
        return (NZ + (1 - 2 * ((j + 1) % 2)) * ((j + 1) // 2)) % NZ

    def g_receive(t):
        unpack(t, r)

        @pl.loop(1, NZ)
        def _(j):
            i = near(j)
            item = col(-i, yl)
            ref = gpart.at[t, item]
            send(ref, ref, sg.at[t, i], rg.at[t, i], sibling).wait_recv()
            send(ref, ref, sg.at[t, 8 + i], rg.at[t, 8 + i], sibling).start()
            unpack(t, item)

        @pl.loop(0, NZ)
        def _(j):
            i = near(j)
            item = col(-i, 1 - yl)
            ref = gpart.at[t, item]
            send(ref, ref, sg.at[t, 8 + i], rg.at[t, 8 + i], sibling).wait_recv()
            unpack(t, item)

        @pl.loop(1, 2 * NZ)
        def _(i):
            ref = gpart.at[t, r]
            send(ref, ref, sg.at[t, i], rg.at[t, i], sibling).wait_send()

    mine, other = oth.at[yh, x], oth.at[1 - yh, x]
    same(mine, YH, dev(yh=1 - yh))
    same(mine, XR, right)
    same(mine, XL, left)
    same(own.at[r, low], SIB0 + 8, sibling)
    same(own.at[r], UP, up)
    same(own.at[r], DN, down)
    g_send(0)

    landed(own.at[col(0, 1 - yl), low], SIB0 + 8)
    same(own.at[col(0, 1 - yl), low], UPS, up)
    same(own.at[col(0, 1 - yl), low], DNS, down)
    same(own.at[r, high], SIB0, sibling)

    xl, xr, xo = (x + NX - 1) % NX, (x + 1) % NX, (x + 2) % NX

    def x_first(hi, a, b, a2, b2):
        landed(oth.at[hi, xl], a)
        same(oth.at[hi, xl, low], a2, right)
        landed(oth.at[hi, xr], b)
        same(oth.at[hi, xr, high], b2, left)

    def x_last(hi, a2, b2):
        landed(oth.at[hi, xo, low], a2)
        landed(oth.at[hi, xo, high], b2)

    def z_own(s):
        a, b = col(-s, yl), col(s, yl)
        if s < 4:
            landed(own.at[a], UP + s - 1)
            same(own.at[a] if s < 3 else own.at[a, low], UP + s, up)
            same(own.at[a, high], SIB0 + s, sibling)
            landed(own.at[b], DN + s - 1)
            same(own.at[b] if s < 3 else own.at[b, high], DN + s, down)
            same(own.at[b, high], SIB0 + NZ - s, sibling)
        else:
            landed(own.at[a, high], DN + 3)
            same(own.at[a, high], SIB0 + 4, sibling)
            landed(own.at[a, low], UP + 3)

    def z_sib(s):
        a, b = col(-s, 1 - yl), col(s, 1 - yl)
        if s < 4:
            landed(own.at[a, low], UPS + s - 1)
            same(own.at[a, low if s < 3 else low_a], UPS + s, up)
            landed(own.at[b, low], DNS + s - 1)
            same(own.at[b, low if s < 3 else low_b], DNS + s, down)
        else:
            landed(own.at[a, low_a], UPS + 3)
            landed(own.at[a, low_b], DNS + 3)

    x_first(yh, XR, XL, XR2, XL2)
    z_own(1)
    landed(other, YH)
    same(other, HR, right)
    same(other, HL, left)
    z_sib(1)
    x_last(yh, XR2, XL2)
    z_own(2)
    x_first(1 - yh, HR, HL, HR2, HL2)
    z_sib(2)
    x_last(1 - yh, HR2, HL2)

    for t in range(ROUNDS):
        m = masks[t]
        stage[t] = oth[yh ^ (m // 8), x ^ ((m // 2) % 4)]
    core_copy = send(stage, sib_stage, s1.at[CORE], r1.at[CORE], dev(c=1 - c))
    pending.append(core_copy)
    core_copy.start()
    core_copy.wait_recv()
    for t in range(ROUNDS):
        crossed = masks[t] % 2 == 1
        theirs[t] = jnp.where(crossed, sib_stage[t].astype(jnp.float32), stage[t].astype(jnp.float32)).astype(jnp.bfloat16)

    def affinity(item):
        rows = own[item]
        at = pl.multiple_of(item * n, n)
        for t in range(ROUNDS):
            scores = lax.dot_general(theirs[t], rows, NT, preferred_element_type=jnp.float32)
            aff[t, :, pl.ds(at, n)] = jnp.exp(scores * scale).astype(jnp.bfloat16)

    def own_range(lo, hi):
        @pl.loop(lo, hi)
        def _(j):
            affinity(col(near(j), yl))

    def sib_range(lo, hi):
        @pl.loop(lo, hi)
        def _(j):
            i = near(j)
            item = col(-i, 1 - yl)
            landed(own.at[item, high], SIB0 + i)
            affinity(item)

    own_range(0, 5)
    z_own(3)
    z_sib(3)
    own_range(5, 7)
    sib_range(0, 5)
    z_own(4)
    own_range(7, 8)
    sib_range(5, 7)
    z_sib(4)
    sib_range(7, 8)

    before, grown = g0, g0
    for t in range(ROUNDS):
        if t > 0:
            gpart[t, r] = grown.astype(jnp.bfloat16)
            g_send(t)
        g_receive(t)
        product = lax.dot_general(aff[t], gfull[...], (((1,), (0,)), ((), ())), preferred_element_type=jnp.float32)
        carried = product[:, :k] / product[:, k:k + 1]
        xbufs[t][x] = pack(carried).astype(jnp.bfloat16)
        for i in range(1, NX):
            ref = xbufs[t].at[x]
            send(ref, ref, sc.at[t, i - 1], rc.at[t, i - 1], dev(x=(x + i) % NX)).start()
        for i in range(1, NX):
            ref = xbufs[t].at[(x + NX - i) % NX]
            send(ref, ref, sc.at[t, i - 1], rc.at[t, i - 1], sibling).wait_recv()
        m = masks[t]
        ybufs[t][yh * 2 + c] = xbufs[t][x ^ ((m // 2) % 4)]
        for i in range(1, 4):
            ref = ybufs[t].at[yh * 2 + c]
            device = dev(yh=(yh + i // 2) % 2, c=(c + i % 2) % 2)
            send(ref, ref, sc.at[t, 2 + i], rc.at[t, 2 + i], device).start()
        for i in range(1, 4):
            ref = ybufs[t].at[((yh + i // 2) % 2) * 2 + (c + i % 2) % 2]
            send(ref, ref, sc.at[t, 2 + i], rc.at[t, 2 + i], sibling).wait_recv()
        came = ybufs[t][(yh ^ (m // 8)) * 2 + (c ^ (m % 2))].astype(jnp.float32)
        before, grown = grown, grown + came
    grown_out[...] = grown

    top = jnp.where(lane < k, before, pltpu.roll(grown, k, 1))
    bottom = jnp.where(lane < k, pltpu.roll(before, k, 1), grown)
    prod[...] = (dot32(top, top, TN) + dot32(bottom, bottom, TN)).reshape(prod.shape)

    def total(ref, count):
        value = ref[0]
        for i in range(1, count):
            value = value + ref[i]
        return value

    def q_dev(i):
        return (yh * 2 * NX + (q + i) % (2 * NX), r)

    nq = 2 * NX

    @pl.loop(1, nq)
    def _(i):
        send(prod.at[(q + i) % nq], rs.at[q], sa.at[i], ra.at[i], q_dev(i)).start()

    rs[q] = prod[q]

    @pl.loop(1, nq)
    def _(i):
        send(prod.at[0], rs.at[(q + nq - i) % nq], sa.at[i], ra.at[i], sibling).wait_recv()

    ys[y] = total(rs, nq)

    @pl.loop(1, 4)
    def _(i):
        there = (y + i) % 4
        device = ((there // 2) * nq + q, z * 2 + there % 2)
        send(ys.at[y], ys.at[y], sa.at[8 + i], ra.at[8 + i], device).start()

    @pl.loop(1, 4)
    def _(i):
        ref = ys.at[(y + 4 - i) % 4]
        send(ref, ref, sa.at[8 + i], ra.at[8 + i], sibling).wait_recv()

    zs[z] = total(ys, 4)

    @pl.loop(1, NZ)
    def _(i):
        send(zs.at[z], zs.at[z], sa.at[12 + i], ra.at[12 + i], (o, ((z + i) % NZ) * 2 + yl)).start()

    @pl.loop(1, NZ)
    def _(i):
        ref = zs.at[(z + NZ - i) % NZ]
        send(ref, ref, sa.at[12 + i], ra.at[12 + i], sibling).wait_recv()

    fin[q] = total(zs, NZ)

    @pl.loop(1, nq)
    def _(i):
        send(fin.at[q], fin.at[q], sa.at[20 + i], ra.at[20 + i], q_dev(i)).start()

    @pl.loop(1, nq)
    def _(i):
        ref = fin.at[(q + nq - i) % nq]
        send(ref, ref, sa.at[20 + i], ra.at[20 + i], sibling).wait_recv()

    sums_out[...] = fin[...].reshape(sums_out.shape)

    for copy in pending:
        copy.wait_send()
    for t in range(ROUNDS):
        for i in range(6):
            ref = xbufs[t].at[x]
            send(ref, ref, sc.at[t, i], rc.at[t, i], sibling).wait_send()

    @pl.loop(1, nq)
    def _(i):
        send(fin.at[q], fin.at[q], sa.at[i], ra.at[i], sibling).wait_send()
        send(fin.at[q], fin.at[q], sa.at[12 + i], ra.at[12 + i], sibling).wait_send()
        send(fin.at[q], fin.at[q], sa.at[20 + i], ra.at[20 + i], sibling).wait_send()

    @pl.loop(1, 4)
    def _(i):
        send(fin.at[q], fin.at[q], sa.at[8 + i], ra.at[8 + i], sibling).wait_send()


def inverse_factor(gram):
    k = gram.shape[0]
    row = lax.broadcasted_iota(jnp.int32, (k, 2 * k), 0)
    lane = lax.broadcasted_iota(jnp.int32, (k, 2 * k), 1)
    rows = lax.broadcasted_iota(jnp.int32, (k, 1), 0)
    work = jnp.concatenate([gram, jnp.where(lane == row, 1.0, 0.0)[:, :k]], axis=1)
    for i in range(k - 1):
        first = (i + 1) // 8 * 8
        pivot = work[i:i + 1, :] * (1.0 / work[i:i + 1, i:i + 1])
        rest = work[first:, :]
        factor = jnp.where(rows[first:] > i, rest[:, i:i + 1], 0.0)
        rest = rest - factor * pivot
        work = rest if first == 0 else jnp.concatenate([work[:first], rest], axis=0)
    diagonal = jnp.sum(jnp.where(lane == row, work, 0.0), axis=1, keepdims=True)
    return work[:, k:] * (1.0 / jnp.sqrt(diagonal))


def finish_kernel(total_rows, grown, sums, iterate, ritz):
    k = ritz.shape[0]
    half = grown.shape[0]
    every = sums[...] * (1.0 / total_rows)
    inv_before = inverse_factor(every[:k, :k])
    inv_last = inverse_factor(every[k:, k:])
    packed = grown[...]
    iterate[:half, :] = dot32(packed[:, :k], inv_last, NT)
    iterate[half:, :] = dot32(packed[:, k:], inv_last, NT)
    left = dot32(inv_before, every[:k, k:], (((1,), (0,)), ((), ())))
    ritz[...] = dot32(left, inv_before, NT)


def shards(shots, basis, round_masks):
    n, feat = shots.shape
    k = basis.shape[1]
    nrep, nown = lax.axis_size("rep"), lax.axis_size("owner")
    half = n // 2
    bf, f32 = jnp.bfloat16, jnp.float32
    vmem = pl.BlockSpec(memory_space=pltpu.VMEM)
    slab = (2 * k) // (2 * NX)
    dma = pltpu.SemaphoreType.DMA
    grown, sums = pl.pallas_call(
        functools.partial(rounds_kernel, SHARPNESS / math.sqrt(feat)),
        out_shape=(jax.ShapeDtypeStruct((half, 2 * k), f32), jax.ShapeDtypeStruct((2 * k, 2 * k), f32)),
        in_specs=[pl.BlockSpec(memory_space=pltpu.SMEM), vmem, vmem],
        out_specs=(vmem, vmem),
        scratch_shapes=[
            pltpu.VMEM((nrep, n, feat), bf),
            pltpu.VMEM((2, NX, n, feat), bf),
            pltpu.VMEM((ROUNDS, n, feat), bf),
            pltpu.VMEM((ROUNDS, n, feat), bf),
            pltpu.VMEM((ROUNDS, n, feat), bf),
            pltpu.VMEM((ROUNDS, n, nrep * n), bf),
            pltpu.VMEM((ROUNDS, nrep, half, 2 * k), bf),
            pltpu.VMEM((nrep * n, 2 * k), bf),
            [pltpu.VMEM((NX, half, 2 * k), bf)] * ROUNDS,
            [pltpu.VMEM((4, half, 2 * k), bf)] * ROUNDS,
            pltpu.VMEM((2 * NX, slab, 2 * k), f32),
            pltpu.VMEM((4, slab, 2 * k), f32),
            pltpu.VMEM((NZ, slab, 2 * k), f32),
            pltpu.VMEM((2 * NX, slab, 2 * k), f32),
            pltpu.VMEM((2 * NX, slab, 2 * k), f32),
            dma((35,)), dma((35,)),
            dma((ROUNDS, 16)), dma((ROUNDS, 16)),
            dma((ROUNDS, 6)), dma((ROUNDS, 6)),
            dma((28,)), dma((28,)),
        ],
        compiler_params=pltpu.CompilerParams(
            collective_id=0, has_side_effects=True, vmem_limit_bytes=48 * 1024 * 1024
        ),
        name="rounds",
    )(round_masks, shots, basis)
    return pl.pallas_call(
        functools.partial(finish_kernel, float(nown * nrep * n)),
        out_shape=(jax.ShapeDtypeStruct((n, k), f32), jax.ShapeDtypeStruct((k, k), f32)),
        in_specs=[vmem, vmem],
        out_specs=(vmem, vmem),
        name="finish",
    )(grown, sums)


def solution(mesh):
    in_specs = (P(("owner", "rep"), None), P(("owner", "rep"), None), P())
    out_specs = (P(("owner", "rep"), None), P())
    return jax.shard_map(shards, mesh=mesh, in_specs=in_specs, out_specs=out_specs, check_vma=False)
```

time: 585 us -> 158 us (0.27)
  waiting for transfers between devices: 341 us -> 0 us
  Pallas kernels: 0 us -> 152 us
  blocking collectives: 117 us -> 0 us
  starting transfers between devices: 55.8 us -> 0 us
  other arithmetic: 27.3 us -> 0 us
  between operations: 22.2 us -> 0.68 us
  matrix products: 19.4 us -> 0 us
    psum x1 -> x0, waiting for transfers between devices: 239 us -> none  [shards(): sums = lax.psum(dot_tn(both, both), ('owner', 'rep')) / total_rows]
    pallas_call x0 -> x2, Pallas kernels: none -> 152 us  [the longest x1 145 us: shards(): pl.pallas_call(functools.partial(rounds_kernel, SHARPNESS / math.sqrt(fea...]
    all_gather x3 -> x0, blocking collectives: 117 us -> none  [shards(): lax.all_gather(grown.astype(jnp.bfloat16), 'rep', axis=0, tiled=True)]
    all_gather x1 -> x0, waiting for transfers between devices: 57.5 us -> none  [shards(): own_units = lax.all_gather(unit_rows, 'rep', axis=0, tiled=True)]
    ppermute x22 -> x0, starting transfers between devices: 55.7 us -> none  [swapped_2(): lax.ppermute(shard, axis, [(i, i ^ 1 << distance) for i in range(lax.axis...]
    ppermute x22 -> x0, waiting for transfers between devices: 44.6 us -> none  [swapped_2(): lax.ppermute(shard, axis, [(i, i ^ 1 << distance) for i in range(lax.axis...]
    another operation x8 -> x0, other arithmetic: 21.7 us -> none  [the longest x5 11.9 us: shards(): lower = jnp.linalg.cholesky(jnp.stack([sums[:k, :k], sums[k:, k:]]))]
    dot_general x7 -> x0, matrix products: 17.5 us -> none  [the longest x3 14.3 us: shards(): lax.dot_general(theirs, own_units, (((1,), (1,)), ((), ())), preferred_el...]
  transfers between devices with their start and end apart: 24 -> 0, of which waited for: 14 -> 0; matrix products, arithmetic and copies ran while one was open for 3% -> 0% of each run, Pallas kernels for 0% -> 0%
where the time goes in v2:
time: 158 us
  Pallas kernels  152 us (96%)
  local copies, waits for them, and re-layouts  4.79 us (3%)
    pallas_call x1, Pallas kernels, shards(): pl.pallas_call(functools.partial(rounds_kernel, SHARPNESS / math.sqrt(fea...  145 us
    pallas_call x1, Pallas kernels, shards(): pl.pallas_call(functools.partial(finish_kernel, float(nown * nrep * n)),...  7.57 us
    unnamed x9, local copies, waits for them, and re-layouts  3.18 us

profile of v2, /device:TPU:1, one launch (start us, length us, event | category | flops | bytes accessed | tf_op | source)
XLA Modules:
  0.0 157.8 jit_solution(1747582321483176823)
XLA Ops:
  0.6 0.0 copy-start.3
  0.6 0.9 copy.5.basis
  1.6 0.0 copy-done.3
  1.6 0.0 copy-start
  1.6 1.0 copy-done
  2.6 144.8 %rounds.1 = (f32[128,128]{1,0:T(8,128)S(1)}, f32[128,128]{1,0:T(8,128)S(1)}) custom-call(s32[3]{0:T(128)S(1)} %copy-done.3, bf16[256,768]{1,0:T(8,128)(2,1)S(1)} %copy-done, f32[256,64]{1,0:T(8,128)S(1)} %copy.5.basis), custom_call_target="tpu_custom_call" | custom-call | tf_op jit(solution)/shard_map/rounds/pallas_call | solution.py:401
  147.4 0.0 copy-start.1
  147.4 0.6 copy-done.1
  148.0 0.0 copy-start.2
  148.0 0.6 copy-done.2
  148.6 7.6 %finish.1 = (f32[256,64]{1,0:T(8,128)}, f32[64,64]{1,0:T(8,128)}) custom-call(f32[128,128]{1,0:T(8,128)} %copy-done.1, f32[128,128]{1,0:T(8,128)} %copy-done.2), custom_call_target="tpu_custom_call" | custom-call | tf_op jit(solution)/shard_map/finish/pallas_call | solution.py:432
  156.2 1.6 %copy.6 = f32[256,64]{0,1:T(8,128)} copy(f32[256,64]{1,0:T(8,128)} %get-tuple-element.6) | data formatting | bytes 131072 | tf_op jit(solution)/shard_map/finish/pallas_call | solution.py:432
Async XLA Ops:
  0.6 1.0 copy-start.3
  1.6 1.0 copy-start
  147.4 0.6 copy-start.1
  148.0 0.6 copy-start.2

commit v3 on v1

v3 whole, which is shorter than its diff:
```python
import functools
import math

import jax
import jax.numpy as jnp
from jax import lax
from jax.experimental import pallas as pl
from jax.experimental.pallas import tpu as pltpu
from jax.sharding import PartitionSpec as P

ROUNDS = 3
SHARPNESS = 1.6
MESH = pl.DeviceIdType.MESH
NT = (((1,), (1,)), ((), ()))
TN = (((0,), (0,)), ((), ()))
NX, NY, NZ = 4, 4, 8


def dot32(a, b, dims):
    return lax.dot_general(a, b, dims, precision=lax.Precision.HIGHEST, preferred_element_type=jnp.float32)


def pack(rows):
    half = rows.shape[0] // 2
    return jnp.concatenate([rows[:half], rows[half:]], axis=1)


def rounds_kernel(
    scale, masks, shots, basis_t, grown_out, sums_out,
    unit, oth, own, stage, sib_stage, aff, gpart, gfull, wsend, wrecv, xbufs, ybufs, homeward, ghome, gsend, gback, gx, gy,
    rs, ys, zs, fin, prod,
    s1, r1, sg, rg, sc, rc, sw, rw, sa, ra,
):
    n, feat = shots.shape
    half, quarter = n // 2, n // 4
    k = basis_t.shape[0]
    o, r = lax.axis_index("owner"), lax.axis_index("rep")
    c, x, yh = o % 2, (o // 2) % NX, o // (2 * NX)
    z, yl = r // 2, r % 2
    y = yh * 2 + yl
    nq = 2 * NX
    q = x * 2 + c

    def dev(y=y, x=x, c=c, z=z):
        return (((y // 2) * NX + x) * 2 + c, z * 2 + y % 2)

    twin_y = yh * 2 + c
    twin = dev(y=twin_y, c=yl)
    other_core = dev(c=1 - c)
    moved = c != yl
    stays = c == yl

    bar = pltpu.get_barrier_semaphore()

    def hello(device):
        pl.semaphore_signal(bar, inc=1, device_id=device, device_id_type=MESH)

    @pl.loop(1, NZ)
    def _(i):
        hello(dev(z=(z + i) % NZ))

    @pl.loop(1, NX)
    def _(i):
        for core in range(2):
            hello(dev(x=(x + i) % NX, c=core))
            hello(dev(y=(y + i) % NY, c=core))

    hello(other_core)

    values = shots[...].astype(jnp.float32)
    inv = lax.rsqrt(jnp.mean(values * values, axis=-1, keepdims=True) + 1e-06)
    units = (values * inv).astype(jnp.bfloat16)
    g0 = pack(basis_t[...].T)

    @pl.when(stays)
    def _():
        oth[y, x] = units
        ghome[...] = g0

    @pl.when(moved)
    def _():
        unit[...] = units
        gsend[0] = g0

    pl.semaphore_wait(bar, (NZ - 1) + 2 * (NX - 1) + 2 * (NY - 1) + 1)

    def send(src, dst, ssem, rsem, device):
        return pltpu.make_async_remote_copy(
            src_ref=src, dst_ref=dst, send_sem=ssem, recv_sem=rsem, device_id=device, device_id_type=MESH
        )

    pending = []

    def move(src, dst, number, device):
        copy = send(src, dst, s1.at[number], r1.at[number], device)
        pending.append(copy)
        copy.start()

    def same(ref, number, device):
        move(ref, ref, number, device)

    def landed(ref, number):
        send(ref, ref, s1.at[number], r1.at[number], other_core).wait_recv()

    halves = (pl.ds(0, half), pl.ds(half, half))
    quarters = tuple((pl.ds(i * half, quarter), pl.ds(i * half + quarter, quarter)) for i in range(2))

    RING, UP, DN, CORE, TRADE = 0, 40, 47, 54, 57

    trades = [
        send(unit.at[halves[0]], oth.at[twin_y, x, halves[0]], s1.at[TRADE], r1.at[TRADE], twin),
        send(unit.at[halves[1]], oth.at[twin_y, x, halves[1]], s1.at[TRADE + 1], r1.at[TRADE + 1], twin),
        send(gsend.at[0], ghome, s1.at[TRADE + 2], r1.at[TRADE + 2], twin),
    ]

    @pl.when(moved)
    def _():
        for copy in trades:
            copy.start()

    def step(axis, i):
        return dev(x=(x + i) % NX) if axis == 0 else dev(y=(y + i) % NY)

    def at(axis, i, j):
        dx, dy = (i, j) if axis == 0 else (j, i)
        return (y + dy) % NY, (x + dx) % NX

    def ring(axis, h, j, first):
        return RING + 4 * ((5 * h) + (0 if first else 1 + j % 4))

    def begin(axis, h, j, first=False):
        number = ring(axis, h, j, first)
        ref = oth.at[(*at(axis, 0, j), halves[h])]
        same(ref, number, step(axis, 1))
        same(ref, number + 1, step(axis, -1 % 4))

    def onward(axis, h, j, first=False):
        number = ring(axis, h, j, first)
        landed(oth.at[(*at(axis, 3, j), halves[h])], number)
        same(oth.at[(*at(axis, 3, j), quarters[h][0])], number + 2, step(axis, 1))
        landed(oth.at[(*at(axis, 1, j), halves[h])], number + 1)
        same(oth.at[(*at(axis, 1, j), quarters[h][1])], number + 3, step(axis, 3))

    def last(axis, h, j, first=False):
        number = ring(axis, h, j, first)
        landed(oth.at[(*at(axis, 2, j), quarters[h][0])], number + 2)
        landed(oth.at[(*at(axis, 2, j), quarters[h][1])], number + 3)

    up, down = dev(z=(z + 1) % NZ), dev(z=(z + NZ - 1) % NZ)

    def z_begin(h):
        move(oth.at[y, x, halves[h]], own.at[z, halves[h]], UP + h, up)
        move(oth.at[y, x, halves[h]], own.at[z, halves[h]], DN + h, down)

    def z_on(s, h):
        a, b = (z + NZ - s) % NZ, (z + s) % NZ
        landed(own.at[a, halves[h]], UP + 2 * (s - 1) + h)
        if s < 3 or h == 0:
            same(own.at[a, halves[h]], UP + 2 * s + (h if s < 3 else 0), up)
        landed(own.at[b, halves[h]], DN + 2 * (s - 1) + h)
        if s < 3 or h == 1:
            same(own.at[b, halves[h]], DN + 2 * s + (h if s < 3 else 0), down)

    def z_last():
        a = (z + 4) % NZ
        landed(own.at[a, halves[0]], UP + 6)
        landed(own.at[a, halves[1]], DN + 6)

    for h in range(2):
        @pl.when(moved)
        def _(h=h):
            send(unit.at[halves[h]], oth.at[y, x, halves[h]], s1.at[TRADE + h], r1.at[TRADE + h], twin).wait_recv()

        begin(h, h, 0, first=True)
        z_begin(h)
        begin(1 - h, h, 0)

    onward(0, 0, 0, first=True)
    begin(1, 0, 3)
    begin(1, 0, 1)
    z_on(1, 0)
    onward(1, 1, 0, first=True)
    begin(0, 1, 3)
    begin(0, 1, 1)
    z_on(1, 1)
    onward(1, 0, 0)
    onward(0, 1, 0)
    last(0, 0, 0, first=True)
    begin(1, 0, 2)
    last(1, 1, 0, first=True)
    begin(0, 1, 2)
    z_on(2, 0)
    own[z] = oth[y, x]
    z_on(2, 1)
    onward(1, 0, 3)
    onward(0, 1, 3)
    last(1, 0, 0)
    last(0, 1, 0)
    onward(1, 0, 1)
    onward(0, 1, 1)
    z_on(3, 0)
    z_on(3, 1)

    @pl.when(moved)
    def _():
        send(gsend.at[0], ghome, s1.at[TRADE + 2], r1.at[TRADE + 2], twin).wait_recv()

    def g_send(t, value):
        gpart[t, z] = value.astype(jnp.bfloat16)

        @pl.loop(1, NZ)
        def _(i):
            send(gpart.at[t, z], gpart.at[t, z], sg.at[t, i], rg.at[t, i], dev(z=(z + i) % NZ)).start()

    grown = ghome[...]
    g_send(0, grown)

    onward(1, 0, 2)
    onward(0, 1, 2)
    last(1, 0, 3)
    last(0, 1, 3)
    last(1, 0, 1)
    last(0, 1, 1)
    last(1, 0, 2)
    last(0, 1, 2)

    def partner(t):
        m = masks[t]
        return y ^ ((m // 8) * 2 + m % 2), x ^ ((m // 2) % 4)

    for t in range(ROUNDS):
        py, px = partner(t)
        stage[t] = oth[py, px]
        move(stage.at[t], sib_stage.at[t], CORE + t, other_core)

    def affinity(t, rows, item, part):
        scores = lax.dot_general(rows, own[item], NT, preferred_element_type=jnp.float32)
        columns = pl.ds(pl.multiple_of(item * n, n), n)
        aff[t, part * n:(part + 1) * n, columns] = jnp.exp(scores * scale).astype(jnp.bfloat16)

    def affinities(t):
        @pl.loop(0, NZ)
        def _(item):
            affinity(t, stage[t], item, 0)

        landed(sib_stage.at[t], CORE + t)

        @pl.loop(0, NZ)
        def _(item):
            affinity(t, sib_stage[t], item, 1)

    z_last()
    affinities(0)

    lane = lax.broadcasted_iota(jnp.int32, (half, 2 * k), 1)
    tail = jnp.where(lane == k, 1.0, 0.0)

    def unpack(t, item):
        p = gpart[t, item].astype(jnp.float32)
        start = pl.multiple_of(item * n, n)
        gfull[pl.ds(start, half), :] = jnp.where(lane < k, p, tail).astype(jnp.bfloat16)
        gfull[pl.ds(start + half, half), :] = jnp.where(lane < k, pltpu.roll(p, k, 1), tail).astype(jnp.bfloat16)

    def near(j):
        return (NZ + (1 - 2 * ((j + 1) % 2)) * ((j + 1) // 2)) % NZ

    def carried(t):
        unpack(t, z)

        @pl.loop(1, NZ)
        def _(j):
            i = near(j)
            item = (z + NZ - i) % NZ
            ref = gpart.at[t, item]
            send(ref, ref, sg.at[t, i], rg.at[t, i], other_core).wait_recv()
            unpack(t, item)

        wsend[t] = jnp.dot(aff[t, n:, :], gfull[...], preferred_element_type=jnp.float32)
        copy = send(wsend.at[t], wrecv.at[t], sw.at[t], rw.at[t], other_core)
        copy.start()
        mine = jnp.dot(aff[t, :n, :], gfull[...], preferred_element_type=jnp.float32)
        copy.wait_recv()
        product = mine + wrecv[t]
        return pack(product[:, :k] / product[:, k:k + 1]).astype(jnp.bfloat16)

    def x_send(ref, sems, t, base):
        for i in range(1, NX):
            send(ref, ref, sems[0].at[t, base + i], sems[1].at[t, base + i], dev(x=(x + i) % NX)).start()

    def x_wait(buf, sems, t, base):
        for i in range(1, NX):
            ref = buf.at[(x + NX - i) % NX]
            send(ref, ref, sems[0].at[t, base + i], sems[1].at[t, base + i], other_core).wait_recv()

    def y_send(ref, sems, t, base):
        for i in range(1, NY):
            send(ref, ref, sems[0].at[t, base + i], sems[1].at[t, base + i], dev(y=(y + i) % NY)).start()

    def y_wait(buf, sems, t, base):
        for i in range(1, NY):
            ref = buf.at[(y + NY - i) % NY]
            send(ref, ref, sems[0].at[t, base + i], sems[1].at[t, base + i], other_core).wait_recv()

    csem = (sc, rc)
    for t in range(ROUNDS - 1):
        if t > 0:
            g_send(t, grown)
        py, px = partner(t)
        xbufs[t][x] = carried(t)
        x_send(xbufs[t].at[x], csem, t, 0)
        if t == 0:
            affinities(1)
        x_wait(xbufs[t], csem, t, 0)
        ybufs[t][y] = xbufs[t][px]
        y_send(ybufs[t].at[y], csem, t, 4)
        if t == 0:
            affinities(2)
        y_wait(ybufs[t], csem, t, 4)
        grown = grown + ybufs[t][py].astype(jnp.float32)

    t = ROUNDS - 1
    py, px = partner(t)
    g_send(t, grown)
    gx[x] = grown
    x_send(gx.at[x], csem, ROUNDS, 0)

    @pl.when(stays)
    def _():
        gback[...] = grown

    @pl.when(moved)
    def _():
        gsend[1] = grown
        send(gsend.at[1], gback, s1.at[TRADE + 3], r1.at[TRADE + 3], twin).start()

    x_wait(gx, csem, ROUNDS, 0)
    gy[y] = gx[px]
    y_send(gy.at[y], csem, ROUNDS, 4)
    came = carried(t)
    xbufs[t][x] = came
    x_send(xbufs[t].at[x], csem, t, 0)
    y_wait(gy, csem, ROUNDS, 4)
    before = gy[py]
    after = before + came.astype(jnp.float32)

    top = jnp.where(lane < k, before, pltpu.roll(after, k, 1))
    bottom = jnp.where(lane < k, pltpu.roll(before, k, 1), after)
    prod[...] = (dot32(top, top, TN) + dot32(bottom, bottom, TN)).reshape(prod.shape)

    def total(ref, count):
        value = ref[0]
        for i in range(1, count):
            value = value + ref[i]
        return value

    def q_dev(i):
        there = (q + i) % nq
        return dev(x=there // 2, c=there % 2)

    @pl.loop(1, nq)
    def _(i):
        send(prod.at[(q + i) % nq], rs.at[q], sa.at[i], ra.at[i], q_dev(i)).start()

    rs[q] = prod[q]

    x_wait(xbufs[t], csem, t, 0)
    homeward[...] = xbufs[t][px]

    @pl.when(stays)
    def _():
        ybufs[t][y] = homeward[...]

    def home_copy(i):
        ty = (y + i) % NY
        device = dev(y=(ty // 2) * 2 + c, c=ty % 2)
        return send(homeward, ybufs[t].at[y], sc.at[t, 4 + i], rc.at[t, 4 + i], device)

    @pl.when(moved)
    def _():
        home_copy(0).start()

    for i in range(1, NY):
        home_copy(i).start()

    @pl.loop(1, nq)
    def _(i):
        send(prod.at[0], rs.at[(q + nq - i) % nq], sa.at[i], ra.at[i], other_core).wait_recv()

    ys[y] = total(rs, nq)

    @pl.loop(1, NY)
    def _(i):
        send(ys.at[y], ys.at[y], sa.at[8 + i], ra.at[8 + i], dev(y=(y + i) % NY)).start()

    @pl.loop(1, NY)
    def _(i):
        ref = ys.at[(y + NY - i) % NY]
        send(ref, ref, sa.at[8 + i], ra.at[8 + i], other_core).wait_recv()

    zs[z] = total(ys, NY)

    @pl.loop(1, NZ)
    def _(i):
        send(zs.at[z], zs.at[z], sa.at[12 + i], ra.at[12 + i], dev(z=(z + i) % NZ)).start()

    @pl.loop(1, NZ)
    def _(i):
        ref = zs.at[(z + NZ - i) % NZ]
        send(ref, ref, sa.at[12 + i], ra.at[12 + i], other_core).wait_recv()

    fin[q] = total(zs, NZ)

    @pl.loop(1, nq)
    def _(i):
        send(fin.at[q], fin.at[q], sa.at[20 + i], ra.at[20 + i], q_dev(i)).start()

    @pl.when(moved)
    def _():
        send(gsend.at[1], gback, s1.at[TRADE + 3], r1.at[TRADE + 3], twin).wait_recv()
        ref = ybufs[t].at[twin_y]
        send(ref, ref, sc.at[t, 4], rc.at[t, 4], other_core).wait_recv()

    for i in range(1, NY):
        ref = ybufs[t].at[(twin_y + NY - i) % NY]
        send(ref, ref, sc.at[t, 4 + i], rc.at[t, 4 + i], other_core).wait_recv()
    m = masks[t]
    grown_out[...] = gback[...] + ybufs[t][twin_y ^ ((m // 8) * 2 + m % 2)].astype(jnp.float32)

    @pl.loop(1, nq)
    def _(i):
        ref = fin.at[(q + nq - i) % nq]
        send(ref, ref, sa.at[20 + i], ra.at[20 + i], other_core).wait_recv()

    sums_out[...] = fin[...].reshape(sums_out.shape)

    for copy in pending:
        copy.wait_send()

    @pl.when(moved)
    def _():
        for copy in trades:
            copy.wait_send()
        send(gsend.at[1], gback, s1.at[TRADE + 3], r1.at[TRADE + 3], twin).wait_send()
        home_copy(0).wait_send()

    @pl.loop(1, NX)
    def _(i):
        for row in range(ROUNDS):
            ref = xbufs[row].at[x]
            send(ref, ref, sc.at[row, i], rc.at[row, i], other_core).wait_send()
            send(ref, ref, sc.at[row, 4 + i], rc.at[row, 4 + i], other_core).wait_send()
        ref = gx.at[x]
        send(ref, ref, sc.at[ROUNDS, i], rc.at[ROUNDS, i], other_core).wait_send()
        send(ref, ref, sc.at[ROUNDS, 4 + i], rc.at[ROUNDS, 4 + i], other_core).wait_send()
        send(ys.at[y], ys.at[y], sa.at[8 + i], ra.at[8 + i], other_core).wait_send()

    @pl.loop(1, NZ)
    def _(i):
        for row in range(ROUNDS):
            ref = gpart.at[row, z]
            send(ref, ref, sg.at[row, i], rg.at[row, i], other_core).wait_send()
        for base in (0, 12, 20):
            send(fin.at[q], fin.at[q], sa.at[base + i], ra.at[base + i], other_core).wait_send()

    for row in range(ROUNDS):
        send(wsend.at[row], wrecv.at[row], sw.at[row], rw.at[row], other_core).wait_send()


def inverse_factor(gram):
    k = gram.shape[0]
    row = lax.broadcasted_iota(jnp.int32, (k, 2 * k), 0)
    lane = lax.broadcasted_iota(jnp.int32, (k, 2 * k), 1)
    rows = lax.broadcasted_iota(jnp.int32, (k, 1), 0)
    work = jnp.concatenate([gram, jnp.where(lane == row, 1.0, 0.0)[:, :k]], axis=1)
    for i in range(k - 1):
        first = (i + 1) // 8 * 8
        pivot = work[i:i + 1, :] * (1.0 / work[i:i + 1, i:i + 1])
        rest = work[first:, :]
        factor = jnp.where(rows[first:] > i, rest[:, i:i + 1], 0.0)
        rest = rest - factor * pivot
        work = rest if first == 0 else jnp.concatenate([work[:first], rest], axis=0)
    diagonal = jnp.sum(jnp.where(lane == row, work, 0.0), axis=1, keepdims=True)
    return work[:, k:] * (1.0 / jnp.sqrt(diagonal))


def finish_kernel(total_rows, grown, sums, iterate_t, ritz):
    k = ritz.shape[0]
    half = grown.shape[0]
    every = sums[...] * (1.0 / total_rows)
    inv_before = inverse_factor(every[:k, :k])
    inv_last = inverse_factor(every[k:, k:])
    packed = grown[...]
    iterate_t[:, :half] = dot32(inv_last, packed[:, :k], NT)
    iterate_t[:, half:] = dot32(inv_last, packed[:, k:], NT)
    left = dot32(inv_before, every[:k, k:], (((1,), (0,)), ((), ())))
    ritz[...] = dot32(left, inv_before, NT)


def shards(shots, basis, round_masks):
    n, feat = shots.shape
    k = basis.shape[1]
    nrep, nown = lax.axis_size("rep"), lax.axis_size("owner")
    half = n // 2
    bf, f32 = jnp.bfloat16, jnp.float32
    vmem = pl.BlockSpec(memory_space=pltpu.VMEM)
    slab = (2 * k) // (2 * NX)
    dma = pltpu.SemaphoreType.DMA
    grown, sums = pl.pallas_call(
        functools.partial(rounds_kernel, SHARPNESS / math.sqrt(feat)),
        out_shape=(jax.ShapeDtypeStruct((half, 2 * k), f32), jax.ShapeDtypeStruct((2 * k, 2 * k), f32)),
        in_specs=[pl.BlockSpec(memory_space=pltpu.SMEM), vmem, vmem],
        out_specs=(vmem, vmem),
        scratch_shapes=[
            pltpu.VMEM((n, feat), bf),
            pltpu.VMEM((NY, NX, n, feat), bf),
            pltpu.VMEM((NZ, n, feat), bf),
            pltpu.VMEM((ROUNDS, n, feat), bf),
            pltpu.VMEM((ROUNDS, n, feat), bf),
            pltpu.VMEM((ROUNDS, 2 * n, NZ * n), bf),
            pltpu.VMEM((ROUNDS, NZ, half, 2 * k), bf),
            pltpu.VMEM((NZ * n, 2 * k), bf),
            pltpu.VMEM((ROUNDS, n, 2 * k), f32),
            pltpu.VMEM((ROUNDS, n, 2 * k), f32),
            [pltpu.VMEM((NX, half, 2 * k), bf)] * ROUNDS,
            [pltpu.VMEM((NY, half, 2 * k), bf)] * ROUNDS,
            pltpu.VMEM((half, 2 * k), bf),
            pltpu.VMEM((half, 2 * k), f32),
            pltpu.VMEM((2, half, 2 * k), f32),
            pltpu.VMEM((half, 2 * k), f32),
            pltpu.VMEM((NX, half, 2 * k), f32),
            pltpu.VMEM((NY, half, 2 * k), f32),
            pltpu.VMEM((2 * NX, slab, 2 * k), f32),
            pltpu.VMEM((NY, slab, 2 * k), f32),
            pltpu.VMEM((NZ, slab, 2 * k), f32),
            pltpu.VMEM((2 * NX, slab, 2 * k), f32),
            pltpu.VMEM((2 * NX, slab, 2 * k), f32),
            dma((61,)), dma((61,)),
            dma((ROUNDS, NZ)), dma((ROUNDS, NZ)),
            dma((ROUNDS + 1, 8)), dma((ROUNDS + 1, 8)),
            dma((ROUNDS,)), dma((ROUNDS,)),
            dma((28,)), dma((28,)),
        ],
        compiler_params=pltpu.CompilerParams(
            collective_id=0, has_side_effects=True, vmem_limit_bytes=48 * 1024 * 1024
        ),
        name="rounds",
    )(round_masks, shots, basis.T)
    iterate_t, ritz = pl.pallas_call(
        functools.partial(finish_kernel, float(nown * nrep * n)),
        out_shape=(jax.ShapeDtypeStruct((k, n), f32), jax.ShapeDtypeStruct((k, k), f32)),
        in_specs=[vmem, vmem],
        out_specs=(vmem, vmem),
        name="finish",
    )(grown, sums)
    return iterate_t.T, ritz


def solution(mesh):
    in_specs = (P(("owner", "rep"), None), P(("owner", "rep"), None), P())
    out_specs = (P(("owner", "rep"), None), P())
    return jax.shard_map(shards, mesh=mesh, in_specs=in_specs, out_specs=out_specs, check_vma=False)
```

time: 585 us -> 135 us (0.23)
  waiting for transfers between devices: 341 us -> 0 us
  Pallas kernels: 0 us -> 131 us
  blocking collectives: 117 us -> 0 us
  starting transfers between devices: 55.8 us -> 0 us
  other arithmetic: 27.3 us -> 0 us
  between operations: 22.2 us -> 0.66 us
  matrix products: 19.4 us -> 0 us
    psum x1 -> x0, waiting for transfers between devices: 239 us -> none  [shards(): sums = lax.psum(dot_tn(both, both), ('owner', 'rep')) / total_rows]
    pallas_call x0 -> x2, Pallas kernels: none -> 131 us  [the longest x1 123 us: shards(): pl.pallas_call(functools.partial(rounds_kernel, SHARPNESS / math.sqrt(fea...]
    all_gather x3 -> x0, blocking collectives: 117 us -> none  [shards(): lax.all_gather(grown.astype(jnp.bfloat16), 'rep', axis=0, tiled=True)]
    all_gather x1 -> x0, waiting for transfers between devices: 57.5 us -> none  [shards(): own_units = lax.all_gather(unit_rows, 'rep', axis=0, tiled=True)]
    ppermute x22 -> x0, starting transfers between devices: 55.7 us -> none  [swapped_2(): lax.ppermute(shard, axis, [(i, i ^ 1 << distance) for i in range(lax.axis...]
    ppermute x22 -> x0, waiting for transfers between devices: 44.6 us -> none  [swapped_2(): lax.ppermute(shard, axis, [(i, i ^ 1 << distance) for i in range(lax.axis...]
    another operation x8 -> x0, other arithmetic: 21.7 us -> none  [the longest x5 11.9 us: shards(): lower = jnp.linalg.cholesky(jnp.stack([sums[:k, :k], sums[k:, k:]]))]
    dot_general x7 -> x0, matrix products: 17.5 us -> none  [the longest x3 14.3 us: shards(): lax.dot_general(theirs, own_units, (((1,), (1,)), ((), ())), preferred_el...]
  transfers between devices with their start and end apart: 24 -> 0, of which waited for: 14 -> 0; matrix products, arithmetic and copies ran while one was open for 3% -> 0% of each run, Pallas kernels for 0% -> 0%
where the time goes in v3:
time: 135 us
  Pallas kernels  131 us (97%)
  local copies, waits for them, and re-layouts  3.73 us (3%)
    pallas_call x1, Pallas kernels, shards(): pl.pallas_call(functools.partial(rounds_kernel, SHARPNESS / math.sqrt(fea...  123 us
    pallas_call x1, Pallas kernels, shards(): pl.pallas_call(functools.partial(finish_kernel, float(nown * nrep * n)),...  7.71 us
    unnamed x10, local copies, waits for them, and re-layouts  3.73 us

profile of v3, /device:TPU:1, one launch (start us, length us, event | category | flops | bytes accessed | tf_op | source)
XLA Modules:
  0.0 135.2 jit_solution(11075727155137172782)
XLA Ops:
  0.6 0.0 copy-start.4
  0.6 0.6 copy-done.4
  1.3 0.0 copy-start
  1.3 1.0 copy-done
  2.3 0.0 copy-start.3
  2.3 0.8 copy-done.3
  3.1 123.1 %rounds.1 = (f32[128,128]{1,0:T(8,128)S(1)}, f32[128,128]{1,0:T(8,128)S(1)}) custom-call(s32[3]{0:T(128)S(1)} %copy-done.4, bf16[256,768]{1,0:T(8,128)(2,1)S(1)} %copy-done, f32[64,256]{1,0:T(8,128)S(1)} %bitcast.2), custom_call_target="tpu_custom_call" | custom-call | tf_op jit(solution)/shard_map/rounds/pallas_call | solution.py:508
  126.3 0.0 copy-start.1
  126.3 0.6 copy-done.1
  126.9 0.0 copy-start.2
  126.9 0.6 copy-done.2
  127.5 7.7 %finish.1 = (f32[64,256]{1,0:T(8,128)}, f32[64,64]{1,0:T(8,128)}) custom-call(f32[128,128]{1,0:T(8,128)} %copy-done.1, f32[128,128]{1,0:T(8,128)} %copy-done.2), custom_call_target="tpu_custom_call" | custom-call | tf_op jit(solution)/shard_map/finish/pallas_call | solution.py:548
Async XLA Ops:
  0.6 0.7 copy-start.4
  1.3 1.0 copy-start
  2.3 0.8 copy-start.3
  126.3 0.6 copy-start.1
  126.9 0.6 copy-start.2

commit v4 on v3

--- a/solution.py
+++ b/solution.py
@@ -26,10 +26,10 @@
 
 
 def rounds_kernel(
-    scale, masks, shots, basis_t, grown_out, sums_out,
-    unit, oth, own, stage, sib_stage, aff, gpart, gfull, wsend, wrecv, xbufs, ybufs, homeward, ghome, gsend, gback, gx, gy,
+    scale, masks_hbm, shots_hbm, basis_hbm, out,
+    masks, shots, basis_t, oth, own, cands, aff, gpart, gfull, wsend, wrecv, xbufs, ybufs, homeward, ghome, gsend, gback, gx, gy,
     rs, ys, zs, fin, prod,
-    s1, r1, sg, rg, sc, rc, sw, rw, sa, ra,
+    s_in, s1, r1, sg, rg, sc, rc, sw, rw, sa, ra,
 ):
     n, feat = shots.shape
     half, quarter = n // 2, n // 4
@@ -50,6 +50,14 @@
     moved = c != yl
     stays = c == yl
 
+    loads = [
+        pltpu.make_async_copy(shots_hbm, shots, s_in.at[0]),
+        pltpu.make_async_copy(basis_hbm, basis_t, s_in.at[1]),
+        pltpu.make_async_copy(masks_hbm, masks, s_in.at[2]),
+    ]
+    for copy in loads:
+        copy.start()
+
     bar = pltpu.get_barrier_semaphore()
 
     def hello(device):
@@ -67,19 +75,20 @@
 
     hello(other_core)
 
+    for copy in loads:
+        copy.wait()
     values = shots[...].astype(jnp.float32)
     inv = lax.rsqrt(jnp.mean(values * values, axis=-1, keepdims=True) + 1e-06)
-    units = (values * inv).astype(jnp.bfloat16)
+    oth[y, x] = (values * inv).astype(jnp.bfloat16)
     g0 = pack(basis_t[...].T)
 
     @pl.when(stays)
     def _():
-        oth[y, x] = units
+        own[z] = oth[y, x]
         ghome[...] = g0
 
     @pl.when(moved)
     def _():
-        unit[...] = units
         gsend[0] = g0
 
     pl.semaphore_wait(bar, (NZ - 1) + 2 * (NX - 1) + 2 * (NY - 1) + 1)
@@ -91,10 +100,14 @@
 
     pending = []
 
+    def all_sent(numbers):
+        for number, rows in numbers:
+            ref = oth.at[0, 0, pl.ds(0, rows)]
+            send(ref, ref, s1.at[number], r1.at[number], other_core).wait_send()
+
     def move(src, dst, number, device):
-        copy = send(src, dst, s1.at[number], r1.at[number], device)
-        pending.append(copy)
-        copy.start()
+        send(src, dst, s1.at[number], r1.at[number], device).start()
+        pending.append((number, src.shape[0]))
 
     def same(ref, number, device):
         move(ref, ref, number, device)
@@ -107,16 +120,7 @@
 
     RING, UP, DN, CORE, TRADE = 0, 40, 47, 54, 57
 
-    trades = [
-        send(unit.at[halves[0]], oth.at[twin_y, x, halves[0]], s1.at[TRADE], r1.at[TRADE], twin),
-        send(unit.at[halves[1]], oth.at[twin_y, x, halves[1]], s1.at[TRADE + 1], r1.at[TRADE + 1], twin),
-        send(gsend.at[0], ghome, s1.at[TRADE + 2], r1.at[TRADE + 2], twin),
-    ]
-
-    @pl.when(moved)
-    def _():
-        for copy in trades:
-            copy.start()
+    trade = send(gsend.at[0], ghome, s1.at[TRADE + 2], r1.at[TRADE + 2], twin)
 
     def step(axis, i):
         return dev(x=(x + i) % NX) if axis == 0 else dev(y=(y + i) % NY)
@@ -149,8 +153,8 @@
     up, down = dev(z=(z + 1) % NZ), dev(z=(z + NZ - 1) % NZ)
 
     def z_begin(h):
-        move(oth.at[y, x, halves[h]], own.at[z, halves[h]], UP + h, up)
-        move(oth.at[y, x, halves[h]], own.at[z, halves[h]], DN + h, down)
+        same(own.at[z, halves[h]], UP + h, up)
+        same(own.at[z, halves[h]], DN + h, down)
 
     def z_on(s, h):
         a, b = (z + NZ - s) % NZ, (z + s) % NZ
@@ -166,50 +170,95 @@
         landed(own.at[a, halves[0]], UP + 6)
         landed(own.at[a, halves[1]], DN + 6)
 
-    for h in range(2):
-        @pl.when(moved)
-        def _(h=h):
-            send(unit.at[halves[h]], oth.at[y, x, halves[h]], s1.at[TRADE + h], r1.at[TRADE + h], twin).wait_recv()
-
-        begin(h, h, 0, first=True)
-        z_begin(h)
-        begin(1 - h, h, 0)
-
-    onward(0, 0, 0, first=True)
-    begin(1, 0, 3)
-    begin(1, 0, 1)
-    z_on(1, 0)
-    onward(1, 1, 0, first=True)
-    begin(0, 1, 3)
-    begin(0, 1, 1)
-    z_on(1, 1)
-    onward(1, 0, 0)
-    onward(0, 1, 0)
-    last(0, 0, 0, first=True)
-    begin(1, 0, 2)
-    last(1, 1, 0, first=True)
-    begin(0, 1, 2)
-    z_on(2, 0)
-    own[z] = oth[y, x]
-    z_on(2, 1)
-    onward(1, 0, 3)
-    onward(0, 1, 3)
-    last(1, 0, 0)
-    last(0, 1, 0)
-    onward(1, 0, 1)
-    onward(0, 1, 1)
-    z_on(3, 0)
-    z_on(3, 1)
+    def hand_over(h):
+        src = oth.at[yh * 2 + 1 - yl, x, halves[h]]
+        move(src, own.at[z, halves[h]], TRADE + h, other_core)
+
+    @pl.when(stays)
+    def _():
+        z_begin(0)
+        z_begin(1)
+        begin(0, 0, 0, first=True)
+        begin(1, 1, 0, first=True)
+        begin(0, 1, 0)
+        begin(1, 0, 0)
+        onward(1, 1, 0, first=True)
+        hand_over(1)
+        begin(0, 1, 3)
+        begin(0, 1, 1)
+        onward(0, 0, 0, first=True)
+        begin(1, 0, 3)
+        begin(1, 0, 1)
+        z_on(1, 0)
+        onward(1, 0, 0)
+        hand_over(0)
+        onward(0, 1, 0)
+        z_on(1, 1)
+        last(0, 0, 0, first=True)
+        begin(1, 0, 2)
+        last(1, 1, 0, first=True)
+        begin(0, 1, 2)
+        z_on(2, 0)
+        z_on(2, 1)
+        onward(1, 0, 3)
+        onward(0, 1, 3)
+        last(1, 0, 0)
+        last(0, 1, 0)
+        z_on(3, 0)
+        z_on(3, 1)
+        onward(1, 0, 1)
+        onward(0, 1, 1)
+
+    sent_if_stays = tuple(pending)
+    pending.clear()
 
     @pl.when(moved)
     def _():
-        send(gsend.at[0], ghome, s1.at[TRADE + 2], r1.at[TRADE + 2], twin).wait_recv()
+        trade.start()
+        begin(1, 1, 0, first=True)
+        begin(1, 0, 0)
+        begin(0, 0, 0, first=True)
+        begin(0, 1, 0)
+        onward(1, 1, 0, first=True)
+        begin(0, 1, 3)
+        begin(0, 1, 1)
+        onward(0, 0, 0, first=True)
+        begin(1, 0, 3)
+        begin(1, 0, 1)
+        landed(own.at[z, halves[1]], TRADE + 1)
+        z_begin(1)
+        onward(1, 0, 0)
+        onward(0, 1, 0)
+        last(0, 0, 0, first=True)
+        begin(1, 0, 2)
+        last(1, 1, 0, first=True)
+        begin(0, 1, 2)
+        landed(own.at[z, halves[0]], TRADE)
+        z_begin(0)
+        z_on(1, 1)
+        onward(1, 0, 3)
+        onward(0, 1, 3)
+        z_on(1, 0)
+        last(1, 0, 0)
+        last(0, 1, 0)
+        z_on(2, 1)
+        z_on(2, 0)
+        onward(1, 0, 1)
+        onward(0, 1, 1)
+        z_on(3, 1)
+        z_on(3, 0)
+
+    sent_if_moved = tuple(pending)
+    pending.clear()
+
+    @pl.when(moved)
+    def _():
+        trade.wait_recv()
 
     def g_send(t, value):
         gpart[t, z] = value.astype(jnp.bfloat16)
 
-        @pl.loop(1, NZ)
-        def _(i):
+        for i in (3, 5, 4, 2, 6, 1, 7):
             send(gpart.at[t, z], gpart.at[t, z], sg.at[t, i], rg.at[t, i], dev(z=(z + i) % NZ)).start()
 
     grown = ghome[...]
@@ -229,25 +278,21 @@
         return y ^ ((m // 8) * 2 + m % 2), x ^ ((m // 2) % 4)
 
     for t in range(ROUNDS):
-        py, px = partner(t)
-        stage[t] = oth[py, px]
-        move(stage.at[t], sib_stage.at[t], CORE + t, other_core)
-
-    def affinity(t, rows, item, part):
-        scores = lax.dot_general(rows, own[item], NT, preferred_element_type=jnp.float32)
-        columns = pl.ds(pl.multiple_of(item * n, n), n)
-        aff[t, part * n:(part + 1) * n, columns] = jnp.exp(scores * scale).astype(jnp.bfloat16)
+        m = masks[t]
+        for a in range(2):
+            cands[t][c, a] = oth[(yh ^ (m // 8)) * 2 + a, x ^ ((m // 2) % 4)]
+        send(cands[t].at[c], cands[t].at[c], s1.at[CORE + t], r1.at[CORE + t], other_core).start()
 
     def affinities(t):
+        landed(cands[t].at[1 - c], CORE + t)
+        holder = yl ^ (masks[t] % 2)
+
         @pl.loop(0, NZ)
         def _(item):
-            affinity(t, stage[t], item, 0)
-
-        landed(sib_stage.at[t], CORE + t)
-
-        @pl.loop(0, NZ)
-        def _(item):
-            affinity(t, sib_stage[t], item, 1)
+            columns = pl.ds(pl.multiple_of(item * n, n), n)
+            for a in range(2):
+                scores = lax.dot_general(cands[t][holder, a], own[item], NT, preferred_element_type=jnp.float32)
+                aff[t, a, :, columns] = jnp.exp(scores * scale).astype(jnp.bfloat16)
 
     z_last()
     affinities(0)
@@ -275,16 +320,16 @@
             send(ref, ref, sg.at[t, i], rg.at[t, i], other_core).wait_recv()
             unpack(t, item)
 
-        wsend[t] = jnp.dot(aff[t, n:, :], gfull[...], preferred_element_type=jnp.float32)
+        wsend[t] = jnp.dot(aff[t, 1 - c], gfull[...], preferred_element_type=jnp.float32)
         copy = send(wsend.at[t], wrecv.at[t], sw.at[t], rw.at[t], other_core)
         copy.start()
-        mine = jnp.dot(aff[t, :n, :], gfull[...], preferred_element_type=jnp.float32)
+        mine = jnp.dot(aff[t, c], gfull[...], preferred_element_type=jnp.float32)
         copy.wait_recv()
         product = mine + wrecv[t]
         return pack(product[:, :k] / product[:, k:k + 1]).astype(jnp.bfloat16)
 
     def x_send(ref, sems, t, base):
-        for i in range(1, NX):
+        for i in (2, 1, 3):
             send(ref, ref, sems[0].at[t, base + i], sems[1].at[t, base + i], dev(x=(x + i) % NX)).start()
 
     def x_wait(buf, sems, t, base):
@@ -293,7 +338,7 @@
             send(ref, ref, sems[0].at[t, base + i], sems[1].at[t, base + i], other_core).wait_recv()
 
     def y_send(ref, sems, t, base):
-        for i in range(1, NY):
+        for i in (2, 1, 3):
             send(ref, ref, sems[0].at[t, base + i], sems[1].at[t, base + i], dev(y=(y + i) % NY)).start()
 
     def y_wait(buf, sems, t, base):
@@ -399,8 +444,7 @@
 
     zs[z] = total(ys, NY)
 
-    @pl.loop(1, NZ)
-    def _(i):
+    for i in (3, 5, 4, 2, 6, 1, 7):
         send(zs.at[z], zs.at[z], sa.at[12 + i], ra.at[12 + i], dev(z=(z + i) % NZ)).start()
 
     @pl.loop(1, NZ)
@@ -424,22 +468,28 @@
         ref = ybufs[t].at[(twin_y + NY - i) % NY]
         send(ref, ref, sc.at[t, 4 + i], rc.at[t, 4 + i], other_core).wait_recv()
     m = masks[t]
-    grown_out[...] = gback[...] + ybufs[t][twin_y ^ ((m // 8) * 2 + m % 2)].astype(jnp.float32)
+    out[:half, :] = gback[...] + ybufs[t][twin_y ^ ((m // 8) * 2 + m % 2)].astype(jnp.float32)
 
     @pl.loop(1, nq)
     def _(i):
         ref = fin.at[(q + nq - i) % nq]
         send(ref, ref, sa.at[20 + i], ra.at[20 + i], other_core).wait_recv()
 
-    sums_out[...] = fin[...].reshape(sums_out.shape)
-
-    for copy in pending:
-        copy.wait_send()
+    out[half:, :] = fin[...].reshape(2 * k, 2 * k)
+
+    all_sent(pending)
+    for t in range(ROUNDS):
+        ref = cands[t].at[c]
+        send(ref, ref, s1.at[CORE + t], r1.at[CORE + t], other_core).wait_send()
+
+    @pl.when(stays)
+    def _():
+        all_sent(sent_if_stays)
 
     @pl.when(moved)
     def _():
-        for copy in trades:
-            copy.wait_send()
+        all_sent(sent_if_moved)
+        trade.wait_send()
         send(gsend.at[1], gback, s1.at[TRADE + 3], r1.at[TRADE + 3], twin).wait_send()
         home_copy(0).wait_send()
 
@@ -466,30 +516,49 @@
         send(wsend.at[row], wrecv.at[row], sw.at[row], rw.at[row], other_core).wait_send()
 
 
-def inverse_factor(gram):
-    k = gram.shape[0]
-    row = lax.broadcasted_iota(jnp.int32, (k, 2 * k), 0)
-    lane = lax.broadcasted_iota(jnp.int32, (k, 2 * k), 1)
-    rows = lax.broadcasted_iota(jnp.int32, (k, 1), 0)
-    work = jnp.concatenate([gram, jnp.where(lane == row, 1.0, 0.0)[:, :k]], axis=1)
-    for i in range(k - 1):
-        first = (i + 1) // 8 * 8
-        pivot = work[i:i + 1, :] * (1.0 / work[i:i + 1, i:i + 1])
-        rest = work[first:, :]
-        factor = jnp.where(rows[first:] > i, rest[:, i:i + 1], 0.0)
-        rest = rest - factor * pivot
-        work = rest if first == 0 else jnp.concatenate([work[:first], rest], axis=0)
-    diagonal = jnp.sum(jnp.where(lane == row, work, 0.0), axis=1, keepdims=True)
-    return work[:, k:] * (1.0 / jnp.sqrt(diagonal))
-
-
-def finish_kernel(total_rows, grown, sums, iterate_t, ritz):
+def inverse_factors(grams, outs):
+    k = grams[0].shape[0]
+    row = lax.broadcasted_iota(jnp.int32, (k, k), 0)
+    lane = lax.broadcasted_iota(jnp.int32, (k, k), 1)
+    identity = jnp.where(lane == row, 1.0, 0.0)
+    for gram, out in zip(grams, outs):
+        whole = jnp.concatenate([gram, identity], axis=1)
+        work = [whole[8 * g:8 * g + 8] for g in range(k // 8)]
+        for i in range(0, k, 4):
+            block = work[i // 8]
+            s = i % 8
+            rows = [block[s + p:s + p + 1, :] for p in range(4)]
+            u = {(p, j): block[s + p:s + p + 1, i + j:i + j + 1] for p in range(4) for j in range(p, 4)}
+            inv = []
+            for p in range(4):
+                inv.append(1.0 / u[p, p])
+                for j in range(p + 1, 4):
+                    factor = u[p, j] * inv[p]
+                    rows[j] = rows[j] - factor * rows[p]
+                    for l in range(j, 4):
+                        u[j, l] = u[j, l] - factor * u[p, l]
+            for p in range(4):
+                out[i + p:i + p + 1, :] = rows[p] * (1.0 / jnp.sqrt(u[p, p]))
+            solved = [None] * 4
+            for p in reversed(range(4)):
+                value = rows[p]
+                for j in range(p + 1, 4):
+                    value = value - u[p, j] * solved[j]
+                solved[p] = value * inv[p]
+            for g in range((i + 4) // 8, k // 8):
+                rest = work[g]
+                for j in range(4):
+                    rest = rest - work[g][:, i + j:i + j + 1] * solved[j]
+                work[g] = rest
+
+
+def finish_kernel(total_rows, both, iterate_t, ritz, work_a, work_b):
     k = ritz.shape[0]
-    half = grown.shape[0]
-    every = sums[...] * (1.0 / total_rows)
-    inv_before = inverse_factor(every[:k, :k])
-    inv_last = inverse_factor(every[k:, k:])
-    packed = grown[...]
+    half = both.shape[0] - 2 * k
+    every = both[half:, :] * (1.0 / total_rows)
+    inverse_factors([every[:k, :k], every[k:, k:]], [work_a, work_b])
+    inv_before, inv_last = work_a[:, k:], work_b[:, k:]
+    packed = both[:half, :]
     iterate_t[:, :half] = dot32(inv_last, packed[:, :k], NT)
     iterate_t[:, half:] = dot32(inv_last, packed[:, k:], NT)
     left = dot32(inv_before, every[:k, k:], (((1,), (0,)), ((), ())))
@@ -505,18 +574,19 @@
     vmem = pl.BlockSpec(memory_space=pltpu.VMEM)
     slab = (2 * k) // (2 * NX)
     dma = pltpu.SemaphoreType.DMA
-    grown, sums = pl.pallas_call(
+    both = pl.pallas_call(
         functools.partial(rounds_kernel, SHARPNESS / math.sqrt(feat)),
-        out_shape=(jax.ShapeDtypeStruct((half, 2 * k), f32), jax.ShapeDtypeStruct((2 * k, 2 * k), f32)),
-        in_specs=[pl.BlockSpec(memory_space=pltpu.SMEM), vmem, vmem],
-        out_specs=(vmem, vmem),
+        out_shape=jax.ShapeDtypeStruct((half + 2 * k, 2 * k), f32),
+        in_specs=[pl.BlockSpec(memory_space=pltpu.HBM)] * 3,
+        out_specs=vmem,
         scratch_shapes=[
+            pltpu.SMEM((ROUNDS,), jnp.int32),
             pltpu.VMEM((n, feat), bf),
+            pltpu.VMEM((k, n), f32),
             pltpu.VMEM((NY, NX, n, feat), bf),
             pltpu.VMEM((NZ, n, feat), bf),
-            pltpu.VMEM((ROUNDS, n, feat), bf),
-            pltpu.VMEM((ROUNDS, n, feat), bf),
-            pltpu.VMEM((ROUNDS, 2 * n, NZ * n), bf),
+            [pltpu.VMEM((2, 2, n, feat), bf)] * ROUNDS,
+            pltpu.VMEM((ROUNDS, 2, n, NZ * n), bf),
             pltpu.VMEM((ROUNDS, NZ, half, 2 * k), bf),
             pltpu.VMEM((NZ * n, 2 * k), bf),
             pltpu.VMEM((ROUNDS, n, 2 * k), f32),
@@ -534,6 +604,7 @@
             pltpu.VMEM((NZ, slab, 2 * k), f32),
             pltpu.VMEM((2 * NX, slab, 2 * k), f32),
             pltpu.VMEM((2 * NX, slab, 2 * k), f32),
+            dma((3,)),
             dma((61,)), dma((61,)),
             dma((ROUNDS, NZ)), dma((ROUNDS, NZ)),
             dma((ROUNDS + 1, 8)), dma((ROUNDS + 1, 8)),
@@ -541,17 +612,18 @@
             dma((28,)), dma((28,)),
         ],
         compiler_params=pltpu.CompilerParams(
-            collective_id=0, has_side_effects=True, vmem_limit_bytes=48 * 1024 * 1024
+            collective_id=0, has_side_effects=True, vmem_limit_bytes=60 * 1024 * 1024
         ),
         name="rounds",
     )(round_masks, shots, basis.T)
     iterate_t, ritz = pl.pallas_call(
         functools.partial(finish_kernel, float(nown * nrep * n)),
         out_shape=(jax.ShapeDtypeStruct((k, n), f32), jax.ShapeDtypeStruct((k, k), f32)),
-        in_specs=[vmem, vmem],
+        in_specs=[vmem],
         out_specs=(vmem, vmem),
+        scratch_shapes=[pltpu.VMEM((k, 2 * k), f32)] * 2,
         name="finish",
-    )(grown, sums)
+    )(both)
     return iterate_t.T, ritz
 
 

time: 135 us -> 131 us (0.970)
  local copies, waits for them, and re-layouts: 3.73 us -> 0 us
    unnamed x10 -> x0, local copies, waits for them, and re-layouts: 3.73 us -> none
    pallas_call x1, Pallas kernels: 123 us -> 121 us  [shards(): pl.pallas_call(functools.partial(rounds_kernel, SHARPNESS / math.sqrt(fea...]
where the time goes in v4:
time: 131 us
  Pallas kernels  130 us (99%)
    pallas_call x1, Pallas kernels, shards(): pl.pallas_call(functools.partial(rounds_kernel, SHARPNESS / math.sqrt(fea...  121 us
    pallas_call x1, Pallas kernels, shards(): pl.pallas_call(functools.partial(finish_kernel, float(nown * nrep * n)),...  8.96 us

profile of v4, /device:TPU:1, one launch (start us, length us, event | category | flops | bytes accessed | tf_op | source)
XLA Modules:
  0.0 130.8 jit_solution(6353434332675155339)
XLA Ops:
  0.6 121.2 %rounds.1.both = f32[256,128]{1,0:T(8,128)} custom-call(s32[3]{0:T(128)} %masks_hbm.1, bf16[256,768]{1,0:T(8,128)(2,1)} %shots_hbm.1, f32[64,256]{1,0:T(8,128)} %bitcast.2), custom_call_target="tpu_custom_call" | custom-call | tf_op jit(solution)/shard_map/rounds/pallas_call | solution.py:577
  121.8 9.0 %finish.1 = (f32[64,256]{1,0:T(8,128)}, f32[64,64]{1,0:T(8,128)}) custom-call(f32[256,128]{1,0:T(8,128)} %rounds.1.both), custom_call_target="tpu_custom_call" | custom-call | tf_op jit(solution)/shard_map/finish/pallas_call | solution.py:619

commit v5 on v4

--- a/solution.py
+++ b/solution.py
@@ -14,6 +14,35 @@
 NT = (((1,), (1,)), ((), ()))
 TN = (((0,), (0,)), ((), ()))
 NX, NY, NZ = 4, 4, 8
+
+ORDER_STAYS = (
+    ("G", 1, 0, 1), ("Y",), ("G", 1, 0, -1), ("F", 0, 0, 0, 1, 3), ("F", 0, 0, 0, 1, 1), ("F", 1, 1, 0, 1, 3),
+    ("F", 1, 1, 0, 1, 1), ("Z", 1, 0, 1), ("Z", 1, 0, -1), ("F", 0, 1, 0, 0, 3), ("F", 0, 1, 0, 0, 1),
+    ("F", 1, 0, 0, 0, 3), ("F", 1, 0, 0, 0, 1), ("Z", 1, 1, 1), ("Z", 1, 1, -1), ("G", 2, 0, 1), ("G", 2, 0, -1),
+    ("Z", 2, 0, 1), ("Z", 2, 0, -1), ("Q", 0, 0, 0, 1, 0), ("Q", 0, 0, 0, 1, 1), ("F", 0, 1, 3, 0, 3),
+    ("F", 0, 1, 3, 0, 1), ("Z", 2, 1, 1), ("Z", 2, 1, -1), ("G", 3, 0, 1), ("G", 3, 0, -1), ("F", 0, 1, 1, 0, 3),
+    ("F", 0, 1, 1, 0, 1), ("Q", 0, 1, 0, 0, 0), ("Q", 0, 1, 0, 0, 1), ("Z", 3, 0, 1), ("F", 1, 0, 3, 0, 3),
+    ("F", 1, 0, 3, 0, 1), ("Z", 3, 0, -1), ("F", 1, 0, 1, 0, 3), ("F", 1, 0, 1, 0, 1), ("Q", 1, 1, 0, 1, 0),
+    ("Q", 1, 1, 0, 1, 1), ("Z", 3, 1, 1), ("Q", 1, 0, 0, 0, 0), ("Q", 1, 0, 0, 0, 1), ("Z", 3, 1, -1), ("G", 4, 0, 1),
+    ("Q", 0, 1, 3, 0, 0), ("Q", 0, 1, 3, 0, 1), ("Q", 0, 1, 1, 0, 0), ("Q", 0, 1, 1, 0, 1), ("Q", 1, 0, 3, 0, 0),
+    ("Q", 1, 0, 3, 0, 1), ("Q", 1, 0, 1, 0, 0), ("Q", 1, 0, 1, 0, 1), ("Z", 4, 0, 1), ("F", 1, 0, 2, 0, 3),
+    ("F", 1, 0, 2, 0, 1), ("Z", 4, 1, -1), ("F", 0, 1, 2, 0, 3), ("F", 0, 1, 2, 0, 1), ("Q", 1, 0, 2, 0, 0),
+    ("Q", 1, 0, 2, 0, 1), ("Q", 0, 1, 2, 0, 0), ("Q", 0, 1, 2, 0, 1),
+)
+ORDER_MOVED = (
+    ("O", 1), ("T",), ("O", 0), ("F", 0, 0, 0, 1, 3), ("F", 0, 0, 0, 1, 1), ("F", 1, 1, 0, 1, 3),
+    ("F", 1, 1, 0, 1, 1), ("F", 0, 1, 0, 0, 3), ("F", 0, 1, 0, 0, 1), ("F", 1, 0, 0, 0, 3), ("F", 1, 0, 0, 0, 1),
+    ("Z", 1, 1, 1), ("Z", 1, 1, -1), ("F", 1, 0, 3, 0, 3), ("F", 1, 0, 3, 0, 1), ("G", 1, 0, 1), ("G", 1, 0, -1),
+    ("F", 1, 0, 1, 0, 3), ("F", 1, 0, 1, 0, 1), ("Q", 1, 1, 0, 1, 0), ("Q", 1, 1, 0, 1, 1), ("Z", 1, 0, 1),
+    ("Q", 1, 0, 0, 0, 0), ("Q", 1, 0, 0, 0, 1), ("Z", 1, 0, -1), ("Q", 0, 0, 0, 1, 0), ("Q", 0, 0, 0, 1, 1),
+    ("F", 0, 1, 3, 0, 3), ("F", 0, 1, 3, 0, 1), ("Z", 2, 1, 1), ("Z", 2, 1, -1), ("F", 0, 1, 1, 0, 3),
+    ("F", 0, 1, 1, 0, 1), ("Q", 0, 1, 0, 0, 0), ("Q", 0, 1, 0, 0, 1), ("G", 2, 0, 1), ("G", 2, 0, -1),
+    ("F", 1, 0, 2, 0, 3), ("F", 1, 0, 2, 0, 1), ("Z", 2, 0, -1), ("Z", 2, 0, 1), ("F", 0, 1, 2, 0, 3),
+    ("F", 0, 1, 2, 0, 1), ("Z", 3, 1, -1), ("Q", 0, 1, 3, 0, 0), ("Q", 0, 1, 3, 0, 1), ("Q", 0, 1, 1, 0, 0),
+    ("Q", 0, 1, 1, 0, 1), ("Z", 3, 1, 1), ("G", 3, 0, -1), ("G", 3, 0, 1), ("Q", 1, 0, 3, 0, 0), ("Q", 1, 0, 3, 0, 1),
+    ("Q", 1, 0, 1, 0, 0), ("Q", 1, 0, 1, 0, 1), ("Q", 0, 1, 2, 0, 0), ("Q", 0, 1, 2, 0, 1), ("Z", 3, 0, -1),
+    ("Z", 3, 0, 1), ("G", 4, 0, 1), ("Q", 1, 0, 2, 0, 0), ("Q", 1, 0, 2, 0, 1), ("Z", 4, 1, -1), ("Z", 4, 0, 1),
+)
 
 
 def dot32(a, b, dims):
@@ -138,17 +167,16 @@
         same(ref, number, step(axis, 1))
         same(ref, number + 1, step(axis, -1 % 4))
 
-    def onward(axis, h, j, first=False):
+    def on_full(axis, h, j, first, k):
         number = ring(axis, h, j, first)
-        landed(oth.at[(*at(axis, 3, j), halves[h])], number)
-        same(oth.at[(*at(axis, 3, j), quarters[h][0])], number + 2, step(axis, 1))
-        landed(oth.at[(*at(axis, 1, j), halves[h])], number + 1)
-        same(oth.at[(*at(axis, 1, j), quarters[h][1])], number + 3, step(axis, 3))
-
-    def last(axis, h, j, first=False):
-        number = ring(axis, h, j, first)
-        landed(oth.at[(*at(axis, 2, j), quarters[h][0])], number + 2)
-        landed(oth.at[(*at(axis, 2, j), quarters[h][1])], number + 3)
+        part = 0 if k == 3 else 1
+        landed(oth.at[(*at(axis, k, j), halves[h])], number + part)
+        same(oth.at[(*at(axis, k, j), quarters[h][part])], number + 2 + part, step(axis, 4 - k))
+        if first:
+            begin(1 - axis, h, k)
+
+    def on_quarter(axis, h, j, first, part):
+        landed(oth.at[(*at(axis, 2, j), quarters[h][part])], ring(axis, h, j, first) + 2 + part)
 
     up, down = dev(z=(z + 1) % NZ), dev(z=(z + NZ - 1) % NZ)
 
@@ -156,105 +184,81 @@
         same(own.at[z, halves[h]], UP + h, up)
         same(own.at[z, halves[h]], DN + h, down)
 
-    def z_on(s, h):
-        a, b = (z + NZ - s) % NZ, (z + s) % NZ
-        landed(own.at[a, halves[h]], UP + 2 * (s - 1) + h)
-        if s < 3 or h == 0:
-            same(own.at[a, halves[h]], UP + 2 * s + (h if s < 3 else 0), up)
-        landed(own.at[b, halves[h]], DN + 2 * (s - 1) + h)
-        if s < 3 or h == 1:
-            same(own.at[b, halves[h]], DN + 2 * s + (h if s < 3 else 0), down)
-
-    def z_last():
-        a = (z + 4) % NZ
-        landed(own.at[a, halves[0]], UP + 6)
-        landed(own.at[a, halves[1]], DN + 6)
+    def on_z(s, h, direction):
+        ref = own.at[(z + NZ - direction * s) % NZ, halves[h]]
+        base = UP if direction == 1 else DN
+        landed(ref, base + (2 * (s - 1) + h if s < 4 else 6))
+        if s < 3 or (s == 3 and (h == 0) == (direction == 1)):
+            same(ref, base + (2 * s + h if s < 3 else 6), up if direction == 1 else down)
+
+    def g_begin():
+        gpart[0, z] = ghome[...].astype(jnp.bfloat16)
+        for i, device in ((1, up), (7, down)):
+            send(gpart.at[0, z], gpart.at[0, z], sg.at[0, i], rg.at[0, i], device).start()
+
+    def on_g(s, direction):
+        ref = gpart.at[0, (z + NZ - direction * s) % NZ]
+        i = s if direction == 1 else NZ - s
+        send(ref, ref, sg.at[0, i], rg.at[0, i], other_core).wait_recv()
+        if s < 3 or (s == 3 and direction == 1):
+            send(ref, ref, sg.at[0, i + direction], rg.at[0, i + direction], up if direction == 1 else down).start()
 
     def hand_over(h):
         src = oth.at[yh * 2 + 1 - yl, x, halves[h]]
         move(src, own.at[z, halves[h]], TRADE + h, other_core)
 
+    def gather(order):
+        seen = set()
+        for kind, *args in order:
+            seen.add((kind, *args))
+            if kind == "F":
+                on_full(*args)
+                axis, h, j, first, k = args
+                if order is ORDER_STAYS and axis == 1 and j == 0 and ("F", axis, h, j, first, 4 - k) in seen:
+                    hand_over(h)
+            elif kind == "Q":
+                on_quarter(*args)
+                axis, h, j, first, part = args
+                if first and ("Q", axis, h, j, first, 1 - part) in seen:
+                    begin(1 - axis, h, 2)
+            elif kind == "Z":
+                on_z(*args)
+            elif kind == "G":
+                on_g(args[0], args[2])
+            elif kind == "O":
+                landed(own.at[z, halves[args[0]]], TRADE + args[0])
+                z_begin(args[0])
+            elif kind == "T":
+                trade.wait_recv()
+                g_begin()
+            else:
+                begin(1, 1, 0, first=True)
+                begin(1, 0, 0)
+
     @pl.when(stays)
     def _():
+        g_begin()
         z_begin(0)
         z_begin(1)
         begin(0, 0, 0, first=True)
-        begin(1, 1, 0, first=True)
         begin(0, 1, 0)
-        begin(1, 0, 0)
-        onward(1, 1, 0, first=True)
-        hand_over(1)
-        begin(0, 1, 3)
-        begin(0, 1, 1)
-        onward(0, 0, 0, first=True)
-        begin(1, 0, 3)
-        begin(1, 0, 1)
-        z_on(1, 0)
-        onward(1, 0, 0)
-        hand_over(0)
-        onward(0, 1, 0)
-        z_on(1, 1)
-        last(0, 0, 0, first=True)
-        begin(1, 0, 2)
-        last(1, 1, 0, first=True)
-        begin(0, 1, 2)
-        z_on(2, 0)
-        z_on(2, 1)
-        onward(1, 0, 3)
-        onward(0, 1, 3)
-        last(1, 0, 0)
-        last(0, 1, 0)
-        z_on(3, 0)
-        z_on(3, 1)
-        onward(1, 0, 1)
-        onward(0, 1, 1)
+        gather(ORDER_STAYS)
 
     sent_if_stays = tuple(pending)
     pending.clear()
 
     @pl.when(moved)
     def _():
-        trade.start()
         begin(1, 1, 0, first=True)
         begin(1, 0, 0)
+        trade.start()
         begin(0, 0, 0, first=True)
         begin(0, 1, 0)
-        onward(1, 1, 0, first=True)
-        begin(0, 1, 3)
-        begin(0, 1, 1)
-        onward(0, 0, 0, first=True)
-        begin(1, 0, 3)
-        begin(1, 0, 1)
-        landed(own.at[z, halves[1]], TRADE + 1)
-        z_begin(1)
-        onward(1, 0, 0)
-        onward(0, 1, 0)
-        last(0, 0, 0, first=True)
-        begin(1, 0, 2)
-        last(1, 1, 0, first=True)
-        begin(0, 1, 2)
-        landed(own.at[z, halves[0]], TRADE)
-        z_begin(0)
-        z_on(1, 1)
-        onward(1, 0, 3)
-        onward(0, 1, 3)
-        z_on(1, 0)
-        last(1, 0, 0)
-        last(0, 1, 0)
-        z_on(2, 1)
-        z_on(2, 0)
-        onward(1, 0, 1)
-        onward(0, 1, 1)
-        z_on(3, 1)
-        z_on(3, 0)
+        gather(ORDER_MOVED)
 
     sent_if_moved = tuple(pending)
     pending.clear()
 
-    @pl.when(moved)
-    def _():
-        trade.wait_recv()
-
     def g_send(t, value):
         gpart[t, z] = value.astype(jnp.bfloat16)
 
@@ -262,16 +266,6 @@
             send(gpart.at[t, z], gpart.at[t, z], sg.at[t, i], rg.at[t, i], dev(z=(z + i) % NZ)).start()
 
     grown = ghome[...]
-    g_send(0, grown)
-
-    onward(1, 0, 2)
-    onward(0, 1, 2)
-    last(1, 0, 3)
-    last(0, 1, 3)
-    last(1, 0, 1)
-    last(0, 1, 1)
-    last(1, 0, 2)
-    last(0, 1, 2)
 
     def partner(t):
         m = masks[t]
@@ -294,7 +288,6 @@
                 scores = lax.dot_general(cands[t][holder, a], own[item], NT, preferred_element_type=jnp.float32)
                 aff[t, a, :, columns] = jnp.exp(scores * scale).astype(jnp.bfloat16)
 
-    z_last()
     affinities(0)
 
     lane = lax.broadcasted_iota(jnp.int32, (half, 2 * k), 1)
@@ -316,8 +309,9 @@
         def _(j):
             i = near(j)
             item = (z + NZ - i) % NZ
-            ref = gpart.at[t, item]
-            send(ref, ref, sg.at[t, i], rg.at[t, i], other_core).wait_recv()
+            if t > 0:
+                ref = gpart.at[t, item]
+                send(ref, ref, sg.at[t, i], rg.at[t, i], other_core).wait_recv()
             unpack(t, item)
 
         wsend[t] = jnp.dot(aff[t, 1 - c], gfull[...], preferred_element_type=jnp.float32)
@@ -516,48 +510,36 @@
         send(wsend.at[row], wrecv.at[row], sw.at[row], rw.at[row], other_core).wait_send()
 
 
-def inverse_factors(grams, outs):
+def inverse_factors(grams):
     k = grams[0].shape[0]
-    row = lax.broadcasted_iota(jnp.int32, (k, k), 0)
-    lane = lax.broadcasted_iota(jnp.int32, (k, k), 1)
-    identity = jnp.where(lane == row, 1.0, 0.0)
-    for gram, out in zip(grams, outs):
-        whole = jnp.concatenate([gram, identity], axis=1)
-        work = [whole[8 * g:8 * g + 8] for g in range(k // 8)]
-        for i in range(0, k, 4):
-            block = work[i // 8]
-            s = i % 8
-            rows = [block[s + p:s + p + 1, :] for p in range(4)]
-            u = {(p, j): block[s + p:s + p + 1, i + j:i + j + 1] for p in range(4) for j in range(p, 4)}
-            inv = []
-            for p in range(4):
-                inv.append(1.0 / u[p, p])
-                for j in range(p + 1, 4):
-                    factor = u[p, j] * inv[p]
-                    rows[j] = rows[j] - factor * rows[p]
-                    for l in range(j, 4):
-                        u[j, l] = u[j, l] - factor * u[p, l]
-            for p in range(4):
-                out[i + p:i + p + 1, :] = rows[p] * (1.0 / jnp.sqrt(u[p, p]))
-            solved = [None] * 4
-            for p in reversed(range(4)):
-                value = rows[p]
-                for j in range(p + 1, 4):
-                    value = value - u[p, j] * solved[j]
-                solved[p] = value * inv[p]
-            for g in range((i + 4) // 8, k // 8):
-                rest = work[g]
-                for j in range(4):
-                    rest = rest - work[g][:, i + j:i + j + 1] * solved[j]
-                work[g] = rest
-
-
-def finish_kernel(total_rows, both, iterate_t, ritz, work_a, work_b):
+    row = lax.broadcasted_iota(jnp.int32, (k, 2 * k), 0)
+    lane = lax.broadcasted_iota(jnp.int32, (k, 2 * k), 1)
+    identity = jnp.where(lane == row, 1.0, 0.0)[:, :k]
+    works = [jnp.concatenate([gram, identity], axis=1) for gram in grams]
+    works = [[work[8 * g:8 * g + 8] for g in range(k // 8)] for work in works]
+    below = lax.broadcasted_iota(jnp.int32, (8, 1), 0)
+    for i in range(k - 1):
+        own, s = i // 8, i % 8
+        for work in works:
+            pivot = work[own][s:s + 1, :] * (1.0 / work[own][s:s + 1, i:i + 1])
+            for g in range(own, k // 8):
+                factor = work[g][:, i:i + 1]
+                if g == own:
+                    factor = jnp.where(below > s, factor, 0.0)
+                work[g] = work[g] - factor * pivot
+    results = []
+    for work in works:
+        whole = jnp.concatenate(work, axis=0)
+        diagonal = jnp.sum(jnp.where(lane == row, whole, 0.0), axis=1, keepdims=True)
+        results.append(whole[:, k:] * (1.0 / jnp.sqrt(diagonal)))
+    return results
+
+
+def finish_kernel(total_rows, both, iterate_t, ritz):
     k = ritz.shape[0]
     half = both.shape[0] - 2 * k
     every = both[half:, :] * (1.0 / total_rows)
-    inverse_factors([every[:k, :k], every[k:, k:]], [work_a, work_b])
-    inv_before, inv_last = work_a[:, k:], work_b[:, k:]
+    inv_before, inv_last = inverse_factors([every[:k, :k], every[k:, k:]])
     packed = both[:half, :]
     iterate_t[:, :half] = dot32(inv_last, packed[:, :k], NT)
     iterate_t[:, half:] = dot32(inv_last, packed[:, k:], NT)
@@ -621,7 +603,6 @@
         out_shape=(jax.ShapeDtypeStruct((k, n), f32), jax.ShapeDtypeStruct((k, k), f32)),
         in_specs=[vmem],
         out_specs=(vmem, vmem),
-        scratch_shapes=[pltpu.VMEM((k, 2 * k), f32)] * 2,
         name="finish",
     )(both)
     return iterate_t.T, ritz

time: 131 us -> 122 us (0.931)
  Pallas kernels: 130 us -> 122 us
    pallas_call x1, Pallas kernels: 121 us -> 114 us  [shards(): pl.pallas_call(functools.partial(rounds_kernel, SHARPNESS / math.sqrt(fea...]
where the time goes in v5:
time: 122 us
  Pallas kernels  122 us (100%)
    pallas_call x1, Pallas kernels, shards(): pl.pallas_call(functools.partial(rounds_kernel, SHARPNESS / math.sqrt(fea...  114 us
    pallas_call x1, Pallas kernels, shards(): pl.pallas_call(functools.partial(finish_kernel, float(nown * nrep * n)),...  7.77 us

profile of v5, /device:TPU:1, one launch (start us, length us, event | category | flops | bytes accessed | tf_op | source)
XLA Modules:
  0.0 122.3 jit_solution(4353867052500762825)
XLA Ops:
  0.6 113.9 %rounds.1.both = f32[256,128]{1,0:T(8,128)} custom-call(s32[3]{0:T(128)} %masks_hbm.1, bf16[256,768]{1,0:T(8,128)(2,1)} %shots_hbm.1, f32[64,256]{1,0:T(8,128)} %bitcast.2), custom_call_target="tpu_custom_call" | custom-call | tf_op jit(solution)/shard_map/rounds/pallas_call | solution.py:559
  114.5 7.8 %finish.1 = (f32[64,256]{1,0:T(8,128)}, f32[64,64]{1,0:T(8,128)}) custom-call(f32[256,128]{1,0:T(8,128)} %rounds.1.both), custom_call_target="tpu_custom_call" | custom-call | tf_op jit(solution)/shard_map/finish/pallas_call | solution.py:601

commit v6 on v5

--- a/solution.py
+++ b/solution.py
@@ -16,32 +16,49 @@
 NX, NY, NZ = 4, 4, 8
 
 ORDER_STAYS = (
-    ("G", 1, 0, 1), ("Y",), ("G", 1, 0, -1), ("F", 0, 0, 0, 1, 3), ("F", 0, 0, 0, 1, 1), ("F", 1, 1, 0, 1, 3),
-    ("F", 1, 1, 0, 1, 1), ("Z", 1, 0, 1), ("Z", 1, 0, -1), ("F", 0, 1, 0, 0, 3), ("F", 0, 1, 0, 0, 1),
-    ("F", 1, 0, 0, 0, 3), ("F", 1, 0, 0, 0, 1), ("Z", 1, 1, 1), ("Z", 1, 1, -1), ("G", 2, 0, 1), ("G", 2, 0, -1),
-    ("Z", 2, 0, 1), ("Z", 2, 0, -1), ("Q", 0, 0, 0, 1, 0), ("Q", 0, 0, 0, 1, 1), ("F", 0, 1, 3, 0, 3),
-    ("F", 0, 1, 3, 0, 1), ("Z", 2, 1, 1), ("Z", 2, 1, -1), ("G", 3, 0, 1), ("G", 3, 0, -1), ("F", 0, 1, 1, 0, 3),
-    ("F", 0, 1, 1, 0, 1), ("Q", 0, 1, 0, 0, 0), ("Q", 0, 1, 0, 0, 1), ("Z", 3, 0, 1), ("F", 1, 0, 3, 0, 3),
-    ("F", 1, 0, 3, 0, 1), ("Z", 3, 0, -1), ("F", 1, 0, 1, 0, 3), ("F", 1, 0, 1, 0, 1), ("Q", 1, 1, 0, 1, 0),
-    ("Q", 1, 1, 0, 1, 1), ("Z", 3, 1, 1), ("Q", 1, 0, 0, 0, 0), ("Q", 1, 0, 0, 0, 1), ("Z", 3, 1, -1), ("G", 4, 0, 1),
-    ("Q", 0, 1, 3, 0, 0), ("Q", 0, 1, 3, 0, 1), ("Q", 0, 1, 1, 0, 0), ("Q", 0, 1, 1, 0, 1), ("Q", 1, 0, 3, 0, 0),
-    ("Q", 1, 0, 3, 0, 1), ("Q", 1, 0, 1, 0, 0), ("Q", 1, 0, 1, 0, 1), ("Z", 4, 0, 1), ("F", 1, 0, 2, 0, 3),
-    ("F", 1, 0, 2, 0, 1), ("Z", 4, 1, -1), ("F", 0, 1, 2, 0, 3), ("F", 0, 1, 2, 0, 1), ("Q", 1, 0, 2, 0, 0),
-    ("Q", 1, 0, 2, 0, 1), ("Q", 0, 1, 2, 0, 0), ("Q", 0, 1, 2, 0, 1),
+    (
+        ("G", 1, 1), ("G", 1, -1), ("F", 1, 1), ("Z", 1, 0, 1), ("Z", 1, 0, -1), ("Z", 1, 1, 1), ("Z", 1, 1, -1),
+        ("G", 2, 1), ("G", 2, -1), ("Q", 1, 1), ("F", 0, 3), ("F", 0, 1), ("F", 1, 3), ("Q", 1, 0), ("Z", 2, 0, 1),
+        ("Z", 2, 0, -1), ("Q", 0, 0), ("Q", 0, 1), ("Z", 2, 1, 1), ("Z", 2, 1, -1), ("G", 3, 1), ("G", 3, -1),
+        ("Z", 3, 0, 1), ("Z", 3, 0, -1), ("F", 5, 3), ("F", 5, 1), ("F", 2, 3), ("F", 2, 1), ("Z", 3, 1, 1),
+        ("Z", 3, 1, -1), ("G", 4, 1), ("Q", 5, 0), ("Q", 5, 1), ("Z", 4, 0, 1), ("Q", 2, 0), ("Q", 2, 1), ("F", 6, 3),
+        ("F", 6, 1), ("Z", 4, 1, -1), ("X", 0),
+    ),
+    (
+        ("Q", 6, 0), ("Q", 6, 1), ("F", 3, 3), ("F", 3, 1), ("F", 7, 3), ("F", 7, 1), ("Q", 3, 0), ("Q", 3, 1),
+    ),
+    (
+        ("Q", 7, 0), ("X", 1),
+    ),
+    (
+        ("Q", 7, 1), ("F", 4, 3), ("F", 4, 1), ("Q", 4, 0), ("Q", 4, 1),
+    ),
+    (
+        ("X", 2),
+    ),
 )
 ORDER_MOVED = (
-    ("O", 1), ("T",), ("O", 0), ("F", 0, 0, 0, 1, 3), ("F", 0, 0, 0, 1, 1), ("F", 1, 1, 0, 1, 3),
-    ("F", 1, 1, 0, 1, 1), ("F", 0, 1, 0, 0, 3), ("F", 0, 1, 0, 0, 1), ("F", 1, 0, 0, 0, 3), ("F", 1, 0, 0, 0, 1),
-    ("Z", 1, 1, 1), ("Z", 1, 1, -1), ("F", 1, 0, 3, 0, 3), ("F", 1, 0, 3, 0, 1), ("G", 1, 0, 1), ("G", 1, 0, -1),
-    ("F", 1, 0, 1, 0, 3), ("F", 1, 0, 1, 0, 1), ("Q", 1, 1, 0, 1, 0), ("Q", 1, 1, 0, 1, 1), ("Z", 1, 0, 1),
-    ("Q", 1, 0, 0, 0, 0), ("Q", 1, 0, 0, 0, 1), ("Z", 1, 0, -1), ("Q", 0, 0, 0, 1, 0), ("Q", 0, 0, 0, 1, 1),
-    ("F", 0, 1, 3, 0, 3), ("F", 0, 1, 3, 0, 1), ("Z", 2, 1, 1), ("Z", 2, 1, -1), ("F", 0, 1, 1, 0, 3),
-    ("F", 0, 1, 1, 0, 1), ("Q", 0, 1, 0, 0, 0), ("Q", 0, 1, 0, 0, 1), ("G", 2, 0, 1), ("G", 2, 0, -1),
-    ("F", 1, 0, 2, 0, 3), ("F", 1, 0, 2, 0, 1), ("Z", 2, 0, -1), ("Z", 2, 0, 1), ("F", 0, 1, 2, 0, 3),
-    ("F", 0, 1, 2, 0, 1), ("Z", 3, 1, -1), ("Q", 0, 1, 3, 0, 0), ("Q", 0, 1, 3, 0, 1), ("Q", 0, 1, 1, 0, 0),
-    ("Q", 0, 1, 1, 0, 1), ("Z", 3, 1, 1), ("G", 3, 0, -1), ("G", 3, 0, 1), ("Q", 1, 0, 3, 0, 0), ("Q", 1, 0, 3, 0, 1),
-    ("Q", 1, 0, 1, 0, 0), ("Q", 1, 0, 1, 0, 1), ("Q", 0, 1, 2, 0, 0), ("Q", 0, 1, 2, 0, 1), ("Z", 3, 0, -1),
-    ("Z", 3, 0, 1), ("G", 4, 0, 1), ("Q", 1, 0, 2, 0, 0), ("Q", 1, 0, 2, 0, 1), ("Z", 4, 1, -1), ("Z", 4, 0, 1),
+    (
+        ("T",), ("F", 1, 1), ("F", 1, 3), ("O", 0), ("G", 1, 1), ("G", 1, -1), ("Q", 1, 1), ("O", 1), ("F", 0, 3),
+        ("F", 0, 1), ("Q", 1, 0), ("Z", 1, 0, 1), ("Z", 1, 0, -1), ("G", 2, 1), ("G", 2, -1), ("Q", 0, 0),
+        ("Q", 0, 1), ("Z", 1, 1, 1), ("Z", 1, 1, -1), ("F", 5, 3), ("F", 5, 1), ("Z", 2, 0, 1), ("Z", 2, 0, -1),
+        ("G", 3, 1), ("G", 3, -1), ("F", 2, 3), ("F", 2, 1), ("Z", 2, 1, -1), ("Q", 5, 0), ("Q", 5, 1),
+        ("Z", 2, 1, 1), ("Z", 3, 0, -1), ("Q", 2, 0), ("Q", 2, 1), ("Z", 3, 0, 1), ("F", 6, 3), ("F", 6, 1),
+        ("G", 4, 1), ("Z", 3, 1, -1), ("X", 0), ("Z", 3, 1, 1), ("Z", 4, 0, 1), ("Q", 6, 0), ("Q", 6, 1), ("F", 3, 3),
+        ("F", 3, 1), ("Z", 4, 1, -1),
+    ),
+    (
+        ("F", 7, 3), ("F", 7, 1), ("Q", 3, 0), ("Q", 3, 1),
+    ),
+    (
+        ("Q", 7, 0), ("Q", 7, 1), ("X", 1),
+    ),
+    (
+        ("F", 4, 3), ("F", 4, 1), ("Q", 4, 0), ("Q", 4, 1),
+    ),
+    (
+        ("X", 2),
+    ),
 )
 
 
@@ -56,12 +73,13 @@
 
 def rounds_kernel(
     scale, masks_hbm, shots_hbm, basis_hbm, out,
-    masks, shots, basis_t, oth, own, cands, aff, gpart, gfull, wsend, wrecv, xbufs, ybufs, homeward, ghome, gsend, gback, gx, gy,
+    masks, shots, basis_t, unit, rowbuf, colbuf, sel0, sel1, own, cands, aff, gpart, gfull, wsend, wrecv, xbufs, ybufs, homeward, ghome, gsend, gback, gx, gy,
     rs, ys, zs, fin, prod,
     s_in, s1, r1, sg, rg, sc, rc, sw, rw, sa, ra,
 ):
     n, feat = shots.shape
-    half, quarter = n // 2, n // 4
+    half, n0 = n // 2, rowbuf.shape[1]
+    n1 = n - n0
     k = basis_t.shape[0]
     o, r = lax.axis_index("owner"), lax.axis_index("rep")
     c, x, yh = o % 2, (o // 2) % NX, o // (2 * NX)
@@ -92,15 +110,14 @@
     def hello(device):
         pl.semaphore_signal(bar, inc=1, device_id=device, device_id_type=MESH)
 
-    @pl.loop(1, NZ)
-    def _(i):
-        hello(dev(z=(z + i) % NZ))
-
-    @pl.loop(1, NX)
-    def _(i):
-        for core in range(2):
-            hello(dev(x=(x + i) % NX, c=core))
-            hello(dev(y=(y + i) % NY, c=core))
+    neighbours = [dev(x=(x + i) % NX) for i in (1, 3)] + [dev(y=(y + i) % NY) for i in (1, 3)]
+    neighbours += [dev(z=(z + i) % NZ) for i in (1, 7)]
+    for neighbour in neighbours:
+        hello(neighbour)
+
+    @pl.when(moved)
+    def _():
+        hello(twin)
 
     hello(other_core)
 
@@ -108,19 +125,22 @@
         copy.wait()
     values = shots[...].astype(jnp.float32)
     inv = lax.rsqrt(jnp.mean(values * values, axis=-1, keepdims=True) + 1e-06)
-    oth[y, x] = (values * inv).astype(jnp.bfloat16)
+    units = (values * inv).astype(jnp.bfloat16)
+    rowbuf[x] = units[:n0]
+    colbuf[y] = units[n0:]
     g0 = pack(basis_t[...].T)
 
     @pl.when(stays)
     def _():
-        own[z] = oth[y, x]
+        own[z] = units
         ghome[...] = g0
 
     @pl.when(moved)
     def _():
+        unit[...] = units
         gsend[0] = g0
 
-    pl.semaphore_wait(bar, (NZ - 1) + 2 * (NX - 1) + 2 * (NY - 1) + 1)
+    pl.semaphore_wait(bar, len(neighbours) + 1 + (c + yl) % 2)
 
     def send(src, dst, ssem, rsem, device):
         return pltpu.make_async_remote_copy(
@@ -131,12 +151,12 @@
 
     def all_sent(numbers):
         for number, rows in numbers:
-            ref = oth.at[0, 0, pl.ds(0, rows)]
+            ref = own.at[0, pl.ds(0, rows)]
             send(ref, ref, s1.at[number], r1.at[number], other_core).wait_send()
 
     def move(src, dst, number, device):
         send(src, dst, s1.at[number], r1.at[number], device).start()
-        pending.append((number, src.shape[0]))
+        pending.append((number, math.prod(src.shape[:-1])))
 
     def same(ref, number, device):
         move(ref, ref, number, device)
@@ -145,38 +165,49 @@
         send(ref, ref, s1.at[number], r1.at[number], other_core).wait_recv()
 
     halves = (pl.ds(0, half), pl.ds(half, half))
-    quarters = tuple((pl.ds(i * half, quarter), pl.ds(i * half + quarter, quarter)) for i in range(2))
-
-    RING, UP, DN, CORE, TRADE = 0, 40, 47, 54, 57
+    RING, UP, DN, CORE, TRADE = 0, 32, 39, 46, 52
 
     trade = send(gsend.at[0], ghome, s1.at[TRADE + 2], r1.at[TRADE + 2], twin)
 
-    def step(axis, i):
-        return dev(x=(x + i) % NX) if axis == 0 else dev(y=(y + i) % NY)
-
-    def at(axis, i, j):
-        dx, dy = (i, j) if axis == 0 else (j, i)
-        return (y + dy) % NY, (x + dx) % NX
-
-    def ring(axis, h, j, first):
-        return RING + 4 * ((5 * h) + (0 if first else 1 + j % 4))
-
-    def begin(axis, h, j, first=False):
-        number = ring(axis, h, j, first)
-        ref = oth.at[(*at(axis, 0, j), halves[h])]
-        same(ref, number, step(axis, 1))
-        same(ref, number + 1, step(axis, -1 % 4))
-
-    def on_full(axis, h, j, first, k):
-        number = ring(axis, h, j, first)
+    def leg(number, i):
+        if number == 0:
+            return rowbuf.at[(x + i) % NX]
+        if number == 1:
+            return colbuf.at[(y + i) % NY]
+        if number < 5:
+            return sel0[number - 2].at[(y + i) % NY]
+        return sel1[number - 5].at[(x + i) % NX]
+
+    def part_of(number, i, part):
+        ref = leg(number, i)
+        if number >= 5:
+            return ref.at[part]
+        size = ref.shape[0] // 2
+        return ref.at[pl.ds(part * size, size)]
+
+    def step(number, i):
+        return dev(x=(x + i) % NX) if number in (0, 5, 6, 7) else dev(y=(y + i) % NY)
+
+    def begin(number):
+        same(leg(number, 0), RING + 4 * number, step(number, 1))
+        same(leg(number, 0), RING + 4 * number + 1, step(number, 3))
+
+    def on_full(number, k):
         part = 0 if k == 3 else 1
-        landed(oth.at[(*at(axis, k, j), halves[h])], number + part)
-        same(oth.at[(*at(axis, k, j), quarters[h][part])], number + 2 + part, step(axis, 4 - k))
-        if first:
-            begin(1 - axis, h, k)
-
-    def on_quarter(axis, h, j, first, part):
-        landed(oth.at[(*at(axis, 2, j), quarters[h][part])], ring(axis, h, j, first) + 2 + part)
+        landed(leg(number, k), RING + 4 * number + part)
+        same(part_of(number, k, part), RING + 4 * number + 2 + part, step(number, 4 - k))
+
+    def on_half(number, part):
+        landed(part_of(number, 2, part), RING + 4 * number + 2 + part)
+
+    def pick():
+        for t in range(ROUNDS):
+            m = masks[t]
+            sel0[t][y] = rowbuf[x ^ ((m // 2) % 4)]
+            for a in range(2):
+                sel1[t][x, a] = colbuf[(yh ^ (m // 8)) * 2 + a]
+        begin(2)
+        begin(5)
 
     up, down = dev(z=(z + 1) % NZ), dev(z=(z + NZ - 1) % NZ)
 
@@ -203,28 +234,53 @@
         if s < 3 or (s == 3 and direction == 1):
             send(ref, ref, sg.at[0, i + direction], rg.at[0, i + direction], up if direction == 1 else down).start()
 
-    def hand_over(h):
-        src = oth.at[yh * 2 + 1 - yl, x, halves[h]]
-        move(src, own.at[z, halves[h]], TRADE + h, other_core)
-
-    def gather(order):
-        seen = set()
-        for kind, *args in order:
-            seen.add((kind, *args))
+    def choose(t):
+        m = masks[t]
+        for a in range(2):
+            cands[t][c, a, :n0] = sel0[t][(yh ^ (m // 8)) * 2 + a]
+            cands[t][c, a, n0:] = sel1[t][x ^ ((m // 2) % 4), a]
+            number = CORE + 2 * t + a
+            same(cands[t].at[c, a], number, other_core)
+
+    def near(j):
+        return (NZ + (1 - 2 * ((j + 1) % 2)) * ((j + 1) // 2)) % NZ
+
+    def affinities(t, lo=0, hi=NZ):
+        holder = yl ^ (masks[t] % 2)
+
+        @pl.loop(lo, hi)
+        def _(j):
+            item = (z + near(j)) % NZ
+            columns = pl.ds(pl.multiple_of(item * n, n), n)
+            for a in range(2):
+                scores = lax.dot_general(cands[t][holder, a], own[item], NT, preferred_element_type=jnp.float32)
+                aff[t, a, :, columns] = jnp.exp(scores * scale).astype(jnp.bfloat16)
+
+    def gather(order, seen, stays_here):
+        def whole(number):
+            return all(e in seen for e in (("F", number, 1), ("F", number, 3), ("Q", number, 0), ("Q", number, 1)))
+
+        def z_here(s):
+            if s == 0:
+                return stays_here or (("O", 0) in seen and ("O", 1) in seen)
+            if s == 4:
+                return ("Z", 4, 0, 1) in seen and ("Z", 4, 1, -1) in seen
+            return all(("Z", s, h, d) in seen for h in (0, 1) for d in (1, -1))
+
+        for event in order:
+            kind, *args = event
+            seen.add(event)
             if kind == "F":
                 on_full(*args)
-                axis, h, j, first, k = args
-                if order is ORDER_STAYS and axis == 1 and j == 0 and ("F", axis, h, j, first, 4 - k) in seen:
-                    hand_over(h)
+                number, k = args
+                if number in (2, 3, 5, 6) and ("F", number, 4 - k) in seen:
+                    begin(number + 1)
             elif kind == "Q":
-                on_quarter(*args)
-                axis, h, j, first, part = args
-                if first and ("Q", axis, h, j, first, 1 - part) in seen:
-                    begin(1 - axis, h, 2)
+                on_half(*args)
             elif kind == "Z":
                 on_z(*args)
             elif kind == "G":
-                on_g(args[0], args[2])
+                on_g(*args)
             elif kind == "O":
                 landed(own.at[z, halves[args[0]]], TRADE + args[0])
                 z_begin(args[0])
@@ -232,32 +288,64 @@
                 trade.wait_recv()
                 g_begin()
             else:
-                begin(1, 1, 0, first=True)
-                begin(1, 0, 0)
+                for a in range(2):
+                    landed(cands[args[0]].at[1 - c, a], CORE + 2 * args[0] + a)
+            if kind in "FQ":
+                if "picked" not in seen and whole(0) and whole(1):
+                    seen.add("picked")
+                    pick()
+                for t in range(ROUNDS):
+                    if ("chosen", t) not in seen and whole(2 + t) and whole(5 + t):
+                        seen.add(("chosen", t))
+                        choose(t)
+            have = sum(("items", j) in seen for j in range(NZ))
+            ready = have
+            while ("X", 0) in seen and ready < NZ and z_here((ready + 1) // 2):
+                seen.add(("items", ready))
+                ready += 1
+            if ready > have:
+                affinities(0, have, ready)
+
+    seen_stays, seen_moved = set(), set()
 
     @pl.when(stays)
     def _():
         g_begin()
         z_begin(0)
         z_begin(1)
-        begin(0, 0, 0, first=True)
-        begin(0, 1, 0)
-        gather(ORDER_STAYS)
-
-    sent_if_stays = tuple(pending)
+        begin(0)
+        begin(1)
+        gather(ORDER_STAYS[0], seen_stays, True)
+
+    sent_if_stays = list(pending)
     pending.clear()
 
     @pl.when(moved)
     def _():
-        begin(1, 1, 0, first=True)
-        begin(1, 0, 0)
         trade.start()
-        begin(0, 0, 0, first=True)
-        begin(0, 1, 0)
-        gather(ORDER_MOVED)
-
-    sent_if_moved = tuple(pending)
+        for h in range(2):
+            move(unit.at[halves[h]], own.at[z, halves[h]], TRADE + h, twin)
+        begin(0)
+        begin(1)
+        gather(ORDER_MOVED[0], seen_moved, False)
+
+    sent_if_moved = list(pending)
     pending.clear()
+
+    def gather_rest(stage):
+        @pl.when(stays)
+        def _():
+            gather(ORDER_STAYS[stage], seen_stays, True)
+
+        sent_if_stays.extend(pending)
+        pending.clear()
+
+        @pl.when(moved)
+        def _():
+            gather(ORDER_MOVED[stage], seen_moved, False)
+
+        sent_if_moved.extend(pending)
+        pending.clear()
 
     def g_send(t, value):
         gpart[t, z] = value.astype(jnp.bfloat16)
@@ -270,25 +358,6 @@
     def partner(t):
         m = masks[t]
         return y ^ ((m // 8) * 2 + m % 2), x ^ ((m // 2) % 4)
-
-    for t in range(ROUNDS):
-        m = masks[t]
-        for a in range(2):
-            cands[t][c, a] = oth[(yh ^ (m // 8)) * 2 + a, x ^ ((m // 2) % 4)]
-        send(cands[t].at[c], cands[t].at[c], s1.at[CORE + t], r1.at[CORE + t], other_core).start()
-
-    def affinities(t):
-        landed(cands[t].at[1 - c], CORE + t)
-        holder = yl ^ (masks[t] % 2)
-
-        @pl.loop(0, NZ)
-        def _(item):
-            columns = pl.ds(pl.multiple_of(item * n, n), n)
-            for a in range(2):
-                scores = lax.dot_general(cands[t][holder, a], own[item], NT, preferred_element_type=jnp.float32)
-                aff[t, a, :, columns] = jnp.exp(scores * scale).astype(jnp.bfloat16)
-
-    affinities(0)
 
     lane = lax.broadcasted_iota(jnp.int32, (half, 2 * k), 1)
     tail = jnp.where(lane == k, 1.0, 0.0)
@@ -298,9 +367,6 @@
         start = pl.multiple_of(item * n, n)
         gfull[pl.ds(start, half), :] = jnp.where(lane < k, p, tail).astype(jnp.bfloat16)
         gfull[pl.ds(start + half, half), :] = jnp.where(lane < k, pltpu.roll(p, k, 1), tail).astype(jnp.bfloat16)
-
-    def near(j):
-        return (NZ + (1 - 2 * ((j + 1) % 2)) * ((j + 1) // 2)) % NZ
 
     def carried(t):
         unpack(t, z)
@@ -344,16 +410,21 @@
     for t in range(ROUNDS - 1):
         if t > 0:
             g_send(t, grown)
+            gather_rest(3)
         py, px = partner(t)
         xbufs[t][x] = carried(t)
         x_send(xbufs[t].at[x], csem, t, 0)
         if t == 0:
-            affinities(1)
+            gather_rest(1)
+        else:
+            gather_rest(4)
+            affinities(2)
         x_wait(xbufs[t], csem, t, 0)
         ybufs[t][y] = xbufs[t][px]
         y_send(ybufs[t].at[y], csem, t, 4)
         if t == 0:
-            affinities(2)
+            gather_rest(2)
+            affinities(1)
         y_wait(ybufs[t], csem, t, 4)
         grown = grown + ybufs[t][py].astype(jnp.float32)
 
@@ -471,10 +542,7 @@
 
     out[half:, :] = fin[...].reshape(2 * k, 2 * k)
 
-    all_sent(pending)
-    for t in range(ROUNDS):
-        ref = cands[t].at[c]
-        send(ref, ref, s1.at[CORE + t], r1.at[CORE + t], other_core).wait_send()
+    assert not pending
 
     @pl.when(stays)
     def _():
@@ -551,7 +619,7 @@
     n, feat = shots.shape
     k = basis.shape[1]
     nrep, nown = lax.axis_size("rep"), lax.axis_size("owner")
-    half = n // 2
+    half, n0 = n // 2, n * 3 // 4
     bf, f32 = jnp.bfloat16, jnp.float32
     vmem = pl.BlockSpec(memory_space=pltpu.VMEM)
     slab = (2 * k) // (2 * NX)
@@ -565,7 +633,11 @@
             pltpu.SMEM((ROUNDS,), jnp.int32),
             pltpu.VMEM((n, feat), bf),
             pltpu.VMEM((k, n), f32),
-            pltpu.VMEM((NY, NX, n, feat), bf),
+            pltpu.VMEM((n, feat), bf),
+            pltpu.VMEM((NX, n0, feat), bf),
+            pltpu.VMEM((NY, n - n0, feat), bf),
+            [pltpu.VMEM((NY, n0, feat), bf)] * ROUNDS,
+            [pltpu.VMEM((NX, 2, n - n0, feat), bf)] * ROUNDS,
             pltpu.VMEM((NZ, n, feat), bf),
             [pltpu.VMEM((2, 2, n, feat), bf)] * ROUNDS,
             pltpu.VMEM((ROUNDS, 2, n, NZ * n), bf),
@@ -587,7 +659,7 @@
             pltpu.VMEM((2 * NX, slab, 2 * k), f32),
             pltpu.VMEM((2 * NX, slab, 2 * k), f32),
             dma((3,)),
-            dma((61,)), dma((61,)),
+            dma((56,)), dma((56,)),
             dma((ROUNDS, NZ)), dma((ROUNDS, NZ)),
             dma((ROUNDS + 1, 8)), dma((ROUNDS + 1, 8)),
             dma((ROUNDS,)), dma((ROUNDS,)),

time: 122 us -> 120 us (0.984)
  Pallas kernels: 122 us -> 119 us
    pallas_call x1, Pallas kernels: 114 us -> 111 us  [shards(): pl.pallas_call(functools.partial(rounds_kernel, SHARPNESS / math.sqrt(fea...]
where the time goes in v6:
time: 120 us
  Pallas kernels  119 us (99%)
    pallas_call x1, Pallas kernels, shards(): pl.pallas_call(functools.partial(rounds_kernel, SHARPNESS / math.sqrt(fea...  111 us
    pallas_call x1, Pallas kernels, shards(): pl.pallas_call(functools.partial(finish_kernel, float(nown * nrep * n)),...  7.77 us

profile of v6, /device:TPU:1, one launch (start us, length us, event | category | flops | bytes accessed | tf_op | source)
XLA Modules:
  0.0 119.6 jit_solution(15257223397270893381)
XLA Ops:
  0.6 111.2 %rounds.1.both = f32[256,128]{1,0:T(8,128)} custom-call(s32[3]{0:T(128)} %masks_hbm.1, bf16[256,768]{1,0:T(8,128)(2,1)} %shots_hbm.1, f32[64,256]{1,0:T(8,128)} %bitcast.2), custom_call_target="tpu_custom_call" | custom-call | tf_op jit(solution)/shard_map/rounds/pallas_call | solution.py:627
  111.8 7.8 %finish.1 = (f32[64,256]{1,0:T(8,128)}, f32[64,64]{1,0:T(8,128)}) custom-call(f32[256,128]{1,0:T(8,128)} %rounds.1.both), custom_call_target="tpu_custom_call" | custom-call | tf_op jit(solution)/shard_map/finish/pallas_call | solution.py:673

commit v7 on v6

--- a/solution.py
+++ b/solution.py
@@ -17,21 +17,21 @@
 
 ORDER_STAYS = (
     (
-        ("G", 1, 1), ("G", 1, -1), ("F", 1, 1), ("Z", 1, 0, 1), ("Z", 1, 0, -1), ("Z", 1, 1, 1), ("Z", 1, 1, -1),
-        ("G", 2, 1), ("G", 2, -1), ("Q", 1, 1), ("F", 0, 3), ("F", 0, 1), ("F", 1, 3), ("Q", 1, 0), ("Z", 2, 0, 1),
-        ("Z", 2, 0, -1), ("Q", 0, 0), ("Q", 0, 1), ("Z", 2, 1, 1), ("Z", 2, 1, -1), ("G", 3, 1), ("G", 3, -1),
-        ("Z", 3, 0, 1), ("Z", 3, 0, -1), ("F", 5, 3), ("F", 5, 1), ("F", 2, 3), ("F", 2, 1), ("Z", 3, 1, 1),
-        ("Z", 3, 1, -1), ("G", 4, 1), ("Q", 5, 0), ("Q", 5, 1), ("Z", 4, 0, 1), ("Q", 2, 0), ("Q", 2, 1), ("F", 6, 3),
-        ("F", 6, 1), ("Z", 4, 1, -1), ("X", 0),
-    ),
-    (
-        ("Q", 6, 0), ("Q", 6, 1), ("F", 3, 3), ("F", 3, 1), ("F", 7, 3), ("F", 7, 1), ("Q", 3, 0), ("Q", 3, 1),
-    ),
-    (
-        ("Q", 7, 0), ("X", 1),
-    ),
-    (
-        ("Q", 7, 1), ("F", 4, 3), ("F", 4, 1), ("Q", 4, 0), ("Q", 4, 1),
+        ("G", 1, 1), ("G", 1, -1), ("Z", 1, 0, 1), ("Z", 1, 0, -1), ("F", 1, 1), ("Z", 1, 1, 1), ("Z", 1, 1, -1),
+        ("G", 2, 1), ("G", 2, -1), ("F", 0, 3), ("F", 0, 1), ("Q", 1, 1), ("F", 1, 3), ("Z", 2, 0, 1),
+        ("Z", 2, 0, -1), ("Q", 1, 0), ("Q", 0, 0), ("Q", 0, 1), ("Z", 2, 1, 1), ("Z", 2, 1, -1), ("G", 3, 1),
+        ("G", 3, -1), ("Z", 3, 0, 1), ("Z", 3, 0, -1), ("F", 5, 3), ("F", 5, 1), ("F", 2, 3), ("F", 2, 1),
+        ("Z", 3, 1, 1), ("Z", 3, 1, -1), ("G", 4, 1), ("F", 6, 3), ("F", 6, 1), ("F", 3, 3), ("F", 3, 1),
+        ("Z", 4, 0, 1), ("Q", 5, 0), ("Q", 5, 1), ("Z", 4, 1, -1), ("Q", 2, 0), ("Q", 2, 1), ("X", 0),
+    ),
+    (
+        ("F", 7, 3), ("F", 7, 1), ("F", 4, 3), ("F", 4, 1), ("Q", 6, 0), ("Q", 6, 1), ("Q", 3, 0), ("Q", 3, 1),
+    ),
+    (
+        ("Q", 7, 0), ("Q", 7, 1), ("X", 1),
+    ),
+    (
+        ("Q", 4, 0), ("Q", 4, 1),
     ),
     (
         ("X", 2),
@@ -39,22 +39,21 @@
 )
 ORDER_MOVED = (
     (
-        ("T",), ("F", 1, 1), ("F", 1, 3), ("O", 0), ("G", 1, 1), ("G", 1, -1), ("Q", 1, 1), ("O", 1), ("F", 0, 3),
-        ("F", 0, 1), ("Q", 1, 0), ("Z", 1, 0, 1), ("Z", 1, 0, -1), ("G", 2, 1), ("G", 2, -1), ("Q", 0, 0),
-        ("Q", 0, 1), ("Z", 1, 1, 1), ("Z", 1, 1, -1), ("F", 5, 3), ("F", 5, 1), ("Z", 2, 0, 1), ("Z", 2, 0, -1),
-        ("G", 3, 1), ("G", 3, -1), ("F", 2, 3), ("F", 2, 1), ("Z", 2, 1, -1), ("Q", 5, 0), ("Q", 5, 1),
-        ("Z", 2, 1, 1), ("Z", 3, 0, -1), ("Q", 2, 0), ("Q", 2, 1), ("Z", 3, 0, 1), ("F", 6, 3), ("F", 6, 1),
-        ("G", 4, 1), ("Z", 3, 1, -1), ("X", 0), ("Z", 3, 1, 1), ("Z", 4, 0, 1), ("Q", 6, 0), ("Q", 6, 1), ("F", 3, 3),
-        ("F", 3, 1), ("Z", 4, 1, -1),
-    ),
-    (
-        ("F", 7, 3), ("F", 7, 1), ("Q", 3, 0), ("Q", 3, 1),
-    ),
-    (
-        ("Q", 7, 0), ("Q", 7, 1), ("X", 1),
-    ),
-    (
-        ("F", 4, 3), ("F", 4, 1), ("Q", 4, 0), ("Q", 4, 1),
+        ("T",), ("F", 1, 1), ("F", 1, 3), ("O", 0), ("G", 1, 1), ("G", 1, -1), ("F", 0, 3), ("F", 0, 1), ("O", 1),
+        ("Q", 1, 1), ("Q", 1, 0), ("Z", 1, 0, 1), ("Z", 1, 0, -1), ("Q", 0, 0), ("Q", 0, 1), ("G", 2, 1),
+        ("G", 2, -1), ("Z", 1, 1, 1), ("Z", 1, 1, -1), ("F", 5, 3), ("F", 5, 1), ("Z", 2, 0, 1), ("Z", 2, 0, -1),
+        ("F", 2, 3), ("F", 2, 1), ("G", 3, 1), ("G", 3, -1), ("Z", 2, 1, -1), ("Z", 2, 1, 1), ("F", 6, 3),
+        ("F", 6, 1), ("F", 3, 3), ("F", 3, 1), ("Z", 3, 0, -1), ("Q", 5, 0), ("Q", 5, 1), ("Z", 3, 0, 1), ("G", 4, 1),
+        ("Q", 2, 0), ("Q", 2, 1), ("Z", 3, 1, -1), ("Z", 3, 1, 1), ("X", 0), ("Z", 4, 0, 1), ("F", 7, 3), ("F", 7, 1),
+        ("Z", 4, 1, -1),
+    ),
+    (
+        ("F", 4, 3), ("F", 4, 1), ("Q", 6, 0), ("Q", 6, 1), ("Q", 3, 0), ("Q", 3, 1),
+    ),
+    (
+        ("Q", 7, 0), ("Q", 7, 1), ("Q", 4, 0), ("Q", 4, 1), ("X", 1),
+    ),
+    (
     ),
     (
         ("X", 2),
@@ -182,8 +181,8 @@
         ref = leg(number, i)
         if number >= 5:
             return ref.at[part]
-        size = ref.shape[0] // 2
-        return ref.at[pl.ds(part * size, size)]
+        first = ref.shape[0] // 32 * 16 + 16
+        return ref.at[pl.ds(0, first)] if part == 0 else ref.at[pl.ds(first, ref.shape[0] - first)]
 
     def step(number, i):
         return dev(x=(x + i) % NX) if number in (0, 5, 6, 7) else dev(y=(y + i) % NY)
@@ -206,8 +205,8 @@
             sel0[t][y] = rowbuf[x ^ ((m // 2) % 4)]
             for a in range(2):
                 sel1[t][x, a] = colbuf[(yh ^ (m // 8)) * 2 + a]
-        begin(2)
-        begin(5)
+        for number in (2, 5, 3, 6):
+            begin(number)
 
     up, down = dev(z=(z + 1) % NZ), dev(z=(z + NZ - 1) % NZ)
 
@@ -273,8 +272,8 @@
             if kind == "F":
                 on_full(*args)
                 number, k = args
-                if number in (2, 3, 5, 6) and ("F", number, 4 - k) in seen:
-                    begin(number + 1)
+                if number in (2, 5) and ("F", number, 4 - k) in seen:
+                    begin(number + 2)
             elif kind == "Q":
                 on_half(*args)
             elif kind == "Z":
@@ -619,7 +618,7 @@
     n, feat = shots.shape
     k = basis.shape[1]
     nrep, nown = lax.axis_size("rep"), lax.axis_size("owner")
-    half, n0 = n // 2, n * 3 // 4
+    half, n0 = n // 2, n * 11 // 16
     bf, f32 = jnp.bfloat16, jnp.float32
     vmem = pl.BlockSpec(memory_space=pltpu.VMEM)
     slab = (2 * k) // (2 * NX)

time: 120 us -> 116 us (0.967)
  Pallas kernels: 119 us -> 115 us
    pallas_call x1, Pallas kernels: 111 us -> 107 us  [shards(): pl.pallas_call(functools.partial(rounds_kernel, SHARPNESS / math.sqrt(fea...]
where the time goes in v7:
time: 116 us
  Pallas kernels  115 us (99%)
    pallas_call x1, Pallas kernels, shards(): pl.pallas_call(functools.partial(rounds_kernel, SHARPNESS / math.sqrt(fea...  107 us
    pallas_call x1, Pallas kernels, shards(): pl.pallas_call(functools.partial(finish_kernel, float(nown * nrep * n)),...  7.77 us

profile of v7, /device:TPU:1, one launch (start us, length us, event | category | flops | bytes accessed | tf_op | source)
XLA Modules:
  0.0 115.6 jit_solution(2166638784625470963)
XLA Ops:
  0.6 107.1 %rounds.1.both = f32[256,128]{1,0:T(8,128)} custom-call(s32[3]{0:T(128)} %masks_hbm.1, bf16[256,768]{1,0:T(8,128)(2,1)} %shots_hbm.1, f32[64,256]{1,0:T(8,128)} %bitcast.2), custom_call_target="tpu_custom_call" | custom-call | tf_op jit(solution)/shard_map/rounds/pallas_call | solution.py:626
  107.8 7.8 %finish.1 = (f32[64,256]{1,0:T(8,128)}, f32[64,64]{1,0:T(8,128)}) custom-call(f32[256,128]{1,0:T(8,128)} %rounds.1.both), custom_call_target="tpu_custom_call" | custom-call | tf_op jit(solution)/shard_map/finish/pallas_call | solution.py:672

commit v8 on v7

--- a/solution.py
+++ b/solution.py
@@ -18,20 +18,20 @@
 ORDER_STAYS = (
     (
         ("G", 1, 1), ("G", 1, -1), ("Z", 1, 0, 1), ("Z", 1, 0, -1), ("F", 1, 1), ("Z", 1, 1, 1), ("Z", 1, 1, -1),
-        ("G", 2, 1), ("G", 2, -1), ("F", 0, 3), ("F", 0, 1), ("Q", 1, 1), ("F", 1, 3), ("Z", 2, 0, 1),
-        ("Z", 2, 0, -1), ("Q", 1, 0), ("Q", 0, 0), ("Q", 0, 1), ("Z", 2, 1, 1), ("Z", 2, 1, -1), ("G", 3, 1),
-        ("G", 3, -1), ("Z", 3, 0, 1), ("Z", 3, 0, -1), ("F", 5, 3), ("F", 5, 1), ("F", 2, 3), ("F", 2, 1),
-        ("Z", 3, 1, 1), ("Z", 3, 1, -1), ("G", 4, 1), ("F", 6, 3), ("F", 6, 1), ("F", 3, 3), ("F", 3, 1),
-        ("Z", 4, 0, 1), ("Q", 5, 0), ("Q", 5, 1), ("Z", 4, 1, -1), ("Q", 2, 0), ("Q", 2, 1), ("X", 0),
+        ("G", 2, 1), ("G", 2, -1), ("F", 0, 3), ("F", 0, 1), ("Q", 1, 1), ("F", 1, 3), ("Z", 2, 0, 1), ("Q", 1, 0),
+        ("Z", 2, 0, -1), ("Q", 0, 0), ("Q", 0, 1), ("Z", 2, 1, 1), ("Z", 2, 1, -1), ("G", 3, 1), ("G", 3, -1),
+        ("Z", 3, 0, 1), ("Z", 3, 0, -1), ("F", 5, 3), ("F", 5, 1), ("F", 2, 3), ("F", 2, 1), ("Z", 3, 1, 1),
+        ("Z", 3, 1, -1), ("G", 4, 1), ("F", 6, 3), ("Z", 4, 0, 1), ("F", 6, 1), ("F", 3, 3), ("F", 3, 1), ("Q", 5, 0),
+        ("Q", 5, 1), ("Z", 4, 1, -1), ("Q", 2, 0), ("Q", 2, 1), ("X", 0),
     ),
     (
         ("F", 7, 3), ("F", 7, 1), ("F", 4, 3), ("F", 4, 1), ("Q", 6, 0), ("Q", 6, 1), ("Q", 3, 0), ("Q", 3, 1),
     ),
     (
-        ("Q", 7, 0), ("Q", 7, 1), ("X", 1),
-    ),
-    (
-        ("Q", 4, 0), ("Q", 4, 1),
+        ("X", 1),
+    ),
+    (
+        ("Q", 7, 0), ("Q", 7, 1), ("Q", 4, 0), ("Q", 4, 1),
     ),
     (
         ("X", 2),
@@ -41,19 +41,20 @@
     (
         ("T",), ("F", 1, 1), ("F", 1, 3), ("O", 0), ("G", 1, 1), ("G", 1, -1), ("F", 0, 3), ("F", 0, 1), ("O", 1),
         ("Q", 1, 1), ("Q", 1, 0), ("Z", 1, 0, 1), ("Z", 1, 0, -1), ("Q", 0, 0), ("Q", 0, 1), ("G", 2, 1),
-        ("G", 2, -1), ("Z", 1, 1, 1), ("Z", 1, 1, -1), ("F", 5, 3), ("F", 5, 1), ("Z", 2, 0, 1), ("Z", 2, 0, -1),
-        ("F", 2, 3), ("F", 2, 1), ("G", 3, 1), ("G", 3, -1), ("Z", 2, 1, -1), ("Z", 2, 1, 1), ("F", 6, 3),
-        ("F", 6, 1), ("F", 3, 3), ("F", 3, 1), ("Z", 3, 0, -1), ("Q", 5, 0), ("Q", 5, 1), ("Z", 3, 0, 1), ("G", 4, 1),
+        ("G", 2, -1), ("Z", 1, 1, 1), ("Z", 1, 1, -1), ("Z", 2, 0, 1), ("Z", 2, 0, -1), ("F", 5, 3), ("F", 5, 1),
+        ("G", 3, 1), ("G", 3, -1), ("F", 2, 3), ("F", 2, 1), ("Z", 2, 1, -1), ("Z", 2, 1, 1), ("F", 6, 3),
+        ("F", 6, 1), ("Z", 3, 0, -1), ("F", 3, 3), ("F", 3, 1), ("Z", 3, 0, 1), ("G", 4, 1), ("Q", 5, 0), ("Q", 5, 1),
         ("Q", 2, 0), ("Q", 2, 1), ("Z", 3, 1, -1), ("Z", 3, 1, 1), ("X", 0), ("Z", 4, 0, 1), ("F", 7, 3), ("F", 7, 1),
-        ("Z", 4, 1, -1),
-    ),
-    (
-        ("F", 4, 3), ("F", 4, 1), ("Q", 6, 0), ("Q", 6, 1), ("Q", 3, 0), ("Q", 3, 1),
-    ),
-    (
-        ("Q", 7, 0), ("Q", 7, 1), ("Q", 4, 0), ("Q", 4, 1), ("X", 1),
-    ),
-    (
+        ("F", 4, 3), ("F", 4, 1), ("Z", 4, 1, -1),
+    ),
+    (
+        ("Q", 6, 0), ("Q", 6, 1), ("Q", 3, 0), ("Q", 3, 1),
+    ),
+    (
+        ("Q", 7, 0), ("X", 1),
+    ),
+    (
+        ("Q", 7, 1), ("Q", 4, 0), ("Q", 4, 1),
     ),
     (
         ("X", 2),
@@ -73,11 +74,12 @@
 def rounds_kernel(
     scale, masks_hbm, shots_hbm, basis_hbm, out,
     masks, shots, basis_t, unit, rowbuf, colbuf, sel0, sel1, own, cands, aff, gpart, gfull, wsend, wrecv, xbufs, ybufs, homeward, ghome, gsend, gback, gx, gy,
-    rs, ys, zs, fin, prod,
+    sums,
     s_in, s1, r1, sg, rg, sc, rc, sw, rw, sa, ra,
 ):
     n, feat = shots.shape
     half, n0 = n // 2, rowbuf.shape[1]
+    rs, zs, fin, prod = sums
     n1 = n - n0
     k = basis_t.shape[0]
     o, r = lax.axis_index("owner"), lax.axis_index("rep")
@@ -462,15 +464,22 @@
             value = value + ref[i]
         return value
 
-    def q_dev(i):
-        there = (q + i) % nq
-        return dev(x=there // 2, c=there % 2)
-
-    @pl.loop(1, nq)
-    def _(i):
-        send(prod.at[(q + i) % nq], rs.at[q], sa.at[i], ra.at[i], q_dev(i)).start()
-
-    rs[q] = prod[q]
+    group = 2 * NX * 2
+    place = q * 2 + yl
+    line = (z * 2 + yh) % group
+
+    def near_dev(i):
+        there = (place + i) % group
+        return there, dev(y=yh * 2 + there % 2, x=there // 4, c=there // 2 % 2)
+
+    def far_dev(i):
+        there = (line + i) % group
+        return dev(y=there % 2 * 2 + yl, z=there // 2)
+
+    for i in range(1, group):
+        there, device = near_dev(i)
+        send(prod.at[there], rs.at[place], sa.at[i], ra.at[i], device).start()
+    rs[place] = prod[place]
 
     x_wait(xbufs[t], csem, t, 0)
     homeward[...] = xbufs[t][px]
@@ -491,36 +500,21 @@
     for i in range(1, NY):
         home_copy(i).start()
 
-    @pl.loop(1, nq)
-    def _(i):
-        send(prod.at[0], rs.at[(q + nq - i) % nq], sa.at[i], ra.at[i], other_core).wait_recv()
-
-    ys[y] = total(rs, nq)
-
-    @pl.loop(1, NY)
-    def _(i):
-        send(ys.at[y], ys.at[y], sa.at[8 + i], ra.at[8 + i], dev(y=(y + i) % NY)).start()
-
-    @pl.loop(1, NY)
-    def _(i):
-        ref = ys.at[(y + NY - i) % NY]
-        send(ref, ref, sa.at[8 + i], ra.at[8 + i], other_core).wait_recv()
-
-    zs[z] = total(ys, NY)
-
-    for i in (3, 5, 4, 2, 6, 1, 7):
-        send(zs.at[z], zs.at[z], sa.at[12 + i], ra.at[12 + i], dev(z=(z + i) % NZ)).start()
-
-    @pl.loop(1, NZ)
-    def _(i):
-        ref = zs.at[(z + NZ - i) % NZ]
-        send(ref, ref, sa.at[12 + i], ra.at[12 + i], other_core).wait_recv()
-
-    fin[q] = total(zs, NZ)
-
-    @pl.loop(1, nq)
-    def _(i):
-        send(fin.at[q], fin.at[q], sa.at[20 + i], ra.at[20 + i], q_dev(i)).start()
+    for i in range(1, group):
+        send(prod.at[0], rs.at[(place + group - i) % group], sa.at[i], ra.at[i], other_core).wait_recv()
+    zs[line] = total(rs, group)
+
+    for i in (8, 7, 9, 6, 10, 5, 11, 4, 12, 3, 13, 2, 14, 1, 15):
+        ref = zs.at[line]
+        send(ref, ref, sa.at[group + i], ra.at[group + i], far_dev(i)).start()
+    for i in range(1, group):
+        ref = zs.at[(line + group - i) % group]
+        send(ref, ref, sa.at[group + i], ra.at[group + i], other_core).wait_recv()
+    fin[place] = total(zs, group)
+
+    for i in range(1, group):
+        ref = fin.at[place]
+        send(ref, ref, sa.at[2 * group + i], ra.at[2 * group + i], near_dev(i)[1]).start()
 
     @pl.when(moved)
     def _():
@@ -534,10 +528,9 @@
     m = masks[t]
     out[:half, :] = gback[...] + ybufs[t][twin_y ^ ((m // 8) * 2 + m % 2)].astype(jnp.float32)
 
-    @pl.loop(1, nq)
-    def _(i):
-        ref = fin.at[(q + nq - i) % nq]
-        send(ref, ref, sa.at[20 + i], ra.at[20 + i], other_core).wait_recv()
+    for i in range(1, group):
+        ref = fin.at[(place + group - i) % group]
+        send(ref, ref, sa.at[2 * group + i], ra.at[2 * group + i], other_core).wait_recv()
 
     out[half:, :] = fin[...].reshape(2 * k, 2 * k)
 
@@ -563,15 +556,18 @@
         ref = gx.at[x]
         send(ref, ref, sc.at[ROUNDS, i], rc.at[ROUNDS, i], other_core).wait_send()
         send(ref, ref, sc.at[ROUNDS, 4 + i], rc.at[ROUNDS, 4 + i], other_core).wait_send()
-        send(ys.at[y], ys.at[y], sa.at[8 + i], ra.at[8 + i], other_core).wait_send()
 
     @pl.loop(1, NZ)
     def _(i):
         for row in range(ROUNDS):
             ref = gpart.at[row, z]
             send(ref, ref, sg.at[row, i], rg.at[row, i], other_core).wait_send()
-        for base in (0, 12, 20):
-            send(fin.at[q], fin.at[q], sa.at[base + i], ra.at[base + i], other_core).wait_send()
+
+    @pl.loop(1, group)
+    def _(i):
+        for base in range(3):
+            ref = fin.at[place]
+            send(ref, ref, sa.at[base * group + i], ra.at[base * group + i], other_core).wait_send()
 
     for row in range(ROUNDS):
         send(wsend.at[row], wrecv.at[row], sw.at[row], rw.at[row], other_core).wait_send()
@@ -621,7 +617,7 @@
     half, n0 = n // 2, n * 11 // 16
     bf, f32 = jnp.bfloat16, jnp.float32
     vmem = pl.BlockSpec(memory_space=pltpu.VMEM)
-    slab = (2 * k) // (2 * NX)
+    slab = (2 * k) // 16
     dma = pltpu.SemaphoreType.DMA
     both = pl.pallas_call(
         functools.partial(rounds_kernel, SHARPNESS / math.sqrt(feat)),
@@ -652,17 +648,13 @@
             pltpu.VMEM((half, 2 * k), f32),
             pltpu.VMEM((NX, half, 2 * k), f32),
             pltpu.VMEM((NY, half, 2 * k), f32),
-            pltpu.VMEM((2 * NX, slab, 2 * k), f32),
-            pltpu.VMEM((NY, slab, 2 * k), f32),
-            pltpu.VMEM((NZ, slab, 2 * k), f32),
-            pltpu.VMEM((2 * NX, slab, 2 * k), f32),
-            pltpu.VMEM((2 * NX, slab, 2 * k), f32),
+            [pltpu.VMEM((16, slab, 2 * k), f32)] * 4,
             dma((3,)),
             dma((56,)), dma((56,)),
             dma((ROUNDS, NZ)), dma((ROUNDS, NZ)),
             dma((ROUNDS + 1, 8)), dma((ROUNDS + 1, 8)),
             dma((ROUNDS,)), dma((ROUNDS,)),
-            dma((28,)), dma((28,)),
+            dma((48,)), dma((48,)),
         ],
         compiler_params=pltpu.CompilerParams(
             collective_id=0, has_side_effects=True, vmem_limit_bytes=60 * 1024 * 1024

time: 116 us -> 113 us (0.974)
  Pallas kernels: 115 us -> 112 us
    pallas_call x1, Pallas kernels: 107 us -> 104 us  [shards(): pl.pallas_call(functools.partial(rounds_kernel, SHARPNESS / math.sqrt(fea...]
where the time goes in v8:
time: 113 us
  Pallas kernels  112 us (99%)
    pallas_call x1, Pallas kernels, shards(): pl.pallas_call(functools.partial(rounds_kernel, SHARPNESS / math.sqrt(fea...  104 us
    pallas_call x1, Pallas kernels, shards(): pl.pallas_call(functools.partial(finish_kernel, float(nown * nrep * n)),...  7.77 us

profile of v8, /device:TPU:1, one launch (start us, length us, event | category | flops | bytes accessed | tf_op | source)
XLA Modules:
  0.0 112.7 jit_solution(13401773964059392358)
XLA Ops:
  0.6 104.3 %rounds.1.both = f32[256,128]{1,0:T(8,128)} custom-call(s32[3]{0:T(128)} %masks_hbm.1, bf16[256,768]{1,0:T(8,128)(2,1)} %shots_hbm.1, f32[64,256]{1,0:T(8,128)} %bitcast.2), custom_call_target="tpu_custom_call" | custom-call | tf_op jit(solution)/shard_map/rounds/pallas_call | solution.py:622
  104.9 7.8 %finish.1 = (f32[64,256]{1,0:T(8,128)}, f32[64,64]{1,0:T(8,128)}) custom-call(f32[256,128]{1,0:T(8,128)} %rounds.1.both), custom_call_target="tpu_custom_call" | custom-call | tf_op jit(solution)/shard_map/finish/pallas_call | solution.py:664

commit v9 on v8

--- a/solution.py
+++ b/solution.py
@@ -72,9 +72,9 @@
 
 
 def rounds_kernel(
-    scale, masks_hbm, shots_hbm, basis_hbm, out,
+    scale, masks_hbm, shots_hbm, basis_hbm, rows_out, sums_out,
     masks, shots, basis_t, unit, rowbuf, colbuf, sel0, sel1, own, cands, aff, gpart, gfull, wsend, wrecv, xbufs, ybufs, homeward, ghome, gsend, gback, gx, gy,
-    sums,
+    sums, result,
     s_in, s1, r1, sg, rg, sc, rc, sw, rw, sa, ra,
 ):
     n, feat = shots.shape
@@ -526,13 +526,16 @@
         ref = ybufs[t].at[(twin_y + NY - i) % NY]
         send(ref, ref, sc.at[t, 4 + i], rc.at[t, 4 + i], other_core).wait_recv()
     m = masks[t]
-    out[:half, :] = gback[...] + ybufs[t][twin_y ^ ((m // 8) * 2 + m % 2)].astype(jnp.float32)
+    result[...] = gback[...] + ybufs[t][twin_y ^ ((m // 8) * 2 + m % 2)].astype(jnp.float32)
+    rows_copy = pltpu.make_async_copy(result, rows_out, s_in.at[3])
+    rows_copy.start()
 
     for i in range(1, group):
         ref = fin.at[(place + group - i) % group]
         send(ref, ref, sa.at[2 * group + i], ra.at[2 * group + i], other_core).wait_recv()
 
-    out[half:, :] = fin[...].reshape(2 * k, 2 * k)
+    sums_copy = pltpu.make_async_copy(fin, sums_out, s_in.at[4])
+    sums_copy.start()
 
     assert not pending
 
@@ -571,6 +574,8 @@
 
     for row in range(ROUNDS):
         send(wsend.at[row], wrecv.at[row], sw.at[row], rw.at[row], other_core).wait_send()
+    rows_copy.wait()
+    sums_copy.wait()
 
 
 def inverse_factors(grams):
@@ -598,12 +603,15 @@
     return results
 
 
-def finish_kernel(total_rows, both, iterate_t, ritz):
+def finish_kernel(total_rows, grown_hbm, sums, iterate_t, ritz, grown, sem):
     k = ritz.shape[0]
-    half = both.shape[0] - 2 * k
-    every = both[half:, :] * (1.0 / total_rows)
+    half = grown.shape[0]
+    copy = pltpu.make_async_copy(grown_hbm, grown, sem)
+    copy.start()
+    every = sums[...].reshape(2 * k, 2 * k) * (1.0 / total_rows)
     inv_before, inv_last = inverse_factors([every[:k, :k], every[k:, k:]])
-    packed = both[:half, :]
+    copy.wait()
+    packed = grown[...]
     iterate_t[:, :half] = dot32(inv_last, packed[:, :k], NT)
     iterate_t[:, half:] = dot32(inv_last, packed[:, k:], NT)
     left = dot32(inv_before, every[:k, k:], (((1,), (0,)), ((), ())))
@@ -616,14 +624,14 @@
     nrep, nown = lax.axis_size("rep"), lax.axis_size("owner")
     half, n0 = n // 2, n * 11 // 16
     bf, f32 = jnp.bfloat16, jnp.float32
-    vmem = pl.BlockSpec(memory_space=pltpu.VMEM)
+    vmem, hbm = pl.BlockSpec(memory_space=pltpu.VMEM), pl.BlockSpec(memory_space=pltpu.HBM)
     slab = (2 * k) // 16
     dma = pltpu.SemaphoreType.DMA
-    both = pl.pallas_call(
+    grown, total_sums = pl.pallas_call(
         functools.partial(rounds_kernel, SHARPNESS / math.sqrt(feat)),
-        out_shape=jax.ShapeDtypeStruct((half + 2 * k, 2 * k), f32),
-        in_specs=[pl.BlockSpec(memory_space=pltpu.HBM)] * 3,
-        out_specs=vmem,
+        out_shape=(jax.ShapeDtypeStruct((half, 2 * k), f32), jax.ShapeDtypeStruct((16, slab, 2 * k), f32)),
+        in_specs=[hbm] * 3,
+        out_specs=(hbm, hbm),
         scratch_shapes=[
             pltpu.SMEM((ROUNDS,), jnp.int32),
             pltpu.VMEM((n, feat), bf),
@@ -649,7 +657,8 @@
             pltpu.VMEM((NX, half, 2 * k), f32),
             pltpu.VMEM((NY, half, 2 * k), f32),
             [pltpu.VMEM((16, slab, 2 * k), f32)] * 4,
-            dma((3,)),
+            pltpu.VMEM((half, 2 * k), f32),
+            dma((5,)),
             dma((56,)), dma((56,)),
             dma((ROUNDS, NZ)), dma((ROUNDS, NZ)),
             dma((ROUNDS + 1, 8)), dma((ROUNDS + 1, 8)),
@@ -664,10 +673,11 @@
     iterate_t, ritz = pl.pallas_call(
         functools.partial(finish_kernel, float(nown * nrep * n)),
         out_shape=(jax.ShapeDtypeStruct((k, n), f32), jax.ShapeDtypeStruct((k, k), f32)),
-        in_specs=[vmem],
+        in_specs=[hbm, vmem],
         out_specs=(vmem, vmem),
+        scratch_shapes=[pltpu.VMEM((half, 2 * k), f32), pltpu.SemaphoreType.DMA],
         name="finish",
-    )(both)
+    )(grown, total_sums)
     return iterate_t.T, ritz
 
 

time: 113 us -> 112 us (level)
  no operation moved by 1% of the time
where the time goes in v9:
time: 112 us
  Pallas kernels  111 us (99%)
    pallas_call x1, Pallas kernels, shards(): pl.pallas_call(functools.partial(rounds_kernel, SHARPNESS / math.sqrt(fea...  104 us
    pallas_call x1, Pallas kernels, shards(): pl.pallas_call(functools.partial(finish_kernel, float(nown * nrep * n)),...  7.54 us

profile of v9, /device:TPU:1, one launch (start us, length us, event | category | flops | bytes accessed | tf_op | source)
XLA Modules:
  0.0 111.7 jit_solution(1244801894508965203)
XLA Ops:
  0.6 103.5 %rounds.1 = (f32[128,128]{1,0:T(8,128)}, f32[16,8,128]{2,1,0:T(8,128)}) custom-call(s32[3]{0:T(128)} %masks_hbm.1, bf16[256,768]{1,0:T(8,128)(2,1)} %shots_hbm.1, f32[64,256]{1,0:T(8,128)} %bitcast.2), custom_call_target="tpu_custom_call" | custom-call | tf_op jit(solution)/shard_map/rounds/pallas_call | solution.py:630
  104.1 7.5 %finish.1 = (f32[64,256]{1,0:T(8,128)}, f32[64,64]{1,0:T(8,128)}) custom-call(f32[128,128]{1,0:T(8,128)} %get-tuple-element.6.grown_hbm, f32[16,8,128]{2,1,0:T(8,128)} %get-tuple-element.7.sums), custom_call_target="tpu_custom_call" | custom-call | tf_op jit(solution)/shard_map/finish/pallas_call | solution.py:673

commit v10 on v9

--- a/solution.py
+++ b/solution.py
@@ -129,7 +129,7 @@
     units = (values * inv).astype(jnp.bfloat16)
     rowbuf[x] = units[:n0]
     colbuf[y] = units[n0:]
-    g0 = pack(basis_t[...].T)
+    g0 = pack(basis_t[...].T) * 0.25
 
     @pl.when(stays)
     def _():

time: 112 us -> 112 us (level)
  no operation moved by 1% of the time
where the time goes in v10:
time: 112 us
  Pallas kernels  111 us (99%)
    pallas_call x1, Pallas kernels, shards(): pl.pallas_call(functools.partial(rounds_kernel, SHARPNESS / math.sqrt(fea...  103 us
    pallas_call x1, Pallas kernels, shards(): pl.pallas_call(functools.partial(finish_kernel, float(nown * nrep * n)),...  7.54 us

profile of v10, /device:TPU:1, one launch (start us, length us, event | category | flops | bytes accessed | tf_op | source)
XLA Modules:
  0.0 111.7 jit_solution(9023478350366291149)
XLA Ops:
  0.6 103.5 %rounds.1 = (f32[128,128]{1,0:T(8,128)}, f32[16,8,128]{2,1,0:T(8,128)}) custom-call(s32[3]{0:T(128)} %masks_hbm.1, bf16[256,768]{1,0:T(8,128)(2,1)} %shots_hbm.1, f32[64,256]{1,0:T(8,128)} %bitcast.2), custom_call_target="tpu_custom_call" | custom-call | tf_op jit(solution)/shard_map/rounds/pallas_call | solution.py:630
  104.1 7.5 %finish.1 = (f32[64,256]{1,0:T(8,128)}, f32[64,64]{1,0:T(8,128)}) custom-call(f32[128,128]{1,0:T(8,128)} %get-tuple-element.6.grown_hbm, f32[16,8,128]{2,1,0:T(8,128)} %get-tuple-element.7.sums), custom_call_target="tpu_custom_call" | custom-call | tf_op jit(solution)/shard_map/finish/pallas_call | solution.py:673

commit v11 on v10

--- a/solution.py
+++ b/solution.py
@@ -210,6 +210,15 @@
         for number in (2, 5, 3, 6):
             begin(number)
 
+    lane = lax.broadcasted_iota(jnp.int32, (half, 2 * k), 1)
+    tail = jnp.where(lane == k, 1.0, 0.0)
+
+    def unpack(t, item):
+        p = gpart[t, item].astype(jnp.float32)
+        start = pl.multiple_of(item * n, n)
+        gfull[pl.ds(start, half), :] = jnp.where(lane < k, p, tail).astype(jnp.bfloat16)
+        gfull[pl.ds(start + half, half), :] = jnp.where(lane < k, pltpu.roll(p, k, 1), tail).astype(jnp.bfloat16)
+
     up, down = dev(z=(z + 1) % NZ), dev(z=(z + NZ - 1) % NZ)
 
     def z_begin(h):
@@ -225,6 +234,7 @@
 
     def g_begin():
         gpart[0, z] = ghome[...].astype(jnp.bfloat16)
+        unpack(0, z)
         for i, device in ((1, up), (7, down)):
             send(gpart.at[0, z], gpart.at[0, z], sg.at[0, i], rg.at[0, i], device).start()
 
@@ -234,6 +244,7 @@
         send(ref, ref, sg.at[0, i], rg.at[0, i], other_core).wait_recv()
         if s < 3 or (s == 3 and direction == 1):
             send(ref, ref, sg.at[0, i + direction], rg.at[0, i + direction], up if direction == 1 else down).start()
+        unpack(0, (z + NZ - direction * s) % NZ)
 
     def choose(t):
         m = masks[t]
@@ -360,26 +371,17 @@
         m = masks[t]
         return y ^ ((m // 8) * 2 + m % 2), x ^ ((m // 2) % 4)
 
-    lane = lax.broadcasted_iota(jnp.int32, (half, 2 * k), 1)
-    tail = jnp.where(lane == k, 1.0, 0.0)
-
-    def unpack(t, item):
-        p = gpart[t, item].astype(jnp.float32)
-        start = pl.multiple_of(item * n, n)
-        gfull[pl.ds(start, half), :] = jnp.where(lane < k, p, tail).astype(jnp.bfloat16)
-        gfull[pl.ds(start + half, half), :] = jnp.where(lane < k, pltpu.roll(p, k, 1), tail).astype(jnp.bfloat16)
-
     def carried(t):
-        unpack(t, z)
-
-        @pl.loop(1, NZ)
-        def _(j):
-            i = near(j)
-            item = (z + NZ - i) % NZ
-            if t > 0:
+        if t > 0:
+            unpack(t, z)
+
+            @pl.loop(1, NZ)
+            def _(j):
+                i = near(j)
+                item = (z + NZ - i) % NZ
                 ref = gpart.at[t, item]
                 send(ref, ref, sg.at[t, i], rg.at[t, i], other_core).wait_recv()
-            unpack(t, item)
+                unpack(t, item)
 
         wsend[t] = jnp.dot(aff[t, 1 - c], gfull[...], preferred_element_type=jnp.float32)
         copy = send(wsend.at[t], wrecv.at[t], sw.at[t], rw.at[t], other_core)

time: 112 us -> 112 us (level)
  no operation moved by 1% of the time
where the time goes in v11:
time: 112 us
  Pallas kernels  111 us (99%)
    pallas_call x1, Pallas kernels, shards(): pl.pallas_call(functools.partial(rounds_kernel, SHARPNESS / math.sqrt(fea...  103 us
    pallas_call x1, Pallas kernels, shards(): pl.pallas_call(functools.partial(finish_kernel, float(nown * nrep * n)),...  7.54 us

profile of v11, /device:TPU:1, one launch (start us, length us, event | category | flops | bytes accessed | tf_op | source)
XLA Modules:
  0.0 111.5 jit_solution(11078797374716856248)
XLA Ops:
  0.6 103.3 %rounds.1 = (f32[128,128]{1,0:T(8,128)}, f32[16,8,128]{2,1,0:T(8,128)}) custom-call(s32[3]{0:T(128)} %masks_hbm.1, bf16[256,768]{1,0:T(8,128)(2,1)} %shots_hbm.1, f32[64,256]{1,0:T(8,128)} %bitcast.2), custom_call_target="tpu_custom_call" | custom-call | tf_op jit(solution)/shard_map/rounds/pallas_call | solution.py:632
  104.0 7.5 %finish.1 = (f32[64,256]{1,0:T(8,128)}, f32[64,64]{1,0:T(8,128)}) custom-call(f32[128,128]{1,0:T(8,128)} %get-tuple-element.6.grown_hbm, f32[16,8,128]{2,1,0:T(8,128)} %get-tuple-element.7.sums), custom_call_target="tpu_custom_call" | custom-call | tf_op jit(solution)/shard_map/finish/pallas_call | solution.py:675
